TPU v7x, 32 devices: a whole 2x2x4 slice. The times are simulated.
32 devices in a mesh: groups: 2 (over y), gz: 4 (over z), view: 2 (over x), gy: 2 (over core).
Axes of the slice: x: 2, y: 2, z: 4, core: 2. Of those that a mesh axis runs over, the one named last changes fastest.
Arguments:
- camera: float32 [2, 256, 3, 128, 128], P('view', ('groups', 'gz'), None, 'gy'), parts along dimension 1, may hold values from 0 to 4
- background: int32 [2, 2, 8], P('view', 'gy', ('groups', 'gz')), parts along dimension 2, may hold values from 0 to 2
- destination: int32 [2, 2, 256, 1], P('view', 'gy', ('groups', 'gz')), parts along dimension 2, may hold values from 0 to 3; in each aligned block of 32 rows (0 to 31, 32 to 63, ..., all dimensions but the last counted through in order) at most 16 rows name the same one
- offsets: int32 [2, 2, 256], P('view', 'gy', ('groups', 'gz')), parts along dimension 2, may hold values from 0 to 6
- shift_frac: float32 [2, 3], P('view'), may hold values from 0.15 to 0.85
- psf_taps: float32 [2, 3, 9], P('view'), may hold values from 0.05 to 1
Outputs:
- estimate: float32 [64, 128, 128], P(('groups', 'gz'), 'gy'), parts along dimension 0
- joined_views: float32 [2, 64, 128, 128], P('view', ('groups', 'gz'), 'gy'), parts along dimension 1
There are 2 independent parts, one for each index of `groups`. A program takes and returns all parts, laid end to end along the dimension named above; an argument that names none is the same for every part. Nothing has to cross between parts.
Inputs may be any that keep to these rules, and one draw needn't show every extreme that they name: `destination`: within the 32 block rows of one tile, no slab is named more than 16 times; some tile names one slab exactly 16 times.
All inputs are finite; a program needn't handle non-finite values.
Results may differ from a plain program's by a relative error of at most 0.0001.
Values sent between devices are 32-bit elements; how exact they have to be, the bound alone decides.
No kernel may reach another device: no remote copies, remote signals or barrier semaphores. Data moves between devices by JAX's collectives and lax.ppermute only.
A program may use at most 64 MiB of HBM per device.

v0:
```python
import jax
import jax.numpy as jnp
from jax import lax
from jax.sharding import PartitionSpec as P

CZ = 8
ITERS = 2


DATA_FLOOR = 0.25
PRECISE = lax.Precision.HIGHEST


def extended(block, sides, width):
    for axis, dim in sides:
        count = lax.axis_size(axis)
        forward = [(i, i + 1) for i in range(count - 1)]
        backward = [(target, source) for source, target in forward]
        low = lax.ppermute(
            lax.slice_in_dim(block, block.shape[dim] - width, None, axis=dim), axis, forward
        )
        high = lax.ppermute(lax.slice_in_dim(block, 0, width, axis=dim), axis, backward)
        block = jnp.concatenate([low, block, high], axis=dim)
    return block


def interp_matrix(length, fraction):
    places = jnp.arange(length, dtype=jnp.int32)
    follow = jnp.minimum(places + 1, length - 1)
    same_row = (places[:, None] == places[None, :]).astype(jnp.float32)
    next_row = (follow[:, None] == places[None, :]).astype(jnp.float32)
    return (1.0 - fraction) * same_row + fraction * next_row


def interp_blocks(blocks, fraction_z, y_matrix, x_matrix):
    lower = blocks[..., :-1, :, :]
    upper = blocks[..., 1:, :, :]
    planes = (1.0 - fraction_z) * lower + fraction_z * upper
    planes = jnp.einsum("ry,...yx->...rx", y_matrix, planes, precision=PRECISE)
    return jnp.einsum("...rx,cx->...rc", planes, x_matrix, precision=PRECISE)


def along_last(volume, weights):
    margin = weights.shape[0] // 2
    span_cells = volume.shape[-1]
    padded = jnp.pad(volume, [(0, 0)] * (volume.ndim - 1) + [(margin, margin)])
    result = weights[0] * padded[..., 0:span_cells]
    for offset in range(1, weights.shape[0]):
        result = result + weights[offset] * padded[..., offset : offset + span_cells]
    return result


def valid_pass(padded, weights, out_len, along_axis):
    result = weights[0] * lax.slice_in_dim(padded, 0, out_len, axis=along_axis)
    for offset in range(1, weights.shape[0]):
        result = result + weights[offset] * lax.slice_in_dim(
            padded, offset, offset + out_len, axis=along_axis
        )
    return result


def apply_passes(padded, kernel, planes_out, rows_out):
    x_done = along_last(padded, kernel[2])
    y_done = valid_pass(x_done, kernel[1], rows_out, 1)
    return valid_pass(y_done, kernel[0], planes_out, 0)


def spread(volume, kernel):
    margin = kernel.shape[1] // 2
    padded = extended(volume, (("gz", 0), ("gy", 1)), margin)
    return apply_passes(padded, kernel, volume.shape[0], volume.shape[1])


def on_device(camera, background, destination, offsets, shift_frac, psf_taps):
    level = background[0, 0, 0].astype(jnp.float32)
    blocks = camera[0] - level
    block_count = blocks.shape[0]
    tile_rows = blocks.shape[2]
    tile_cols = blocks.shape[3]
    slabs = lax.axis_size("gz")
    most = max(2, 2 * block_count // slabs)
    target = destination[0, 0, :, 0]
    first_plane = offsets[0, 0]
    same_slab = target[:, None] == target[None, :]
    positions = jnp.arange(block_count, dtype=jnp.int32)
    earlier = positions[None, :] < positions[:, None]
    rank = jnp.sum((same_slab & earlier).astype(jnp.int32), axis=1)
    slot = target * most + rank
    select = (jnp.arange(slabs * most, dtype=jnp.int32)[:, None] == slot[None, :]).astype(
        jnp.float32
    )
    codes_out = jnp.dot(select, (first_plane + 1).astype(jnp.float32), precision=PRECISE).reshape(
        slabs, most
    )
    fraction = shift_frac[0]
    y_matrix = interp_matrix(tile_rows, fraction[1])
    x_matrix = interp_matrix(tile_cols, fraction[2])
    smoothed = interp_blocks(blocks, fraction[0], y_matrix, x_matrix)
    packed = jnp.dot(select, smoothed.reshape(block_count, -1), precision=PRECISE)
    packed = packed.reshape((slabs, most) + smoothed.shape[1:])
    planes, codes = (
        lax.all_to_all(packed, "gz", split_axis=0, concat_axis=0, tiled=True),
        lax.all_to_all(codes_out, "gz", split_axis=0, concat_axis=0, tiled=True),
    )
    plane_count = planes.shape[2]
    valid = (codes > 0.5)[:, :, None]
    landing = (codes - 1.0)[:, :, None] + jnp.arange(plane_count, dtype=jnp.float32)[None, None, :]
    valid_wide = jnp.broadcast_to(valid, landing.shape).reshape(1, -1)
    deposit = (jnp.arange(CZ, dtype=jnp.float32)[:, None] == landing.reshape(1, -1)) & valid_wide
    deposit = deposit.astype(jnp.float32)
    total = jnp.dot(deposit, planes.reshape(-1, tile_rows * tile_cols), precision=PRECISE).reshape(
        CZ, tile_rows, tile_cols
    )
    covered = jnp.sum(deposit, axis=1)
    joined = jnp.maximum(total / (covered[:, None, None] + 1.0), DATA_FLOOR)
    kernel = psf_taps[0] / jnp.sum(psf_taps[0], axis=-1, keepdims=True)
    flipped = kernel[:, ::-1]
    view_count = lax.axis_size("view")
    estimate = lax.psum(joined, "view") / view_count
    for iteration in range(ITERS):
        blurred = spread(estimate, kernel)
        ratio = joined / blurred
        correction = spread(ratio, flipped)
        logs = jnp.log(correction)
        log_total = lax.psum(logs, "view")
        estimate = estimate * jnp.exp(log_total / view_count)
    return (estimate, joined[None])


def solution(mesh):
    return jax.shard_map(
        on_device,
        mesh=mesh,
        in_specs=(
            P("view", ("groups", "gz"), None, "gy", None),
            P("view", "gy", ("groups", "gz")),
            P("view", "gy", ("groups", "gz"), None),
            P("view", "gy", ("groups", "gz")),
            P("view", None),
            P("view", None, None),
        ),
        out_specs=(P(("groups", "gz"), "gy", None), P("view", ("groups", "gz"), "gy", None)),
        check_vma=False,
    )
```

profile of v0, /device:TPU:0, one launch (start us, length us, event | category | flops | bytes accessed | tf_op | source)
XLA Modules:
  0.0 365.3 jit_solution(4947907883737901542)
XLA Ops:
  10.3 6.3 %all-to-all-start = ((f32[4,1,16]{2,1,0:T(1,128)}), f32[4,1,16]{2,1,0:T(1,128)S(1)}, u32[]{:S(2)}, u32[]{:S(2)}) async-start(f32[4,1,16]{2,1,0:T(1,128)} %convolution_bitcast_fusion), calls=%async_computation | async-start | bytes 4096 | tf_op jit(solution)/shard_map/all_to_all | solution.py:103
  22.8 3.6 fusion.1
  30.6 5.2 %fusion.3 = f32[4,16,2,64,128]{4,1,3,2,0:T(8,128)} fusion(f32[2,64,128,32]{2,1,0,3:T(8,128)S(1)} %bitcast.103, s32[32]{0:T(128)S(1)} %multiply_add_fusion.1, s32[4,16]{1,0:T(4,128)S(1)} %multiply_add_fusion), kind=kOutput, calls=%fused_computation.39 | convolution fusion | flops 402655232 | bytes 6291840 | tf_op jit(solution)/shard_map/dot_general | solution.py:99
  35.8 5.1 %all-to-all-start.1 = ((f32[4,16,2,64,128]{4,1,3,2,0:T(8,128)}), f32[4,16,2,64,128]{4,1,3,2,0:T(8,128)}, u32[]{:S(2)}, u32[]{:S(2)}) async-start(f32[4,16,2,64,128]{4,1,3,2,0:T(8,128)} %fusion.3), calls=%async_computation.1 | async-start | bytes 8388608 | tf_op jit(solution)/shard_map/all_to_all | solution.py:102
  41.6 92.4 %all-to-all-done.1 = f32[4,16,2,64,128]{4,1,3,2,0:T(8,128)} async-done(((f32[4,16,2,64,128]{4,1,3,2,0:T(8,128)}), f32[4,16,2,64,128]{4,1,3,2,0:T(8,128)}, u32[]{:S(2)}, u32[]{:S(2)}) %all-to-all-start.1) | async-done | bytes 4194336 | tf_op jit(solution)/shard_map/all_to_all | solution.py:102
  133.9 3.5 copy.29
  137.4 5.2 %copy.50 = f32[16,8,64,128]{3,1,2,0:T(8,128)} copy(f32[16,8,64,128]{3,2,1,0:T(8,128)S(1)} %bitcast.101) | data formatting | bytes 8388608
  142.6 5.7 %copy.30 = f32[8192,128]{1,0:T(8,128)} copy(f32[8192,128]{0,1:T(8,128)} %bitcast.102) | data formatting | bytes 8388608 | tf_op jit(solution)/shard_map/dot_general | solution.py:111
  148.3 4.9 %fusion.8 = f32[8,64,128]{2,0,1:T(8,128)} fusion(f32[64,128,128]{2,1,0:T(8,128)} %bitcast.100, f32[8]{0:T(128)S(1)} %broadcast_add_fusion.1, f32[128]{0:T(128)S(1)} %add.390, pred[128]{0:T(512)(128)(4,1)S(1)} %and.14), kind=kOutput, calls=%fused_computation.45 | convolution fusion | flops 100796416 | bytes 4457120 | tf_op jit(solution)/shard_map/dot_general | solution.py:111
  153.3 22.3 %all-reduce.8.cloned.1.call-done = f32[8,64,128]{2,0,1:T(8,128)} async-done(((f32[8,64,128]{2,0,1:T(8,128)}), f32[8,64,128]{2,0,1:T(8,128)}) %all-reduce.8.cloned.1.call-update) | async-done | bytes 262160 | tf_op jit(solution)/shard_map/psum | solution.py:119
  176.6 3.4 collective-permute-start
  182.5 4.4 %collective-permute-done.1 = f32[4,64,128]{2,0,1:T(4,128)S(1)} collective-permute-done((f32[4,64,128]{2,0,1:T(4,128)S(1)}, f32[4,64,128]{2,0,1:T(4,128)S(1)}, u32[]{:S(2)}, u32[]{:S(2)}) %collective-permute-start.1) | collective-permute-done | bytes 131104 | tf_op jit(solution)/shard_map/ppermute | solution.py:22
  191.4 6.9 %fusion.19 = f32[16,72,128]{2,0,1:T(8,128)S(1)} fusion(f32[16,72,128]{2,0,1:T(8,128)S(1)} %pad_maximum_fusion, f32[]{:T(128)} %bitcast.37, f32[]{:T(128)} %bitcast.36, f32[]{:T(128)} %bitcast.35, f32[]{:T(128)} %bitcast.34, f32[]{:T(128)} %bitcast.33, f32[]{:T(128)} %bitcast.32, f32[]{:T(128)} %bitcast.31, f32[]{:T(128)} %bitcast.30, f32[]{:T(128)} %bitcast.27), kind=kLoop, calls=%fused_computation.57 | loop fusion | flops 2506752 | bytes 1179684 | tf_op jit(solution)/shard_map/add | solution.py:49
  198.4 6.0 %fusion.99 = f32[16,64,128]{2,0,1:T(8,128)S(1)} fusion(f32[16,72,128]{2,0,1:T(8,128)S(1)} %fusion.19, f32[]{:T(128)} %bitcast.44, f32[]{:T(128)} %bitcast.43, f32[]{:T(128)} %bitcast.42, f32[]{:T(128)} %bitcast.41, f32[]{:T(128)} %bitcast.40, f32[]{:T(128)} %bitcast.39, f32[]{:T(128)} %bitcast.38, f32[]{:T(128)} %bitcast.29, f32[]{:T(128)} %bitcast.26), kind=kLoop, calls=%fused_computation.169 | loop fusion | flops 2228224 | bytes 5242916 | tf_op jit(solution)/shard_map/add | solution.py:56
  204.4 5.8 %fusion.135 = f32[8,64,128]{2,0,1:T(8,128)S(1)} fusion(f32[8,64,128]{2,0,1:T(8,128)S(1)} %copy-done, f32[16,64,128]{2,0,1:T(8,128)S(1)} %fusion.99, f32[]{:T(128)} %bitcast.51, f32[]{:T(128)} %bitcast.50, f32[]{:T(128)} %bitcast.49, f32[]{:T(128)} %bitcast.48, f32[]{:T(128)} %bitcast.47, f32[]{:T(128)} %bitcast.46, f32[]{:T(128)} %bitcast.45, f32[]{:T(128)} %bitcast.28, ...), kind=kLoop, calls=%fused_computation.241 | loop fusion | flops 1179648 | bytes 2883620 | tf_op jit(solution)/shard_map/div | solution.py:122
  210.3 3.4 collective-permute-start.4
  216.7 4.1 %collective-permute-done.5 = f32[4,64,128]{2,0,1:T(4,128)S(1)} collective-permute-done((f32[4,64,128]{2,0,1:T(4,128)S(1)}, f32[4,64,128]{2,0,1:T(4,128)S(1)}, u32[]{:S(2)}, u32[]{:S(2)}) %collective-permute-start.5) | collective-permute-done | bytes 131104 | tf_op jit(solution)/shard_map/ppermute | solution.py:22
  225.4 6.9 %fusion.35 = f32[16,72,128]{2,0,1:T(8,128)S(1)} fusion(f32[16,72,128]{2,0,1:T(8,128)S(1)} %pad_maximum_fusion.1, f32[]{:T(128)} %bitcast.37, f32[]{:T(128)} %bitcast.36, f32[]{:T(128)} %bitcast.35, f32[]{:T(128)} %bitcast.34, f32[]{:T(128)} %bitcast.33, f32[]{:T(128)} %bitcast.32, f32[]{:T(128)} %bitcast.31, f32[]{:T(128)} %bitcast.30, f32[]{:T(128)} %bitcast.27), kind=kLoop, calls=%fused_computation.73 | loop fusion | flops 2506752 | bytes 1179684 | tf_op jit(solution)/shard_map/add | solution.py:49
  232.3 6.0 %fusion.91 = f32[16,64,128]{2,0,1:T(8,128)S(1)} fusion(f32[16,72,128]{2,0,1:T(8,128)S(1)} %fusion.35, f32[]{:T(128)} %bitcast.44, f32[]{:T(128)} %bitcast.43, f32[]{:T(128)} %bitcast.42, f32[]{:T(128)} %bitcast.41, f32[]{:T(128)} %bitcast.40, f32[]{:T(128)} %bitcast.39, f32[]{:T(128)} %bitcast.38, f32[]{:T(128)} %bitcast.29, f32[]{:T(128)} %bitcast.26), kind=kLoop, calls=%fused_computation.152 | loop fusion | flops 2228224 | bytes 5242916 | tf_op jit(solution)/shard_map/add | solution.py:56
  238.3 6.6 %fusion.126 = f32[8,64,128]{2,0,1:T(8,128)} fusion(f32[16,64,128]{2,0,1:T(8,128)S(1)} %fusion.91, f32[]{:T(128)} %bitcast.51, f32[]{:T(128)} %bitcast.50, f32[]{:T(128)} %bitcast.49, f32[]{:T(128)} %bitcast.48, f32[]{:T(128)} %bitcast.47, f32[]{:T(128)} %bitcast.46, f32[]{:T(128)} %bitcast.45, f32[]{:T(128)} %bitcast.28, f32[]{:T(128)} %bitcast.25), kind=kLoop, calls=%fused_computation.223 | loop fusion | flops 1114112 | bytes 2621476 | tf_op jit(solution)/shard_map/log | solution.py:124
  244.9 21.5 %all-reduce.10.cloned.1.call-done = f32[8,64,128]{2,0,1:T(8,128)} async-done(((f32[8,64,128]{2,0,1:T(8,128)}), f32[8,64,128]{2,0,1:T(8,128)}) %all-reduce.10.cloned.1.call-update) | async-done | bytes 262160 | tf_op jit(solution)/shard_map/psum | solution.py:125
  267.4 3.4 collective-permute-start.8
  273.3 4.4 %collective-permute-done.9 = f32[4,64,128]{2,0,1:T(4,128)S(1)} collective-permute-done((f32[4,64,128]{2,0,1:T(4,128)S(1)}, f32[4,64,128]{2,0,1:T(4,128)S(1)}, u32[]{:S(2)}, u32[]{:S(2)}) %collective-permute-start.9) | collective-permute-done | bytes 131104 | tf_op jit(solution)/shard_map/ppermute | solution.py:22
  282.2 6.9 %fusion.51 = f32[16,72,128]{2,0,1:T(8,128)S(1)} fusion(f32[16,72,128]{2,0,1:T(8,128)S(1)} %pad_maximum_fusion.2, f32[]{:T(128)} %bitcast.37, f32[]{:T(128)} %bitcast.36, f32[]{:T(128)} %bitcast.35, f32[]{:T(128)} %bitcast.34, f32[]{:T(128)} %bitcast.33, f32[]{:T(128)} %bitcast.32, f32[]{:T(128)} %bitcast.31, f32[]{:T(128)} %bitcast.30, f32[]{:T(128)} %bitcast.27), kind=kLoop, calls=%fused_computation.89 | loop fusion | flops 2506752 | bytes 1179684 | tf_op jit(solution)/shard_map/add | solution.py:49
  289.2 6.0 %fusion.83 = f32[16,64,128]{2,0,1:T(8,128)S(1)} fusion(f32[16,72,128]{2,0,1:T(8,128)S(1)} %fusion.51, f32[]{:T(128)} %bitcast.44, f32[]{:T(128)} %bitcast.43, f32[]{:T(128)} %bitcast.42, f32[]{:T(128)} %bitcast.41, f32[]{:T(128)} %bitcast.40, f32[]{:T(128)} %bitcast.39, f32[]{:T(128)} %bitcast.38, f32[]{:T(128)} %bitcast.29, f32[]{:T(128)} %bitcast.26), kind=kLoop, calls=%fused_computation.135 | loop fusion | flops 2228224 | bytes 5242916 | tf_op jit(solution)/shard_map/add | solution.py:56
  295.1 5.8 %fusion.117 = f32[8,64,128]{2,0,1:T(8,128)S(1)} fusion(f32[8,64,128]{2,0,1:T(8,128)S(1)} %copy-done, f32[16,64,128]{2,0,1:T(8,128)S(1)} %fusion.83, f32[]{:T(128)} %bitcast.51, f32[]{:T(128)} %bitcast.50, f32[]{:T(128)} %bitcast.49, f32[]{:T(128)} %bitcast.48, f32[]{:T(128)} %bitcast.47, f32[]{:T(128)} %bitcast.46, f32[]{:T(128)} %bitcast.45, f32[]{:T(128)} %bitcast.28, ...), kind=kLoop, calls=%fused_computation.205 | loop fusion | flops 1179648 | bytes 2883620 | tf_op jit(solution)/shard_map/div | solution.py:122
  301.0 3.4 collective-permute-start.12
  307.5 4.1 %collective-permute-done.13 = f32[4,64,128]{2,0,1:T(4,128)S(1)} collective-permute-done((f32[4,64,128]{2,0,1:T(4,128)S(1)}, f32[4,64,128]{2,0,1:T(4,128)S(1)}, u32[]{:S(2)}, u32[]{:S(2)}) %collective-permute-start.13) | collective-permute-done | bytes 131104 | tf_op jit(solution)/shard_map/ppermute | solution.py:22
  316.1 6.9 %fusion.67 = f32[16,72,128]{2,0,1:T(8,128)S(1)} fusion(f32[16,72,128]{2,0,1:T(8,128)S(1)} %pad_maximum_fusion.3, f32[]{:T(128)} %bitcast.37, f32[]{:T(128)} %bitcast.36, f32[]{:T(128)} %bitcast.35, f32[]{:T(128)} %bitcast.34, f32[]{:T(128)} %bitcast.33, f32[]{:T(128)} %bitcast.32, f32[]{:T(128)} %bitcast.31, f32[]{:T(128)} %bitcast.30, f32[]{:T(128)} %bitcast.27), kind=kLoop, calls=%fused_computation.105 | loop fusion | flops 2506752 | bytes 1179684 | tf_op jit(solution)/shard_map/add | solution.py:49
  323.1 6.0 %fusion.75 = f32[16,64,128]{2,0,1:T(8,128)S(1)} fusion(f32[16,72,128]{2,0,1:T(8,128)S(1)} %fusion.67, f32[]{:T(128)} %bitcast.44, f32[]{:T(128)} %bitcast.43, f32[]{:T(128)} %bitcast.42, f32[]{:T(128)} %bitcast.41, f32[]{:T(128)} %bitcast.40, f32[]{:T(128)} %bitcast.39, f32[]{:T(128)} %bitcast.38, f32[]{:T(128)} %bitcast.29, f32[]{:T(128)} %bitcast.26), kind=kLoop, calls=%fused_computation.118 | loop fusion | flops 2228224 | bytes 5242916 | tf_op jit(solution)/shard_map/add | solution.py:56
  329.0 6.5 %fusion.108 = f32[8,64,128]{2,0,1:T(8,128)} fusion(f32[16,64,128]{2,0,1:T(8,128)S(1)} %fusion.75, f32[]{:T(128)} %bitcast.51, f32[]{:T(128)} %bitcast.50, f32[]{:T(128)} %bitcast.49, f32[]{:T(128)} %bitcast.48, f32[]{:T(128)} %bitcast.47, f32[]{:T(128)} %bitcast.46, f32[]{:T(128)} %bitcast.45, f32[]{:T(128)} %bitcast.28, f32[]{:T(128)} %bitcast.25), kind=kLoop, calls=%fused_computation.187 | loop fusion | flops 1114112 | bytes 2621476 | tf_op jit(solution)/shard_map/log | solution.py:124
  336.3 20.7 %all-reduce.12.cloned.1.call-done = f32[8,64,128]{2,0,1:T(8,128)} async-done(((f32[8,64,128]{2,0,1:T(8,128)}), f32[8,64,128]{2,0,1:T(8,128)}) %all-reduce.12.cloned.1.call-update) | async-done | bytes 262160 | tf_op jit(solution)/shard_map/psum | solution.py:125
  (78 shorter events, 45.5 us)
Async XLA Ops:
  10.3 25.5 %all-to-all-start = ((f32[4,1,16]{2,1,0:T(1,128)}), f32[4,1,16]{2,1,0:T(1,128)S(1)}, u32[]{:S(2)}, u32[]{:S(2)}) async-start(f32[4,1,16]{2,1,0:T(1,128)} %convolution_bitcast_fusion), calls=%async_computation | async-start | bytes 4096 | tf_op jit(solution)/shard_map/all_to_all | solution.py:103
  35.8 98.1 %all-to-all-start.1 = ((f32[4,16,2,64,128]{4,1,3,2,0:T(8,128)}), f32[4,16,2,64,128]{4,1,3,2,0:T(8,128)}, u32[]{:S(2)}, u32[]{:S(2)}) async-start(f32[4,16,2,64,128]{4,1,3,2,0:T(8,128)} %fusion.3), calls=%async_computation.1 | async-start | bytes 8388608 | tf_op jit(solution)/shard_map/all_to_all | solution.py:102
  40.9 134.7 %all-reduce.8.cloned.1.call-start = ((), (), s32[]{:S(2)}) async-start(), calls=%async_computation.2 | async-start | bytes 524288 | tf_op jit(solution)/shard_map/psum | solution.py:119
  148.3 5.0 %copy-start.2 = (f32[1,3,9]{2,0,1:T(1,128)S(1)}, f32[1,3,9]{2,0,1:T(1,128)}, u32[]{:S(2)}) copy-start(f32[1,3,9]{2,0,1:T(1,128)} %param.11) | copy-start | bytes 328
  153.2 113.2 %all-reduce.10.cloned.1.call-start = ((), (), s32[]{:S(2)}) async-start(), calls=%async_computation.3 | async-start | bytes 524288 | tf_op jit(solution)/shard_map/psum | solution.py:125
  176.6 5.9 %collective-permute-start = (f32[4,64,128]{2,0,1:T(4,128)S(1)}, f32[4,64,128]{2,0,1:T(4,128)S(1)}, u32[]{:S(2)}, u32[]{:S(2)}) collective-permute-start(f32[4,64,128]{2,0,1:T(4,128)S(1)} %get-tuple-element.26), channel_id=1, source_target_pairs={{0,4},{4,8},{8,12},{1,5},{5,9},{9,13},{2,6},{6,10},{10,14},{3,7},{... | collective-permute-start | bytes 393224 | tf_op jit(solution)/shard_map/ppermute | solution.py:19
  180.0 6.9 %collective-permute-start.1 = (f32[4,64,128]{2,0,1:T(4,128)S(1)}, f32[4,64,128]{2,0,1:T(4,128)S(1)}, u32[]{:S(2)}, u32[]{:S(2)}) collective-permute-start(f32[4,64,128]{2,0,1:T(4,128)S(1)} %get-tuple-element.27), channel_id=1, source_target_pairs={{4,0},{8,4},{12,8},{5,1},{9,5},{13,9},{6,2},{10,6},{14,10},{7,3},{... | collective-permute-start | bytes 393224 | tf_op jit(solution)/shard_map/ppermute | solution.py:22
  186.9 3.3 collective-permute-start.2
  188.2 3.1 collective-permute-start.3
  198.4 6.0 %copy-start = (f32[8,64,128]{2,0,1:T(8,128)S(1)}, f32[8,64,128]{2,0,1:T(8,128)}, u32[]{:S(2)}) copy-start(f32[8,64,128]{2,0,1:T(8,128)} %fusion.8) | copy-start | bytes 786436
  210.3 6.5 %collective-permute-start.4 = (f32[4,64,128]{2,0,1:T(4,128)S(1)}, f32[4,64,128]{2,0,1:T(4,128)S(1)}, u32[]{:S(2)}, u32[]{:S(2)}) collective-permute-start(f32[4,64,128]{2,0,1:T(4,128)S(1)} %get-tuple-element.24), channel_id=1, source_target_pairs={{0,4},{4,8},{8,12},{1,5},{5,9},{9,13},{2,6},{6,10},{10,14},{3,7},{... | collective-permute-start | bytes 393224 | tf_op jit(solution)/shard_map/ppermute | solution.py:19
  213.7 7.2 %collective-permute-start.5 = (f32[4,64,128]{2,0,1:T(4,128)S(1)}, f32[4,64,128]{2,0,1:T(4,128)S(1)}, u32[]{:S(2)}, u32[]{:S(2)}) collective-permute-start(f32[4,64,128]{2,0,1:T(4,128)S(1)} %get-tuple-element.25), channel_id=1, source_target_pairs={{4,0},{8,4},{12,8},{5,1},{9,5},{13,9},{6,2},{10,6},{14,10},{7,3},{... | collective-permute-start | bytes 393224 | tf_op jit(solution)/shard_map/ppermute | solution.py:22
  220.9 2.8 collective-permute-start.6
  222.2 3.1 collective-permute-start.7
  238.3 28.1 %copy-start.1 = (f32[8,64,128]{2,0,1:T(8,128)S(1)}, f32[8,64,128]{2,0,1:T(8,128)}, u32[]{:S(2)}) copy-start(f32[8,64,128]{2,0,1:T(8,128)} %all-reduce.8.cloned.1.call-done) | copy-start | bytes 786436
  244.9 112.2 %all-reduce.12.cloned.1.call-start = ((), (), s32[]{:S(2)}) async-start(), calls=%async_computation.4 | async-start | bytes 524288 | tf_op jit(solution)/shard_map/psum | solution.py:125
  267.4 5.9 %collective-permute-start.8 = (f32[4,64,128]{2,0,1:T(4,128)S(1)}, f32[4,64,128]{2,0,1:T(4,128)S(1)}, u32[]{:S(2)}, u32[]{:S(2)}) collective-permute-start(f32[4,64,128]{2,0,1:T(4,128)S(1)} %get-tuple-element.22), channel_id=1, source_target_pairs={{0,4},{4,8},{8,12},{1,5},{5,9},{9,13},{2,6},{6,10},{10,14},{3,7},{... | collective-permute-start | bytes 393224 | tf_op jit(solution)/shard_map/ppermute | solution.py:19
  270.8 6.9 %collective-permute-start.9 = (f32[4,64,128]{2,0,1:T(4,128)S(1)}, f32[4,64,128]{2,0,1:T(4,128)S(1)}, u32[]{:S(2)}, u32[]{:S(2)}) collective-permute-start(f32[4,64,128]{2,0,1:T(4,128)S(1)} %get-tuple-element.23), channel_id=1, source_target_pairs={{4,0},{8,4},{12,8},{5,1},{9,5},{13,9},{6,2},{10,6},{14,10},{7,3},{... | collective-permute-start | bytes 393224 | tf_op jit(solution)/shard_map/ppermute | solution.py:22
  277.7 2.6 collective-permute-start.10
  279.0 3.1 collective-permute-start.11
  301.0 6.5 %collective-permute-start.12 = (f32[4,64,128]{2,0,1:T(4,128)S(1)}, f32[4,64,128]{2,0,1:T(4,128)S(1)}, u32[]{:S(2)}, u32[]{:S(2)}) collective-permute-start(f32[4,64,128]{2,0,1:T(4,128)S(1)} %get-tuple-element.20), channel_id=1, source_target_pairs={{0,4},{4,8},{8,12},{1,5},{5,9},{9,13},{2,6},{6,10},{10,14},{3,7},{... | collective-permute-start | bytes 393224 | tf_op jit(solution)/shard_map/ppermute | solution.py:19
  304.4 7.2 %collective-permute-start.13 = (f32[4,64,128]{2,0,1:T(4,128)S(1)}, f32[4,64,128]{2,0,1:T(4,128)S(1)}, u32[]{:S(2)}, u32[]{:S(2)}) collective-permute-start(f32[4,64,128]{2,0,1:T(4,128)S(1)} %get-tuple-element.21), channel_id=1, source_target_pairs={{4,0},{8,4},{12,8},{5,1},{9,5},{13,9},{6,2},{10,6},{14,10},{7,3},{... | collective-permute-start | bytes 393224 | tf_op jit(solution)/shard_map/ppermute | solution.py:22
  311.6 2.6 collective-permute-start.14
  312.9 3.1 collective-permute-start.15
Sparse Core Ops, SparseCore 0:
  153.3 22.2 all-reduce.7
  245.0 21.3 all-reduce.9
  335.7 21.3 all-reduce.11
where the time goes:
time: 367 us; the launch traced here: 365 us
  waiting for transfers between devices  185 us (50%)
  other arithmetic  83.9 us (23%)
  starting transfers between devices  40.8 us (11%)
  local copies, waits for them, and re-layouts  20.8 us (6%)
  matrix products  17.8 us (5%)
  between operations  16.7 us (5%)
    all_to_all x1, waiting for transfers between devices, on_device(): lax.all_to_all(packed, 'gz', split_axis=0, concat_axis=0, tiled=True)  92.4 us
    psum x2, waiting for transfers between devices, on_device(): log_total = lax.psum(logs, 'view')  42.2 us
    add x4, other arithmetic, along_last(): result = result + weights[offset] * padded[..., offset:offset + span_cells]  27.7 us
    add x4, other arithmetic, valid_pass(): result + weights[offset] * lax.slice_in_dim(padded, offset, offset + out_...  23.9 us
    ppermute x8, waiting for transfers between devices, extended(): lax.ppermute(lax.slice_in_dim(block, 0, width, axis=dim), axis, backward)  23.2 us
    psum x1, waiting for transfers between devices, on_device(): estimate = lax.psum(joined, 'view') / view_count  22.3 us
    ppermute x8, starting transfers between devices, extended(): lax.ppermute(lax.slice_in_dim(block, block.shape[dim] - width, None, axis...  18.7 us
    log x2, other arithmetic, on_device(): logs = jnp.log(correction)  13.1 us
  transfers between devices with their start and end apart: 21, of which 16 were waited for; matrix products, arithmetic and copies ran while one was open for 5% of the time, Pallas kernels for 0%

commit v1 on v0

v1 whole, which is shorter than its diff:
```python
import functools

import jax
import jax.numpy as jnp
from jax import lax
from jax.experimental import pallas as pl
from jax.experimental.pallas import tpu as pltpu
from jax.sharding import PartitionSpec as P

CZ = 8
ITERS = 2


DATA_FLOOR = 0.25
PRECISE = lax.Precision.HIGHEST
F32 = jnp.float32
SUB = 8
SMEM = pl.BlockSpec(memory_space=pltpu.SMEM)
VMEM = pl.BlockSpec(memory_space=pltpu.VMEM)
VMEM_BYTES = 48 * 1024 * 1024


def bit_count(count):
    bits = count.bit_length() - 1
    assert count == 1 << bits
    return bits


def reversed_bits(value, bits):
    result = 0
    for bit in range(bits):
        result = result | (((value >> bit) & 1) << (bits - 1 - bit))
    return result


def deposit_kernel(place_ref, target_ref, first_ref, level_ref, fraction_ref, camera_ref, out_ref, *, bits, section):
    per_step, planes, rows, cols = camera_ref.shape
    step = pl.program_id(0)

    @pl.when(step == 0)
    def _():
        out_ref[...] = jnp.zeros(out_ref.shape, F32)

    level = level_ref[0].astype(F32)
    fraction = fraction_ref[0]
    keep = 1.0 - fraction
    plane_at = lax.broadcasted_iota(jnp.int32, (CZ, cols), 0)

    def one(index, carry):
        block = step * per_step + index
        slab = reversed_bits(target_ref[block] ^ place_ref[0], bits)
        first = first_ref[block]
        start = pl.multiple_of(slab * section, SUB)
        base = pl.multiple_of(start + first * rows, SUB)
        lower = camera_ref[index, 0] - level
        for plane in range(planes - 1):
            upper = camera_ref[index, plane + 1] - level
            here = pl.ds(pl.multiple_of(base + plane * rows, SUB), rows)
            out_ref[here, :] += keep * lower + fraction * upper
            lower = upper
        counts = pl.ds(pl.multiple_of(start + CZ * rows, SUB), CZ)
        landed = (plane_at >= first) & (plane_at < first + planes - 1)
        out_ref[counts, :] += landed.astype(F32)
        return carry

    lax.fori_loop(0, per_step, one, 0)


def deposit(camera, target, first, level, fraction, place, slabs):
    blocks, planes, rows, cols = camera.shape
    section = CZ * rows + CZ
    per_step = SUB if blocks % SUB == 0 else 1
    return pl.pallas_call(
        functools.partial(deposit_kernel, bits=bit_count(slabs), section=section),
        grid=(blocks // per_step,),
        in_specs=[SMEM] * 5 + [pl.BlockSpec((per_step, planes, rows, cols), lambda i: (i, 0, 0, 0))],
        out_specs=pl.BlockSpec((slabs * section, cols), lambda i: (0, 0)),
        out_shape=jax.ShapeDtypeStruct((slabs * section, cols), F32),
        compiler_params=pltpu.CompilerParams(vmem_limit_bytes=VMEM_BYTES),
        name="deposit",
    )(place, target, first, level, fraction, camera)


def butterfly(sums, slabs, section):
    bits = bit_count(slabs)
    own = sums
    count = slabs
    late = None
    for bit in range(bits):
        half = count // 2
        pairs = [(i, i ^ (1 << bit)) for i in range(slabs)]
        keep, send = own[: half * section], own[half * section :]
        if late is not None:
            send = send + late[1]
            keep = keep + late[0]
        if half > 1:
            cut = half // 2 * section
            onward = lax.ppermute(send[cut:], "gz", pairs)
            stays = lax.ppermute(send[:cut], "gz", pairs)
            late = (stays, onward)
            next_half = half // 2
            own = keep
        else:
            arrived = lax.ppermute(send, "gz", pairs)
            return keep, arrived
        count = half
    return own, jnp.zeros_like(own)


def join_kernel(fraction_ref, kept_ref, arrived_ref, taps_ref, joined_ref, message_ref, *, rows):
    cols = kept_ref.shape[1]
    total = kept_ref[...] + arrived_ref[...]
    planes = total[: CZ * rows].reshape(CZ, rows, cols)
    counts = total[CZ * rows :]
    fy, fx = fraction_ref[1], fraction_ref[2]
    row_at = lax.broadcasted_iota(jnp.int32, (rows, cols), 0)
    col_at = lax.broadcasted_iota(jnp.int32, (rows, cols), 1)
    for plane in range(CZ):
        part = planes[plane]
        follow = jnp.where(row_at == rows - 1, part, pltpu.roll(part, rows - 1, 0))
        part = (1.0 - fy) * part + fy * follow
        follow = jnp.where(col_at == cols - 1, part, pltpu.roll(part, cols - 1, 1))
        part = (1.0 - fx) * part + fx * follow
        part = jnp.maximum(part / (counts[plane : plane + 1] + 1.0), DATA_FLOOR)
        joined_ref[plane] = part
        message_ref[plane * rows : (plane + 1) * rows] = part
    message_ref[CZ * rows :] = taps_ref[...]


def join(kept, arrived, fraction, taps, rows):
    cols = kept.shape[1]
    return pl.pallas_call(
        functools.partial(join_kernel, rows=rows),
        in_specs=[SMEM, VMEM, VMEM, VMEM],
        out_specs=[VMEM, VMEM],
        out_shape=[jax.ShapeDtypeStruct((CZ, rows, cols), F32), jax.ShapeDtypeStruct(kept.shape, F32)],
        compiler_params=pltpu.CompilerParams(vmem_limit_bytes=VMEM_BYTES),
        name="join",
    )(fraction, kept, arrived, taps)


def taps_sum(values, weights):
    result = weights[0] * values[0]
    for offset in range(1, len(weights)):
        result = result + weights[offset] * values[offset]
    return result


def update_kernel(
    flag_ref, taps_ref, band_ref, own_ref, below_ref, above_ref, low_rows_ref, high_rows_ref, *rest, views, margin, first
):
    if first:
        out_ref, *scratch = rest
    else:
        est_ref, est_below_ref, est_above_ref, est_low_ref, est_high_ref, out_ref, *scratch = rest
    estimate, joined, first_pass, second_pass, ratio, back_first, back_second = scratch
    _, planes, rows, cols = own_ref.shape
    wide = 2 * margin
    flag_low, flag_high = flag_ref[0], flag_ref[1]
    low, body, high = slice(0, wide), slice(wide, wide + rows), slice(wide + rows, 2 * wide + rows)

    def spread_rows(ref, part):
        return [(body, part[0], part[1], None), (low, part[2], part[3], flag_low), (high, part[4], part[3], flag_high)]

    below_at = 0
    above_at = below_ref.shape[0]
    own_at = 2 * above_at
    for view in range(views):
        pieces = (
            (0, margin, below_ref, view * margin, below_at + view * margin),
            (margin, planes, own_ref.at[view], 0, own_at + view * planes),
            (margin + planes, margin, above_ref, view * margin, above_at + view * margin),
        )
        for to, length, source, at, edge_at in pieces:
            joined[view, to : to + length, body] = source[at : at + length]
            joined[view, to : to + length, low] = low_rows_ref[edge_at : edge_at + length] * flag_low
            joined[view, to : to + length, high] = high_rows_ref[edge_at : edge_at + length] * flag_high
    if first:
        inner = joined[0]
        for view in range(1, views):
            inner = inner + joined[view]
        estimate[margin : margin + planes + 2 * margin] = inner / views
        at = views * margin
        for to, source, edge_at in ((0, below_ref, below_at + at), (planes + 3 * margin, above_ref, above_at + at)):
            estimate[to : to + margin, body] = source[at : at + margin]
            estimate[to : to + margin, low] = low_rows_ref[edge_at : edge_at + margin] * flag_low
            estimate[to : to + margin, high] = high_rows_ref[edge_at : edge_at + margin] * flag_high
    else:
        for to, source, edge_at in ((0, est_below_ref, 0), (planes, est_ref, planes), (2 * planes, est_above_ref, 2 * planes)):
            estimate[to : to + planes, body] = source[...]
            estimate[to : to + planes, low] = est_low_ref[edge_at : edge_at + planes] * flag_low
            estimate[to : to + planes, high] = est_high_ref[edge_at : edge_at + planes] * flag_high

    taps = 2 * margin + 1
    mid_planes, mid_rows = planes + 2 * margin, rows + 2 * margin
    weights = [[[taps_ref[(view * 3 + dim) * taps + tap] for tap in range(taps)] for dim in range(3)] for view in range(views)]

    def along_z(tile, carry):
        here = pl.ds(pl.multiple_of(tile * SUB, SUB), SUB)
        values = [estimate[plane, here, :] for plane in range(planes + 4 * margin)]
        for view in range(views):
            for plane in range(mid_planes):
                first_pass[view, plane, here, :] = taps_sum(values[plane : plane + taps], weights[view][0])
        return carry

    lax.fori_loop(0, (rows + 4 * margin) // SUB, along_z, 0)

    def along_y(plane, carry):
        for view in range(views):
            values = [first_pass[view, plane, tap : tap + mid_rows, :] for tap in range(taps)]
            second_pass[view, plane] = taps_sum(values, weights[view][1])
        return carry

    lax.fori_loop(0, mid_planes, along_y, 0)

    per = 4
    for view in range(views):
        def along_x(index, carry, view=view):
            here = pl.ds(index * per, per)
            values = second_pass[view, here].reshape(per * mid_rows, cols)
            blurred = jnp.dot(values, band_ref[view, 0], precision=PRECISE, preferred_element_type=F32)
            ratio[view, here] = joined[view, here, margin : margin + mid_rows, :] / blurred.reshape(per, mid_rows, cols)
            return carry

        lax.fori_loop(0, mid_planes // per, along_x, 0)

    def back_z(tile, carry):
        here = pl.ds(pl.multiple_of(tile * SUB, SUB), SUB)
        for view in range(views):
            values = [ratio[view, plane, here, :] for plane in range(mid_planes)]
            for plane in range(planes):
                back_first[view, plane, here, :] = taps_sum(values[plane : plane + taps], weights[view][0][::-1])
        return carry

    lax.fori_loop(0, mid_rows // SUB, back_z, 0)

    def back_y(plane, carry):
        for view in range(views):
            values = [back_first[view, plane, tap : tap + rows, :] for tap in range(taps)]
            back_second[view, plane] = taps_sum(values, weights[view][1][::-1])
        return carry

    lax.fori_loop(0, planes, back_y, 0)

    def back_x(index, carry):
        here = pl.ds(index * per, per)
        logs = None
        for view in range(views):
            values = back_second[view, here].reshape(per * rows, cols)
            correction = jnp.dot(values, band_ref[view, 1], precision=PRECISE, preferred_element_type=F32)
            one = jnp.log(correction)
            logs = one if logs is None else logs + one
        old = estimate[pl.ds(2 * margin + index * per, per), body, :]
        out_ref[here] = old * jnp.exp(logs / views).reshape(per, rows, cols)
        return carry

    lax.fori_loop(0, planes // per, back_x, 0)


def update(flags, taps, bands, own, below, above, low_rows, high_rows, later, margin):
    views, planes, rows, cols = own.shape
    arrays = [flags, taps, bands, own, below, above, low_rows, high_rows] + list(later)
    mid_planes, mid_rows = planes + 2 * margin, rows + 2 * margin
    scratch = [
        (planes + 4 * margin, rows + 4 * margin),
        (views, mid_planes, rows + 4 * margin),
        (views, mid_planes, rows + 4 * margin),
        (views, mid_planes, mid_rows),
        (views, mid_planes, mid_rows),
        (views, planes, mid_rows),
        (views, planes, rows),
    ]
    return pl.pallas_call(
        functools.partial(update_kernel, views=views, margin=margin, first=not later),
        in_specs=[SMEM, SMEM] + [VMEM] * (len(arrays) - 2),
        out_specs=VMEM,
        out_shape=jax.ShapeDtypeStruct((planes, rows, cols), F32),
        scratch_shapes=[pltpu.VMEM(shape + (cols,), F32) for shape in scratch],
        compiler_params=pltpu.CompilerParams(vmem_limit_bytes=VMEM_BYTES),
        name="update",
    )(*arrays)


def from_beside(axis, upward, downward):
    count = lax.axis_size(axis)
    up = [(i, i + 1) for i in range(count - 1)]
    down = [(target, source) for source, target in up]
    return lax.ppermute(upward, axis, up), lax.ppermute(downward, axis, down)


def edge_rows(pieces, width):
    count = lax.axis_size("gy")
    rows = pieces[0].shape[-2]
    if count == 2:
        at = jnp.where(lax.axis_index("gy") == 0, rows - width, 0)
        parts = [lax.dynamic_slice_in_dim(piece, at, width, axis=1) for piece in pieces]
        arrived = lax.ppermute(jnp.concatenate(parts), "gy", [(0, 1), (1, 0)])
        return arrived, arrived
    upward = jnp.concatenate([piece[:, rows - width :] for piece in pieces])
    downward = jnp.concatenate([piece[:, :width] for piece in pieces])
    return from_beside("gy", upward, downward)


def from_views(message):
    count = lax.axis_size("view")
    if count == 2:
        return jnp.stack([message, lax.ppermute(message, "view", [(0, 1), (1, 0)])])
    return lax.all_gather(message, "view")


def on_device(camera, background, destination, offsets, shift_frac, psf_taps):
    slabs = lax.axis_size("gz")
    views = lax.axis_size("view")
    _, blocks, _, rows, cols = camera.shape
    taps = psf_taps.shape[-1]
    margin = taps // 2
    section = CZ * rows + CZ
    place = lax.axis_index("gz").astype(jnp.int32).reshape(1)
    fraction = shift_frac[0]
    sums = deposit(
        camera[0], destination.reshape(blocks), offsets.reshape(blocks), background.reshape(1), fraction, place, slabs
    )
    kept, arrived = butterfly(sums, slabs, section)
    own_taps = jnp.pad(psf_taps[0], ((0, CZ - 3), (0, cols - taps)))
    joined, message = join(kept, arrived, fraction, own_taps, rows)

    messages = from_views(message)
    all_joined = messages[:, : CZ * rows].reshape(views, CZ, rows, cols)
    all_taps = messages[:, CZ * rows : CZ * rows + 3, :taps]
    kernels = all_taps / jnp.sum(all_taps, axis=-1, keepdims=True)
    places = jnp.arange(cols, dtype=jnp.int32)
    shift = places[:, None] - places[None, :] + margin
    band = sum(jnp.where(shift == tap, kernels[:, 2, tap, None, None], 0.0) for tap in range(taps))
    bands = jnp.stack([band, jnp.swapaxes(band, 1, 2)], axis=1)
    flat_taps = kernels.reshape(-1)

    estimate = jnp.sum(all_joined, axis=0) / views
    upward = jnp.concatenate([all_joined[:, CZ - margin :].reshape(views * margin, rows, cols), estimate[: CZ - margin]])
    downward = jnp.concatenate([all_joined[:, :margin].reshape(views * margin, rows, cols), estimate[margin:]])
    below, above = from_beside("gz", upward, downward)
    wide = 2 * margin
    low_rows, high_rows = edge_rows([below, above, all_joined.reshape(views * CZ, rows, cols)], wide)
    row_band = lax.axis_index("gy")
    flags = jnp.stack([row_band > 0, row_band < lax.axis_size("gy") - 1]).astype(F32)

    later = ()
    for iteration in range(ITERS):
        if iteration:
            est_below, est_above = from_beside("gz", estimate, estimate)
            later = (estimate, est_below, est_above) + edge_rows([est_below, estimate, est_above], wide)
        estimate = update(flags, flat_taps, bands, all_joined, below, above, low_rows, high_rows, later, margin)
    return (estimate, joined[None])


def solution(mesh):
    return jax.shard_map(
        on_device,
        mesh=mesh,
        in_specs=(
            P("view", ("groups", "gz"), None, "gy", None),
            P("view", "gy", ("groups", "gz")),
            P("view", "gy", ("groups", "gz"), None),
            P("view", "gy", ("groups", "gz")),
            P("view", None),
            P("view", None, None),
        ),
        out_specs=(P(("groups", "gz"), "gy", None), P("view", ("groups", "gz"), "gy", None)),
        check_vma=False,
    )
```

time: 367 us -> 79.6 us (0.22)
  waiting for transfers between devices: 185 us -> 37.9 us
  other arithmetic: 83.9 us -> 1.26 us
  starting transfers between devices: 40.8 us -> 18.6 us
  matrix products: 17.8 us -> 0 us
  local copies, waits for them, and re-layouts: 20.8 us -> 4.27 us
  Pallas kernels: 0 us -> 15.8 us
  between operations: 16.7 us -> 1.57 us
    all_to_all x2 -> x0, waiting for transfers between devices: 92.4 us -> none  [the longest x1 92.4 us: on_device(): lax.all_to_all(packed, 'gz', split_axis=0, concat_axis=0, tiled=True)]
    psum x3 -> x0, waiting for transfers between devices: 64.5 us -> none  [the longest x2 42.2 us: on_device(): log_total = lax.psum(logs, 'view')]
    add x11 -> x4, other arithmetic: 52.4 us -> 0.57 us  [the longest x2 0.46 us: on_device(): sum((jnp.where(shift == tap, kernels[:, 2, tap, None, None], 0.0) for tap...]
    dot_general x5 -> x0, matrix products: 17.8 us -> none  [the longest x1 5.21 us: on_device(): jnp.dot(select, smoothed.reshape(block_count, -1), precision=PRECISE)]
    pallas_call x0 -> x4, Pallas kernels: none -> 15.8 us  [the longest x2 13 us: update(): pl.pallas_call(functools.partial(update_kernel, views=views, margin=margi...]
    log x2 -> x0, other arithmetic: 13.1 us -> none  [on_device(): logs = jnp.log(correction)]
    div x4 -> x2, other arithmetic: 12.7 us -> 0.1 us  [the longest x1 0.08 us: on_device(): kernels = all_taps / jnp.sum(all_taps, axis=-1, keepdims=True)]
    all_to_all x2 -> x0, starting transfers between devices: 11.4 us -> none  [the longest x1 6.32 us: on_device(): lax.all_to_all(codes_out, 'gz', split_axis=0, concat_axis=0, tiled=True)]
  transfers between devices with their start and end apart: 21 -> 10, of which waited for: 16 -> 10; matrix products, arithmetic and copies ran while one was open for 5% -> 2% of each run, Pallas kernels for 0% -> 0%
where the time goes in v1:
time: 79.6 us; the launch traced here: 79.3 us
  waiting for transfers between devices  37.9 us (48%)
  starting transfers between devices  18.6 us (23%)
  Pallas kernels  15.8 us (20%)
  local copies, waits for them, and re-layouts  4.27 us (5%)
  between operations  1.57 us (2%)
  other arithmetic  1.26 us (2%)
    ppermute x4, waiting for transfers between devices, from_beside(): return (lax.ppermute(upward, axis, up), lax.ppermute(downward, axis, down))  13.6 us
    pallas_call x2, Pallas kernels, update(): pl.pallas_call(functools.partial(update_kernel, views=views, margin=margi...  13 us
    ppermute x4, starting transfers between devices, from_beside(): return (lax.ppermute(upward, axis, up), lax.ppermute(downward, axis, down))  9.4 us
    ppermute x1, waiting for transfers between devices, butterfly(): stays = lax.ppermute(send[:cut], 'gz', pairs)  8.53 us
    ppermute x1, waiting for transfers between devices, butterfly(): onward = lax.ppermute(send[cut:], 'gz', pairs)  6.21 us
    ppermute x1, waiting for transfers between devices, from_views(): return jnp.stack([message, lax.ppermute(message, 'view', [(0, 1), (1, 0)])])  4.78 us
    unnamed x13, local copies, waits for them, and re-layouts  3.86 us
    ppermute x1, starting transfers between devices, butterfly(): onward = lax.ppermute(send[cut:], 'gz', pairs)  3.09 us
  transfers between devices with their start and end apart: 10, of which 10 were waited for; matrix products, arithmetic and copies ran while one was open for 2% of the time, Pallas kernels for 0%

profile of v1, /device:TPU:0, one launch (start us, length us, event | category | flops | bytes accessed | tf_op | source)
XLA Modules:
  0.0 79.3 jit_solution(14158630314005273362)
XLA Ops:
  1.3 1.9 %copy-done = f32[1,32,3,64,128]{4,3,2,1,0:T(8,128)S(1)} copy-done((f32[1,32,3,64,128]{4,3,2,1,0:T(8,128)S(1)}, f32[1,32,3,64,128]{4,3,2,1,0:T(8,128)}, u32[]{:S(2)}) %copy-start) | copy-done | bytes 3145752
  3.2 0.7 copy-done.1
  3.8 0.7 copy-done.3
  4.5 0.7 copy-done.4
  5.1 1.4 %deposit.1 = f32[2080,128]{1,0:T(8,128)S(1)} custom-call(s32[1]{0:T(128)} %bitcast.3.place_ref, s32[32]{0:T(128)S(1)} %bitcast.30, s32[32]{0:T(128)S(1)} %bitcast.31, s32[1]{0:T(128)} %bitcast.20.level_ref, f32[3]{0:T(128)S(1)} %bitcast.28, f32[32,3,64,128]{3,2,1,0:T(8,128)S(1)} %bitcast.25), custom_call_target="tpu_custom_call" | custom-call | tf_op jit(solution)/shard_map/deposit/pallas_call | solution.py:73
  6.6 3.1 %collective-permute-start.1 = (f32[520,128]{1,0:T(8,128)S(1)}, f32[520,128]{1,0:T(8,128)S(1)}, u32[]{:S(2)}, u32[]{:S(2)}) collective-permute-start(f32[520,128]{1,0:T(8,128)S(1)} %slice.93), channel_id=1, source_target_pairs={{0,4},{4,0},{8,12},{12,8},{1,5},{5,1},{9,13},{13,9},{2,6},{6,2},{1... | collective-permute-start | bytes 798728 | tf_op jit(solution)/shard_map/ppermute | solution.py:98
  9.8 6.2 %collective-permute-done.1 = f32[520,128]{1,0:T(8,128)S(1)} collective-permute-done((f32[520,128]{1,0:T(8,128)S(1)}, f32[520,128]{1,0:T(8,128)S(1)}, u32[]{:S(2)}, u32[]{:S(2)}) %collective-permute-start.1) | collective-permute-done | bytes 266272 | tf_op jit(solution)/shard_map/ppermute | solution.py:98
  16.1 1.8 %collective-permute-start = (f32[520,128]{1,0:T(8,128)S(1)}, f32[520,128]{1,0:T(8,128)S(1)}, u32[]{:S(2)}, u32[]{:S(2)}) collective-permute-start(f32[520,128]{1,0:T(8,128)S(1)} %get-tuple-element.20), channel_id=1, source_target_pairs={{0,4},{4,0},{8,12},{12,8},{1,5},{5,1},{9,13},{13,9},{2,6},{6,2},{1... | collective-permute-start | bytes 798728 | tf_op jit(solution)/shard_map/ppermute | solution.py:99
  18.0 2.7 %collective-permute-start.2 = (f32[520,128]{1,0:T(8,128)S(1)}, f32[520,128]{1,0:T(8,128)S(1)}, u32[]{:S(2)}, u32[]{:S(2)}) collective-permute-start(f32[520,128]{1,0:T(8,128)S(1)} %get-tuple-element.19), channel_id=1, source_target_pairs={{0,8},{4,12},{8,0},{12,4},{1,9},{5,13},{9,1},{13,5},{2,10},{6,14},... | collective-permute-start | bytes 798728 | tf_op jit(solution)/shard_map/ppermute | solution.py:104
  20.7 8.5 %collective-permute-done = f32[520,128]{1,0:T(8,128)S(1)} collective-permute-done((f32[520,128]{1,0:T(8,128)S(1)}, f32[520,128]{1,0:T(8,128)S(1)}, u32[]{:S(2)}, u32[]{:S(2)}) %collective-permute-start) | collective-permute-done | bytes 266272 | tf_op jit(solution)/shard_map/ppermute | solution.py:99
  29.3 2.4 %collective-permute-done.2.arrived_ref = f32[520,128]{1,0:T(8,128)S(1)} collective-permute-done((f32[520,128]{1,0:T(8,128)S(1)}, f32[520,128]{1,0:T(8,128)S(1)}, u32[]{:S(2)}, u32[]{:S(2)}) %collective-permute-start.2) | collective-permute-done | bytes 266272 | tf_op jit(solution)/shard_map/ppermute | solution.py:104
  31.7 1.4 %join.1 = (f32[8,64,128]{2,1,0:T(8,128)}, f32[520,128]{1,0:T(8,128)S(1)}) custom-call(f32[3]{0:T(128)S(1)} %bitcast.29, f32[520,128]{1,0:T(8,128)S(1)} %slice_add_fusion.1.kept_ref, f32[520,128]{1,0:T(8,128)S(1)} %collective-permute-done.2.arrived_ref, f32[8,128]{1,0:T(8,128)S(1)} %pad.4.taps_ref), custom_call_target="tpu_custom_call" | custom-call | tf_op jit(solution)/shard_map/join/pallas_call | solution.py:132
  33.1 1.5 %collective-permute-start.3 = (f32[520,128]{1,0:T(8,128)S(1)}, f32[520,128]{1,0:T(8,128)S(1)}, u32[]{:S(2)}, u32[]{:S(2)}) collective-permute-start(f32[520,128]{1,0:T(8,128)S(1)} %get-tuple-element.4), channel_id=1, source_target_pairs={{0,2},{2,0},{1,3},{3,1},{4,6},{6,4},{5,7},{7,5},{8,10},{10,8},{9,1... | collective-permute-start | bytes 798728 | tf_op jit(solution)/shard_map/ppermute | solution.py:307
  34.7 4.8 %collective-permute-done.3 = f32[520,128]{1,0:T(8,128)S(1)} collective-permute-done((f32[520,128]{1,0:T(8,128)S(1)}, f32[520,128]{1,0:T(8,128)S(1)}, u32[]{:S(2)}, u32[]{:S(2)}) %collective-permute-start.3) | collective-permute-done | bytes 266272 | tf_op jit(solution)/shard_map/ppermute | solution.py:307
  39.5 0.1 fusion.19
  39.6 0.1 fusion.18
  39.8 2.3 %collective-permute-start.4 = (f32[12,64,128]{2,1,0:T(8,128)S(1)}, f32[12,64,128]{2,1,0:T(8,128)S(1)}, u32[]{:S(2)}, u32[]{:S(2)}) collective-permute-start(f32[12,64,128]{2,1,0:T(8,128)S(1)} %pad_maximum_fusion.1), channel_id=1, source_target_pairs={{0,4},{4,8},{8,12},{1,5},{5,9},{9,13},{2,6},{6,10},{10,14},{3,7},{... | collective-permute-start | bytes 1179656 | tf_op jit(solution)/shard_map/ppermute | solution.py:288
  42.2 0.2 slice_reduce_fusion.8
  42.4 1.3 %collective-permute-start.5 = (f32[12,64,128]{2,1,0:T(8,128)S(1)}, f32[12,64,128]{2,1,0:T(8,128)S(1)}, u32[]{:S(2)}, u32[]{:S(2)}) collective-permute-start(f32[12,64,128]{2,1,0:T(8,128)S(1)} %pad_maximum_fusion.2), channel_id=1, source_target_pairs={{4,0},{8,4},{12,8},{5,1},{9,5},{13,9},{6,2},{10,6},{14,10},{7,3},{... | collective-permute-start | bytes 1179656 | tf_op jit(solution)/shard_map/ppermute | solution.py:288
  43.7 0.2 select_add_fusion
  43.9 3.5 %collective-permute-done.4.below_ref = f32[12,64,128]{2,1,0:T(8,128)S(1)} collective-permute-done((f32[12,64,128]{2,1,0:T(8,128)S(1)}, f32[12,64,128]{2,1,0:T(8,128)S(1)}, u32[]{:S(2)}, u32[]{:S(2)}) %collective-permute-start.4) | collective-permute-done | bytes 393248 | tf_op jit(solution)/shard_map/ppermute | solution.py:288
  47.4 4.6 %collective-permute-done.5.above_ref = f32[12,64,128]{2,1,0:T(8,128)S(1)} collective-permute-done((f32[12,64,128]{2,1,0:T(8,128)S(1)}, f32[12,64,128]{2,1,0:T(8,128)S(1)}, u32[]{:S(2)}, u32[]{:S(2)}) %collective-permute-start.5) | collective-permute-done | bytes 393248 | tf_op jit(solution)/shard_map/ppermute | solution.py:288
  52.2 0.2 select_add_fusion.1
  52.4 0.1 reshape.176.taps_ref
  52.5 1.0 %collective-permute-done.6.low_rows_ref.high_rows_ref = f32[40,8,128]{2,1,0:T(8,128)S(1)} collective-permute-done((f32[40,8,128]{2,1,0:T(8,128)S(1)}, f32[40,8,128]{2,1,0:T(8,128)S(1)}, u32[]{:S(2)}, u32[]{:S(2)}) %collective-permute-start.6) | collective-permute-done | bytes 163872 | tf_op jit(solution)/shard_map/ppermute | solution.py:297
  53.5 6.2 %update.2.rest_0_ = f32[8,64,128]{2,1,0:T(8,128)S(1)} custom-call(f32[2]{0:T(128)S(1)} %add_convert_fusion.flag_ref, f32[54]{0:T(128)S(1)} %reshape.176.taps_ref, f32[2,2,128,128]{3,2,1,0:T(8,128)S(1)} %pad_maximum_fusion.3.band_ref, f32[2,8,64,128]{3,2,1,0:T(8,128)S(1)} %bitcast.23, f32[12,64,128]{2,1,0:T(8,128)S(1)} %collective-permute-done.4.below_ref, ...), custom_call_target="tpu_custom_call" | custom-call | tf_op jit(solution)/shard_map/update/pallas_call | solution.py:273
  59.7 1.3 %collective-permute-start.8 = (f32[8,64,128]{2,1,0:T(8,128)S(1)}, f32[8,64,128]{2,1,0:T(8,128)S(1)}, u32[]{:S(2)}, u32[]{:S(2)}) collective-permute-start(f32[8,64,128]{2,1,0:T(8,128)S(1)} %update.2.rest_0_), channel_id=1, source_target_pairs={{4,0},{8,4},{12,8},{5,1},{9,5},{13,9},{6,2},{10,6},{14,10},{7,3},{... | collective-permute-start | bytes 786440 | tf_op jit(solution)/shard_map/ppermute | solution.py:288
  61.0 4.6 %collective-permute-start.7 = (f32[8,64,128]{2,1,0:T(8,128)S(1)}, f32[8,64,128]{2,1,0:T(8,128)S(1)}, u32[]{:S(2)}, u32[]{:S(2)}) collective-permute-start(f32[8,64,128]{2,1,0:T(8,128)S(1)} %update.2.rest_0_), channel_id=1, source_target_pairs={{0,4},{4,8},{8,12},{1,5},{5,9},{9,13},{2,6},{6,10},{10,14},{3,7},{... | collective-permute-start | bytes 786440 | tf_op jit(solution)/shard_map/ppermute | solution.py:288
  65.6 4.4 %collective-permute-done.8.rest_2_ = f32[8,64,128]{2,1,0:T(8,128)S(1)} collective-permute-done((f32[8,64,128]{2,1,0:T(8,128)S(1)}, f32[8,64,128]{2,1,0:T(8,128)S(1)}, u32[]{:S(2)}, u32[]{:S(2)}) %collective-permute-start.8) | collective-permute-done | bytes 262176 | tf_op jit(solution)/shard_map/ppermute | solution.py:288
  70.0 1.2 %collective-permute-done.7.rest_1_ = f32[8,64,128]{2,1,0:T(8,128)S(1)} collective-permute-done((f32[8,64,128]{2,1,0:T(8,128)S(1)}, f32[8,64,128]{2,1,0:T(8,128)S(1)}, u32[]{:S(2)}, u32[]{:S(2)}) %collective-permute-start.7) | collective-permute-done | bytes 262176 | tf_op jit(solution)/shard_map/ppermute | solution.py:288
  71.2 1.3 %collective-permute-done.9.rest_3_.rest_4_ = f32[24,8,128]{2,1,0:T(8,128)S(1)} collective-permute-done((f32[24,8,128]{2,1,0:T(8,128)S(1)}, f32[24,8,128]{2,1,0:T(8,128)S(1)}, u32[]{:S(2)}, u32[]{:S(2)}) %collective-permute-start.9) | collective-permute-done | bytes 98336 | tf_op jit(solution)/shard_map/ppermute | solution.py:297
  72.5 6.8 %update.3 = f32[8,64,128]{2,1,0:T(8,128)} custom-call(f32[2]{0:T(128)S(1)} %add_convert_fusion.flag_ref, f32[54]{0:T(128)S(1)} %reshape.176.taps_ref, f32[2,2,128,128]{3,2,1,0:T(8,128)S(1)} %pad_maximum_fusion.3.band_ref, f32[2,8,64,128]{3,2,1,0:T(8,128)S(1)} %bitcast.24, f32[12,64,128]{2,1,0:T(8,128)S(1)} %collective-permute-done.4.below_ref, ...), custom_call_target="tpu_custom_call" | custom-call | tf_op jit(solution)/shard_map/update/pallas_call | solution.py:273
  (41 shorter events, 1.0 us)
Async XLA Ops:
  1.3 1.9 %copy-start = (f32[1,32,3,64,128]{4,3,2,1,0:T(8,128)S(1)}, f32[1,32,3,64,128]{4,3,2,1,0:T(8,128)}, u32[]{:S(2)}) copy-start(f32[1,32,3,64,128]{4,3,2,1,0:T(8,128)} %param.6) | copy-start | bytes 9437188
  3.2 0.7 copy-start.1
  3.8 0.7 copy-start.3
  4.5 0.7 copy-start.4
  6.5 14.1 %copy-start.5 = (f32[1,3,9]{2,0,1:T(1,128)S(1)}, f32[1,3,9]{2,0,1:T(1,128)}, u32[]{:S(2)}) copy-start(f32[1,3,9]{2,0,1:T(1,128)} %param.11) | copy-start | bytes 328
  6.6 9.5 %collective-permute-start.1 = (f32[520,128]{1,0:T(8,128)S(1)}, f32[520,128]{1,0:T(8,128)S(1)}, u32[]{:S(2)}, u32[]{:S(2)}) collective-permute-start(f32[520,128]{1,0:T(8,128)S(1)} %slice.93), channel_id=1, source_target_pairs={{0,4},{4,0},{8,12},{12,8},{1,5},{5,1},{9,13},{13,9},{2,6},{6,2},{1... | collective-permute-start | bytes 798728 | tf_op jit(solution)/shard_map/ppermute | solution.py:98
  9.8 21.9 %copy-start.2 = (f32[1,3]{1,0:T(1,128)S(1)}, f32[1,3]{1,0:T(1,128)}, u32[]{:S(2)}) copy-start(f32[1,3]{1,0:T(1,128)} %param.10) | copy-start | bytes 40
  16.1 13.1 %collective-permute-start = (f32[520,128]{1,0:T(8,128)S(1)}, f32[520,128]{1,0:T(8,128)S(1)}, u32[]{:S(2)}, u32[]{:S(2)}) collective-permute-start(f32[520,128]{1,0:T(8,128)S(1)} %get-tuple-element.20), channel_id=1, source_target_pairs={{0,4},{4,0},{8,12},{12,8},{1,5},{5,1},{9,13},{13,9},{2,6},{6,2},{1... | collective-permute-start | bytes 798728 | tf_op jit(solution)/shard_map/ppermute | solution.py:99
  18.0 13.7 %collective-permute-start.2 = (f32[520,128]{1,0:T(8,128)S(1)}, f32[520,128]{1,0:T(8,128)S(1)}, u32[]{:S(2)}, u32[]{:S(2)}) collective-permute-start(f32[520,128]{1,0:T(8,128)S(1)} %get-tuple-element.19), channel_id=1, source_target_pairs={{0,8},{4,12},{8,0},{12,4},{1,9},{5,13},{9,1},{13,5},{2,10},{6,14},... | collective-permute-start | bytes 798728 | tf_op jit(solution)/shard_map/ppermute | solution.py:104
  33.1 6.4 %collective-permute-start.3 = (f32[520,128]{1,0:T(8,128)S(1)}, f32[520,128]{1,0:T(8,128)S(1)}, u32[]{:S(2)}, u32[]{:S(2)}) collective-permute-start(f32[520,128]{1,0:T(8,128)S(1)} %get-tuple-element.4), channel_id=1, source_target_pairs={{0,2},{2,0},{1,3},{3,1},{4,6},{6,4},{5,7},{7,5},{8,10},{10,8},{9,1... | collective-permute-start | bytes 798728 | tf_op jit(solution)/shard_map/ppermute | solution.py:307
  39.8 7.6 %collective-permute-start.4 = (f32[12,64,128]{2,1,0:T(8,128)S(1)}, f32[12,64,128]{2,1,0:T(8,128)S(1)}, u32[]{:S(2)}, u32[]{:S(2)}) collective-permute-start(f32[12,64,128]{2,1,0:T(8,128)S(1)} %pad_maximum_fusion.1), channel_id=1, source_target_pairs={{0,4},{4,8},{8,12},{1,5},{5,9},{9,13},{2,6},{6,10},{10,14},{3,7},{... | collective-permute-start | bytes 1179656 | tf_op jit(solution)/shard_map/ppermute | solution.py:288
  42.4 9.7 %collective-permute-start.5 = (f32[12,64,128]{2,1,0:T(8,128)S(1)}, f32[12,64,128]{2,1,0:T(8,128)S(1)}, u32[]{:S(2)}, u32[]{:S(2)}) collective-permute-start(f32[12,64,128]{2,1,0:T(8,128)S(1)} %pad_maximum_fusion.2), channel_id=1, source_target_pairs={{4,0},{8,4},{12,8},{5,1},{9,5},{13,9},{6,2},{10,6},{14,10},{7,3},{... | collective-permute-start | bytes 1179656 | tf_op jit(solution)/shard_map/ppermute | solution.py:288
  52.1 1.5 %collective-permute-start.6 = (f32[40,8,128]{2,1,0:T(8,128)S(1)}, f32[40,8,128]{2,1,0:T(8,128)S(1)}, u32[]{:S(2)}, u32[]{:S(2)}) collective-permute-start(f32[40,8,128]{2,1,0:T(8,128)S(1)} %pad_maximum_fusion.4), channel_id=1, source_target_pairs={{0,1},{1,0},{2,3},{3,2},{4,5},{5,4},{6,7},{7,6},{8,9},{9,8},{10,11... | collective-permute-start | bytes 491528 | tf_op jit(solution)/shard_map/ppermute | solution.py:297
  59.7 10.2 %collective-permute-start.8 = (f32[8,64,128]{2,1,0:T(8,128)S(1)}, f32[8,64,128]{2,1,0:T(8,128)S(1)}, u32[]{:S(2)}, u32[]{:S(2)}) collective-permute-start(f32[8,64,128]{2,1,0:T(8,128)S(1)} %update.2.rest_0_), channel_id=1, source_target_pairs={{4,0},{8,4},{12,8},{5,1},{9,5},{13,9},{6,2},{10,6},{14,10},{7,3},{... | collective-permute-start | bytes 786440 | tf_op jit(solution)/shard_map/ppermute | solution.py:288
  61.0 10.1 %collective-permute-start.7 = (f32[8,64,128]{2,1,0:T(8,128)S(1)}, f32[8,64,128]{2,1,0:T(8,128)S(1)}, u32[]{:S(2)}, u32[]{:S(2)}) collective-permute-start(f32[8,64,128]{2,1,0:T(8,128)S(1)} %update.2.rest_0_), channel_id=1, source_target_pairs={{0,4},{4,8},{8,12},{1,5},{5,9},{9,13},{2,6},{6,10},{10,14},{3,7},{... | collective-permute-start | bytes 786440 | tf_op jit(solution)/shard_map/ppermute | solution.py:288
  71.2 1.4 %collective-permute-start.9 = (f32[24,8,128]{2,1,0:T(8,128)S(1)}, f32[24,8,128]{2,1,0:T(8,128)S(1)}, u32[]{:S(2)}, u32[]{:S(2)}) collective-permute-start(f32[24,8,128]{2,1,0:T(8,128)S(1)} %pad_maximum_fusion.5), channel_id=1, source_target_pairs={{0,1},{1,0},{2,3},{3,2},{4,5},{5,4},{6,7},{7,6},{8,9},{9,8},{10,11... | collective-permute-start | bytes 294920 | tf_op jit(solution)/shard_map/ppermute | solution.py:297

commit v2 on v1

v2 whole, which is shorter than its diff:
```python
import functools

import jax
import jax.numpy as jnp
from jax import lax
from jax.experimental import pallas as pl
from jax.experimental.pallas import tpu as pltpu
from jax.sharding import PartitionSpec as P

CZ = 8
ITERS = 2


DATA_FLOOR = 0.25
PRECISE = lax.Precision.HIGHEST
F32 = jnp.float32
SUB = 8
VMEM = pl.BlockSpec(memory_space=pltpu.VMEM)
HBM = pl.BlockSpec(memory_space=pltpu.HBM)
VMEM_BYTES = 48 * 1024 * 1024
DEPOSIT_VMEM_BYTES = 60 * 1024 * 1024


def bit_count(count):
    bits = count.bit_length() - 1
    assert count == 1 << bits
    return bits


def reversed_bits(value, bits):
    result = 0
    for bit in range(bits):
        result = result | (((value >> bit) & 1) << (bits - 1 - bit))
    return result


def deposit_kernel(
    target_hbm, first_hbm, level_hbm, fraction_hbm, camera_hbm, out_ref, target, first, level, fraction, camera,
    small_sems, camera_sems, *, bits, section, chunk
):
    blocks, planes, rows, cols = camera.shape
    sources = ((target_hbm, target), (first_hbm, first), (level_hbm, level), (fraction_hbm, fraction))
    smalls = [pltpu.make_async_copy(*pair, small_sems.at[i]) for i, pair in enumerate(sources)]
    parts = []
    for i in range(blocks // chunk):
        here = pl.ds(i * chunk, chunk)
        parts.append(pltpu.make_async_copy(camera_hbm.at[here], camera.at[here], camera_sems.at[i]))
    for copy in smalls + parts:
        copy.start()
    out_ref[...] = jnp.zeros(out_ref.shape, F32)
    for copy in smalls:
        copy.wait()
    place = lax.axis_index("gz").astype(jnp.int32)
    base_level = level[0].astype(F32)
    upper_share = fraction[0]
    lower_share = 1.0 - upper_share
    plane_at = lax.broadcasted_iota(jnp.int32, (CZ, cols), 0)

    def one(block, carry):
        slab = reversed_bits(target[block] ^ place, bits)
        at = first[block]
        start = pl.multiple_of(slab * section, SUB)
        base = pl.multiple_of(start + at * rows, SUB)
        lower = camera[block, 0] - base_level
        for plane in range(planes - 1):
            upper = camera[block, plane + 1] - base_level
            here = pl.ds(pl.multiple_of(base + plane * rows, SUB), rows)
            out_ref[here, :] += lower_share * lower + upper_share * upper
            lower = upper
        counts = pl.ds(pl.multiple_of(start + CZ * rows, SUB), CZ)
        out_ref[counts, :] += ((plane_at >= at) & (plane_at < at + planes - 1)).astype(F32)
        return carry

    for i, copy in enumerate(parts):
        copy.wait()
        lax.fori_loop(i * chunk, (i + 1) * chunk, one, 0, unroll=True)


def deposit(camera, target, first, level, fraction, slabs):
    blocks, planes, rows, cols = camera.shape
    section = CZ * rows + CZ
    chunk = SUB if blocks % SUB == 0 else blocks
    return pl.pallas_call(
        functools.partial(deposit_kernel, bits=bit_count(slabs), section=section, chunk=chunk),
        in_specs=[HBM] * 5,
        out_specs=VMEM,
        out_shape=jax.ShapeDtypeStruct((slabs * section, cols), F32),
        scratch_shapes=[
            pltpu.SMEM(target.shape, jnp.int32),
            pltpu.SMEM(first.shape, jnp.int32),
            pltpu.SMEM(level.shape, jnp.int32),
            pltpu.SMEM(fraction.shape, F32),
            pltpu.VMEM(camera.shape, F32),
            pltpu.SemaphoreType.DMA((4,)),
            pltpu.SemaphoreType.DMA((blocks // chunk,)),
        ],
        compiler_params=pltpu.CompilerParams(vmem_limit_bytes=DEPOSIT_VMEM_BYTES),
        name="deposit",
    )(target, first, level, fraction, camera)


def butterfly(sums, slabs, section):
    bits = bit_count(slabs)
    own = sums
    count = slabs
    late = None
    for bit in range(bits):
        half = count // 2
        pairs = [(i, i ^ (1 << bit)) for i in range(slabs)]
        keep, send = own[: half * section], own[half * section :]
        if late is not None:
            send = send + late[1]
            keep = keep + late[0]
        if half > 1:
            cut = half // 2 * section
            onward = lax.ppermute(send[cut:], "gz", pairs)
            stays = lax.ppermute(send[:cut], "gz", pairs)
            late = (stays, onward)
            next_half = half // 2
            own = keep
        else:
            arrived = lax.ppermute(send, "gz", pairs)
            return keep, arrived
        count = half
    return own, jnp.zeros_like(own)


def join_kernel(small_ref, kept_ref, arrived_ref, message_ref, *, rows):
    cols = kept_ref.shape[1]
    total = kept_ref[...] + arrived_ref[...]
    planes = total[: CZ * rows].reshape(CZ, rows, cols)
    counts = total[CZ * rows :]
    fy, fx = small_ref[3:4], small_ref[4:5]
    row_at = lax.broadcasted_iota(jnp.int32, (rows, cols), 0)
    col_at = lax.broadcasted_iota(jnp.int32, (rows, cols), 1)
    for plane in range(CZ):
        part = planes[plane]
        follow = jnp.where(row_at == rows - 1, part, pltpu.roll(part, rows - 1, 0))
        part = (1.0 - fy) * part + fy * follow
        follow = jnp.where(col_at == cols - 1, part, pltpu.roll(part, cols - 1, 1))
        part = (1.0 - fx) * part + fx * follow
        part = jnp.maximum(part / (counts[plane : plane + 1] + 1.0), DATA_FLOOR)
        message_ref[plane * rows : (plane + 1) * rows] = part
    message_ref[CZ * rows :] = small_ref[...]


def join(small, kept, arrived, rows):
    return pl.pallas_call(
        functools.partial(join_kernel, rows=rows),
        in_specs=[VMEM] * 3,
        out_specs=VMEM,
        out_shape=jax.ShapeDtypeStruct(kept.shape, F32),
        compiler_params=pltpu.CompilerParams(vmem_limit_bytes=VMEM_BYTES),
        name="join",
    )(small, kept, arrived)


def taps_sum(values, weights):
    result = weights[0] * values[0]
    for offset in range(1, len(weights)):
        result = result + weights[offset] * values[offset]
    return result


def band_dot(values, high_part, low_part):
    cols = values.shape[1]
    top = values.astype(jnp.bfloat16)
    rest = (values - top.astype(F32)).astype(jnp.bfloat16)
    both = jnp.dot(top, jnp.concatenate([high_part, low_part], axis=1), preferred_element_type=F32)
    return both[:, :cols] + both[:, cols:] + jnp.dot(rest, high_part, preferred_element_type=F32)


def update_kernel(
    weight_ref, high_band_ref, low_band_ref, own_ref, below_ref, above_ref, low_rows_ref, high_rows_ref, *rest,
    views, margin, first
):
    if first:
        message_ref, out_ref, copied_hbm, *scratch, copied_sem = rest
        copied = pltpu.make_async_copy(message_ref.at[pl.ds(0, copied_hbm.shape[0])], copied_hbm, copied_sem)
        copied.start()
    else:
        est_ref, est_below_ref, est_above_ref, est_low_ref, est_high_ref, out_ref, *scratch = rest
    estimate, joined, first_pass, ratio, back_first = scratch
    _, planes, rows, cols = own_ref.shape
    taps = 2 * margin + 1
    wide = 2 * margin
    flag_low, flag_high = weight_ref[views * 3 * taps], weight_ref[views * 3 * taps + 1]
    low, body, high = slice(0, wide), slice(wide, wide + rows), slice(wide + rows, 2 * wide + rows)

    above_at = below_ref.shape[0]
    own_at = 2 * above_at
    for view in range(views):
        pieces = (
            (0, margin, below_ref, view * margin, view * margin),
            (margin, planes, own_ref.at[view], 0, own_at + view * planes),
            (margin + planes, margin, above_ref, view * margin, above_at + view * margin),
        )
        for to, length, source, at, edge_at in pieces:
            joined[view, to : to + length, body] = source[at : at + length]
            joined[view, to : to + length, low] = low_rows_ref[edge_at : edge_at + length] * flag_low
            joined[view, to : to + length, high] = high_rows_ref[edge_at : edge_at + length] * flag_high
    if first:
        inner = joined[0]
        for view in range(1, views):
            inner = inner + joined[view]
        estimate[margin : planes + 3 * margin] = inner / views
        at = views * margin
        for to, source, edge_at in ((0, below_ref, at), (planes + 3 * margin, above_ref, above_at + at)):
            estimate[to : to + margin, body] = source[at : at + margin]
            estimate[to : to + margin, low] = low_rows_ref[edge_at : edge_at + margin] * flag_low
            estimate[to : to + margin, high] = high_rows_ref[edge_at : edge_at + margin] * flag_high
    else:
        for index, source in enumerate((est_below_ref, est_ref, est_above_ref)):
            here = slice(index * planes, (index + 1) * planes)
            estimate[here, body] = source[...]
            estimate[here, low] = est_low_ref[here] * flag_low
            estimate[here, high] = est_high_ref[here] * flag_high

    mid_planes, mid_rows = planes + 2 * margin, rows + 2 * margin
    weights = [
        [[weight_ref[(view * 3 + dim) * taps + tap] for tap in range(taps)] for dim in range(3)] for view in range(views)
    ]

    def along_z(tile, carry):
        here = pl.ds(pl.multiple_of(tile * SUB, SUB), SUB)
        values = [estimate[plane, here, :] for plane in range(planes + 4 * margin)]
        for view in range(views):
            for plane in range(mid_planes):
                first_pass[view, plane, here, :] = taps_sum(values[plane : plane + taps], weights[view][0])
        return carry

    lax.fori_loop(0, (rows + 4 * margin) // SUB, along_z, 0)

    for view in range(views):
        values = [first_pass[view, :, tap : tap + mid_rows, :].reshape(-1, SUB, cols) for tap in range(taps)]
        blurred = band_dot(
            taps_sum(values, weights[view][1]).reshape(-1, cols), high_band_ref[view, 0], low_band_ref[view, 0]
        )
        ratio[view] = joined[view, :, margin : margin + mid_rows, :] / blurred.reshape(mid_planes, mid_rows, cols)

    def back_z(tile, carry):
        here = pl.ds(pl.multiple_of(tile * SUB, SUB), SUB)
        for view in range(views):
            values = [ratio[view, plane, here, :] for plane in range(mid_planes)]
            for plane in range(planes):
                back_first[view, plane, here, :] = taps_sum(values[plane : plane + taps], weights[view][0][::-1])
        return carry

    lax.fori_loop(0, mid_rows // SUB, back_z, 0)

    logs = None
    for view in range(views):
        values = [back_first[view, :, tap : tap + rows, :].reshape(-1, SUB, cols) for tap in range(taps)]
        correction = band_dot(
            taps_sum(values, weights[view][1][::-1]).reshape(-1, cols), high_band_ref[view, 1], low_band_ref[view, 1]
        )
        one = jnp.log(correction)
        logs = one if logs is None else logs + one
    out_ref[...] = estimate[wide : wide + planes, body] * jnp.exp(logs / views).reshape(planes, rows, cols)
    if first:
        copied.wait()


def update(weights, bands, own, below, above, low_rows, high_rows, message, later, margin):
    views, planes, rows, cols = own.shape
    first = not later
    arrays = [weights, *bands, own, below, above, low_rows, high_rows] + ([message] if first else list(later))
    mid_planes, mid_rows = planes + 2 * margin, rows + 2 * margin
    scratch = [
        (planes + 4 * margin, rows + 4 * margin),
        (views, mid_planes, rows + 4 * margin),
        (views, mid_planes, rows + 4 * margin),
        (views, mid_planes, mid_rows),
        (views, planes, mid_rows),
    ]
    out_shape = jax.ShapeDtypeStruct((planes, rows, cols), F32)
    copy_shape = jax.ShapeDtypeStruct((planes * rows, cols), F32)
    return pl.pallas_call(
        functools.partial(update_kernel, views=views, margin=margin, first=first),
        in_specs=[VMEM] * len(arrays),
        out_specs=[VMEM, HBM] if first else VMEM,
        out_shape=[out_shape, copy_shape] if first else out_shape,
        scratch_shapes=[pltpu.VMEM(shape + (cols,), F32) for shape in scratch] + [pltpu.SemaphoreType.DMA] * first,
        compiler_params=pltpu.CompilerParams(vmem_limit_bytes=VMEM_BYTES),
        name="update",
    )(*arrays)


def from_beside(axis, upward, downward):
    count = lax.axis_size(axis)
    up = [(i, i + 1) for i in range(count - 1)]
    down = [(target, source) for source, target in up]
    return lax.ppermute(upward, axis, up), lax.ppermute(downward, axis, down)


def edge_rows(pieces, width):
    count = lax.axis_size("gy")
    rows = pieces[0].shape[-2]
    if count == 2:
        at = jnp.where(lax.axis_index("gy") == 0, rows - width, 0)
        parts = [lax.dynamic_slice_in_dim(piece, at, width, axis=1) for piece in pieces]
        arrived = lax.ppermute(jnp.concatenate(parts), "gy", [(0, 1), (1, 0)])
        return arrived, arrived
    upward = jnp.concatenate([piece[:, rows - width :] for piece in pieces])
    downward = jnp.concatenate([piece[:, :width] for piece in pieces])
    return from_beside("gy", upward, downward)


def from_views(message):
    count = lax.axis_size("view")
    if count == 2:
        return jnp.stack([message, lax.ppermute(message, "view", [(0, 1), (1, 0)])])
    return lax.all_gather(message, "view")


def on_device(camera, background, destination, offsets, shift_frac, psf_taps):
    slabs = lax.axis_size("gz")
    views = lax.axis_size("view")
    _, blocks, _, rows, cols = camera.shape
    taps = psf_taps.shape[-1]
    margin = taps // 2
    section = CZ * rows + CZ
    fraction = shift_frac[0]
    sums = deposit(
        camera[0], destination.reshape(blocks), offsets.reshape(blocks), background.reshape(1), fraction, slabs
    )
    kept, arrived = butterfly(sums, slabs, section)
    small = jnp.concatenate(
        [
            jnp.pad(psf_taps[0], ((0, 0), (0, cols - taps))),
            jnp.broadcast_to(fraction[1:, None], (2, cols)),
            jnp.zeros((CZ - 5, cols), F32),
        ]
    )
    message = join(small, kept, arrived, rows)

    messages = from_views(message)
    all_joined = messages[:, : CZ * rows].reshape(views, CZ, rows, cols)
    estimate = jnp.sum(all_joined, axis=0) / views
    upward = jnp.concatenate([all_joined[:, CZ - margin :].reshape(views * margin, rows, cols), estimate[: CZ - margin]])
    downward = jnp.concatenate([all_joined[:, :margin].reshape(views * margin, rows, cols), estimate[margin:]])
    below, above = from_beside("gz", upward, downward)
    wide = 2 * margin
    low_rows, high_rows = edge_rows([below, above, all_joined.reshape(views * CZ, rows, cols)], wide)

    all_taps = messages[:, CZ * rows : CZ * rows + 3, :taps]
    kernels = all_taps / jnp.sum(all_taps, axis=-1, keepdims=True)
    places = jnp.arange(cols, dtype=jnp.int32)
    shift = places[:, None] - places[None, :] + margin
    band = sum(jnp.where(shift == tap, kernels[:, 2, tap, None, None], 0.0) for tap in range(taps))
    band = jnp.stack([band, jnp.swapaxes(band, 1, 2)], axis=1)
    high_part = lax.reduce_precision(band, 8, 7)
    bands = (high_part.astype(jnp.bfloat16), (band - high_part).astype(jnp.bfloat16))
    row_band = lax.axis_index("gy")
    flags = jnp.stack([row_band > 0, row_band < lax.axis_size("gy") - 1]).astype(F32)
    weights = jnp.broadcast_to(jnp.concatenate([kernels.reshape(-1), flags])[:, None, None], (views * 3 * taps + 2, SUB, cols))

    later = ()
    for iteration in range(ITERS):
        if iteration:
            est_below, est_above = from_beside("gz", estimate, estimate)
            later = (estimate, est_below, est_above) + edge_rows([est_below, estimate, est_above], wide)
        result = update(weights, bands, all_joined, below, above, low_rows, high_rows, message, later, margin)
        estimate = result if later else result[0]
        joined = joined if later else result[1]
    return (estimate, joined.reshape(1, CZ, rows, cols))


def solution(mesh):
    return jax.shard_map(
        on_device,
        mesh=mesh,
        in_specs=(
            P("view", ("groups", "gz"), None, "gy", None),
            P("view", "gy", ("groups", "gz")),
            P("view", "gy", ("groups", "gz"), None),
            P("view", "gy", ("groups", "gz")),
            P("view", None),
            P("view", None, None),
        ),
        out_specs=(P(("groups", "gz"), "gy", None), P("view", ("groups", "gz"), "gy", None)),
        check_vma=False,
    )
```

time: 79.6 us -> 72 us (0.905)
  Pallas kernels: 15.8 us -> 9.77 us
  local copies, waits for them, and re-layouts: 4.27 us -> 1.71 us
  other arithmetic: 1.26 us -> 3.41 us
  waiting for transfers between devices: 37.9 us -> 36.6 us
    pallas_call x2, Pallas kernels: 13 us -> 6.59 us  [update(): pl.pallas_call(functools.partial(update_kernel, views=views, margin=margi...]
    unnamed x13 -> x5, local copies, waits for them, and re-layouts: 3.86 us -> 0.01 us
    pallas_call x1, Pallas kernels: 1.39 us -> 3.03 us  [deposit(): pl.pallas_call(functools.partial(deposit_kernel, bits=bit_count(slabs), s...]
    pallas_call x1, Pallas kernels: 1.39 us -> 0.15 us  [join(): pl.pallas_call(functools.partial(join_kernel, rows=rows), in_specs=[VMEM]...]
    add x1, other arithmetic: 0.07 us -> 1.09 us  [butterfly(): send = send + late[1]]
    ppermute x1, waiting for transfers between devices: 2.41 us -> 1.45 us  [butterfly(): arrived = lax.ppermute(send, 'gz', pairs)]
    slice x1, local copies, waits for them, and re-layouts: 0.02 us -> 0.97 us  [butterfly(): onward = lax.ppermute(send[cut:], 'gz', pairs)]
    add x1, other arithmetic: 0.04 us -> 0.98 us  [butterfly(): keep = keep + late[0]]
  transfers between devices with their start and end apart: 10 -> 10, of which waited for: 10 -> 10; matrix products, arithmetic and copies ran while one was open for 2% -> 3% of each run, Pallas kernels for 0% -> 0%
where the time goes in v2:
time: 72 us; the launch traced here: 71.7 us
  waiting for transfers between devices  36.6 us (51%)
  starting transfers between devices  18.7 us (26%)
  Pallas kernels  9.77 us (14%)
  other arithmetic  3.41 us (5%)
  local copies, waits for them, and re-layouts  1.71 us (2%)
  between operations  1.54 us (2%)
    ppermute x4, waiting for transfers between devices, from_beside(): return (lax.ppermute(upward, axis, up), lax.ppermute(downward, axis, down))  13.3 us
    ppermute x4, starting transfers between devices, from_beside(): return (lax.ppermute(upward, axis, up), lax.ppermute(downward, axis, down))  9.41 us
    ppermute x1, waiting for transfers between devices, butterfly(): stays = lax.ppermute(send[:cut], 'gz', pairs)  8.57 us
    pallas_call x2, Pallas kernels, update(): pl.pallas_call(functools.partial(update_kernel, views=views, margin=margi...  6.59 us
    ppermute x1, waiting for transfers between devices, butterfly(): onward = lax.ppermute(send[cut:], 'gz', pairs)  5.91 us
    ppermute x1, waiting for transfers between devices, from_views(): return jnp.stack([message, lax.ppermute(message, 'view', [(0, 1), (1, 0)])])  4.78 us
    ppermute x1, starting transfers between devices, butterfly(): onward = lax.ppermute(send[cut:], 'gz', pairs)  3.09 us
    pallas_call x1, Pallas kernels, deposit(): pl.pallas_call(functools.partial(deposit_kernel, bits=bit_count(slabs), s...  3.03 us
  transfers between devices with their start and end apart: 10, of which 10 were waited for; matrix products, arithmetic and copies ran while one was open for 3% of the time, Pallas kernels for 0%

profile of v2, /device:TPU:0, one launch (start us, length us, event | category | flops | bytes accessed | tf_op | source)
XLA Modules:
  0.0 71.7 jit_solution(6908144008862508764)
XLA Ops:
  1.3 3.0 %deposit.1 = f32[2080,128]{1,0:T(8,128)} custom-call(s32[32]{0:T(128)} %bitcast.36, s32[32]{0:T(128)} %bitcast.37, s32[1]{0:T(128)} %bitcast.21.level_hbm, f32[3]{0:T(128)} %bitcast.38, f32[32,3,64,128]{3,2,1,0:T(8,128)} %bitcast.28), custom_call_target="tpu_custom_call" | custom-call | tf_op jit(solution)/shard_map/deposit/pallas_call | solution.py:83
  4.3 1.0 %slice.98 = f32[520,128]{1,0:T(8,128)S(1)} slice(f32[2080,128]{1,0:T(8,128)} %deposit.1), slice={[1560:2080], [0:128]} | slice | bytes 532480 | tf_op jit(solution)/shard_map/slice | solution.py:116
  5.3 3.1 %collective-permute-start.1 = (f32[520,128]{1,0:T(8,128)S(1)}, f32[520,128]{1,0:T(8,128)S(1)}, u32[]{:S(2)}, u32[]{:S(2)}) collective-permute-start(f32[520,128]{1,0:T(8,128)S(1)} %slice.98), channel_id=1, source_target_pairs={{0,4},{4,0},{8,12},{12,8},{1,5},{5,1},{9,13},{13,9},{2,6},{6,2},{1... | collective-permute-start | bytes 798728 | tf_op jit(solution)/shard_map/ppermute | solution.py:116
  8.7 0.1 pad.25.clone
  8.9 5.9 %collective-permute-done.1 = f32[520,128]{1,0:T(8,128)S(1)} collective-permute-done((f32[520,128]{1,0:T(8,128)S(1)}, f32[520,128]{1,0:T(8,128)S(1)}, u32[]{:S(2)}, u32[]{:S(2)}) %collective-permute-start.1) | collective-permute-done | bytes 266272 | tf_op jit(solution)/shard_map/ppermute | solution.py:116
  14.8 1.1 %slice_add_fusion = (f32[520,128]{1,0:T(8,128)S(1)}, f32[520,128]{1,0:T(8,128)S(1)}) fusion(f32[520,128]{1,0:T(8,128)S(1)} %collective-permute-done.1, f32[2080,128]{1,0:T(8,128)} %deposit.1), kind=kLoop, calls=%fused_computation.5 | loop fusion | flops 66560 | bytes 1331200 | tf_op jit(solution)/shard_map/add | solution.py:112
  15.9 1.8 %collective-permute-start = (f32[520,128]{1,0:T(8,128)S(1)}, f32[520,128]{1,0:T(8,128)S(1)}, u32[]{:S(2)}, u32[]{:S(2)}) collective-permute-start(f32[520,128]{1,0:T(8,128)S(1)} %get-tuple-element.20), channel_id=1, source_target_pairs={{0,4},{4,0},{8,12},{12,8},{1,5},{5,1},{9,13},{13,9},{2,6},{6,2},{1... | collective-permute-start | bytes 798728 | tf_op jit(solution)/shard_map/ppermute | solution.py:117
  17.8 2.7 %collective-permute-start.2 = (f32[520,128]{1,0:T(8,128)S(1)}, f32[520,128]{1,0:T(8,128)S(1)}, u32[]{:S(2)}, u32[]{:S(2)}) collective-permute-start(f32[520,128]{1,0:T(8,128)S(1)} %get-tuple-element.19), channel_id=1, source_target_pairs={{0,8},{4,12},{8,0},{12,4},{1,9},{5,13},{9,1},{13,5},{2,10},{6,14},... | collective-permute-start | bytes 798728 | tf_op jit(solution)/shard_map/ppermute | solution.py:122
  20.4 8.6 %collective-permute-done = f32[520,128]{1,0:T(8,128)S(1)} collective-permute-done((f32[520,128]{1,0:T(8,128)S(1)}, f32[520,128]{1,0:T(8,128)S(1)}, u32[]{:S(2)}, u32[]{:S(2)}) %collective-permute-start) | collective-permute-done | bytes 266272 | tf_op jit(solution)/shard_map/ppermute | solution.py:117
  29.0 1.0 %slice_add_fusion.1.kept_ref = f32[520,128]{1,0:T(8,128)S(1)} fusion(f32[520,128]{1,0:T(8,128)S(1)} %collective-permute-done, f32[2080,128]{1,0:T(8,128)} %deposit.1), kind=kLoop, calls=%fused_computation.6 | loop fusion | flops 66560 | bytes 798720 | tf_op jit(solution)/shard_map/add | solution.py:113
  30.0 1.5 %collective-permute-done.2.arrived_ref = f32[520,128]{1,0:T(8,128)S(1)} collective-permute-done((f32[520,128]{1,0:T(8,128)S(1)}, f32[520,128]{1,0:T(8,128)S(1)}, u32[]{:S(2)}, u32[]{:S(2)}) %collective-permute-start.2) | collective-permute-done | bytes 266272 | tf_op jit(solution)/shard_map/ppermute | solution.py:122
  31.4 0.1 join.1.rest_0_
  31.6 1.6 %collective-permute-start.3 = (f32[520,128]{1,0:T(8,128)S(1)}, f32[520,128]{1,0:T(8,128)S(1)}, u32[]{:S(2)}, u32[]{:S(2)}) collective-permute-start(f32[520,128]{1,0:T(8,128)S(1)} %join.1.rest_0_), channel_id=1, source_target_pairs={{0,2},{2,0},{1,3},{3,1},{4,6},{6,4},{5,7},{7,5},{8,10},{10,8},{9,1... | collective-permute-start | bytes 798728 | tf_op jit(solution)/shard_map/ppermute | solution.py:312
  33.3 4.8 %collective-permute-done.3 = f32[520,128]{1,0:T(8,128)S(1)} collective-permute-done((f32[520,128]{1,0:T(8,128)S(1)}, f32[520,128]{1,0:T(8,128)S(1)}, u32[]{:S(2)}, u32[]{:S(2)}) %collective-permute-start.3) | collective-permute-done | bytes 266272 | tf_op jit(solution)/shard_map/ppermute | solution.py:312
  38.1 0.1 fusion.21
  38.3 0.2 slice_reduce_fusion.8
  38.7 2.3 %collective-permute-start.4 = (f32[12,64,128]{2,1,0:T(8,128)S(1)}, f32[12,64,128]{2,1,0:T(8,128)S(1)}, u32[]{:S(2)}, u32[]{:S(2)}) collective-permute-start(f32[12,64,128]{2,1,0:T(8,128)S(1)} %pad_maximum_fusion.1), channel_id=1, source_target_pairs={{0,4},{4,8},{8,12},{1,5},{5,9},{9,13},{2,6},{6,10},{10,14},{3,7},{... | collective-permute-start | bytes 1179656 | tf_op jit(solution)/shard_map/ppermute | solution.py:293
  41.0 1.3 %collective-permute-start.5 = (f32[12,64,128]{2,1,0:T(8,128)S(1)}, f32[12,64,128]{2,1,0:T(8,128)S(1)}, u32[]{:S(2)}, u32[]{:S(2)}) collective-permute-start(f32[12,64,128]{2,1,0:T(8,128)S(1)} %pad_maximum_fusion.2), channel_id=1, source_target_pairs={{4,0},{8,4},{12,8},{5,1},{9,5},{13,9},{6,2},{10,6},{14,10},{7,3},{... | collective-permute-start | bytes 1179656 | tf_op jit(solution)/shard_map/ppermute | solution.py:293
  42.3 0.2 select_add_fusion
  42.5 0.1 reshape.179
  42.6 0.2 select_add_fusion.1
  42.8 3.4 %collective-permute-done.4.below_ref = f32[12,64,128]{2,1,0:T(8,128)S(1)} collective-permute-done((f32[12,64,128]{2,1,0:T(8,128)S(1)}, f32[12,64,128]{2,1,0:T(8,128)S(1)}, u32[]{:S(2)}, u32[]{:S(2)}) %collective-permute-start.4) | collective-permute-done | bytes 393248 | tf_op jit(solution)/shard_map/ppermute | solution.py:293
  46.3 4.4 %collective-permute-done.5.above_ref = f32[12,64,128]{2,1,0:T(8,128)S(1)} collective-permute-done((f32[12,64,128]{2,1,0:T(8,128)S(1)}, f32[12,64,128]{2,1,0:T(8,128)S(1)}, u32[]{:S(2)}, u32[]{:S(2)}) %collective-permute-start.5) | collective-permute-done | bytes 393248 | tf_op jit(solution)/shard_map/ppermute | solution.py:293
  50.9 1.3 %collective-permute-done.6.low_rows_ref.high_rows_ref = f32[40,8,128]{2,1,0:T(8,128)S(1)} collective-permute-done((f32[40,8,128]{2,1,0:T(8,128)S(1)}, f32[40,8,128]{2,1,0:T(8,128)S(1)}, u32[]{:S(2)}, u32[]{:S(2)}) %collective-permute-start.6) | collective-permute-done | bytes 163872 | tf_op jit(solution)/shard_map/ppermute | solution.py:302
  52.1 0.1 broadcast_in_dim.147.weight_ref
  52.2 3.0 %update.2 = (f32[8,64,128]{2,1,0:T(8,128)S(1)}, f32[512,128]{1,0:T(8,128)}) custom-call(f32[56,8,128]{2,1,0:T(8,128)S(1)} %broadcast_in_dim.147.weight_ref, bf16[2,2,128,128]{3,2,1,0:T(8,128)(2,1)S(1)} %get-tuple-element.26.high_band_ref, bf16[2,2,128,128]{3,2,1,0:T(8,128)(2,1)S(1)} %get-tuple-element.25.low_band_ref, f32[2,8,64,128]{3,2,1,0:T(8,128)S(1)} %bitcast.24, ...), custom_call_target="tpu_custom_call" | custom-call | tf_op jit(solution)/shard_map/update/pallas_call | solution.py:278
  55.2 1.3 %collective-permute-start.8 = (f32[8,64,128]{2,1,0:T(8,128)S(1)}, f32[8,64,128]{2,1,0:T(8,128)S(1)}, u32[]{:S(2)}, u32[]{:S(2)}) collective-permute-start(f32[8,64,128]{2,1,0:T(8,128)S(1)} %get-tuple-element.4.rest_0_), channel_id=1, source_target_pairs={{4,0},{8,4},{12,8},{5,1},{9,5},{13,9},{6,2},{10,6},{14,10},{7,3},{... | collective-permute-start | bytes 786440 | tf_op jit(solution)/shard_map/ppermute | solution.py:293
  56.5 4.6 %collective-permute-start.7 = (f32[8,64,128]{2,1,0:T(8,128)S(1)}, f32[8,64,128]{2,1,0:T(8,128)S(1)}, u32[]{:S(2)}, u32[]{:S(2)}) collective-permute-start(f32[8,64,128]{2,1,0:T(8,128)S(1)} %get-tuple-element.4.rest_0_), channel_id=1, source_target_pairs={{0,4},{4,8},{8,12},{1,5},{5,9},{9,13},{2,6},{6,10},{10,14},{3,7},{... | collective-permute-start | bytes 786440 | tf_op jit(solution)/shard_map/ppermute | solution.py:293
  61.1 4.4 %collective-permute-done.8.rest_2_ = f32[8,64,128]{2,1,0:T(8,128)S(1)} collective-permute-done((f32[8,64,128]{2,1,0:T(8,128)S(1)}, f32[8,64,128]{2,1,0:T(8,128)S(1)}, u32[]{:S(2)}, u32[]{:S(2)}) %collective-permute-start.8) | collective-permute-done | bytes 262176 | tf_op jit(solution)/shard_map/ppermute | solution.py:293
  65.5 1.2 %collective-permute-done.7.rest_1_ = f32[8,64,128]{2,1,0:T(8,128)S(1)} collective-permute-done((f32[8,64,128]{2,1,0:T(8,128)S(1)}, f32[8,64,128]{2,1,0:T(8,128)S(1)}, u32[]{:S(2)}, u32[]{:S(2)}) %collective-permute-start.7) | collective-permute-done | bytes 262176 | tf_op jit(solution)/shard_map/ppermute | solution.py:293
  66.8 1.3 %collective-permute-done.9.rest_3_.rest_4_ = f32[24,8,128]{2,1,0:T(8,128)S(1)} collective-permute-done((f32[24,8,128]{2,1,0:T(8,128)S(1)}, f32[24,8,128]{2,1,0:T(8,128)S(1)}, u32[]{:S(2)}, u32[]{:S(2)}) %collective-permute-start.9) | collective-permute-done | bytes 98336 | tf_op jit(solution)/shard_map/ppermute | solution.py:302
  68.1 3.6 %update.3 = f32[8,64,128]{2,1,0:T(8,128)} custom-call(f32[56,8,128]{2,1,0:T(8,128)S(1)} %broadcast_in_dim.147.weight_ref, bf16[2,2,128,128]{3,2,1,0:T(8,128)(2,1)S(1)} %get-tuple-element.26.high_band_ref, bf16[2,2,128,128]{3,2,1,0:T(8,128)(2,1)S(1)} %get-tuple-element.25.low_band_ref, f32[2,8,64,128]{3,2,1,0:T(8,128)S(1)} %bitcast.25, ...), custom_call_target="tpu_custom_call" | custom-call | tf_op jit(solution)/shard_map/update/pallas_call | solution.py:278
  (39 shorter events, 1.2 us)
Async XLA Ops:
  1.3 7.1 %copy-start.1 = (f32[1,3]{1,0:T(1,128)S(1)}, f32[1,3]{1,0:T(1,128)}, u32[]{:S(2)}) copy-start(f32[1,3]{1,0:T(1,128)} %param.10) | copy-start | bytes 40
  1.3 7.5 %copy-start = (f32[1,3,9]{2,0,1:T(1,128)S(1)}, f32[1,3,9]{2,0,1:T(1,128)}, u32[]{:S(2)}) copy-start(f32[1,3,9]{2,0,1:T(1,128)} %param.11) | copy-start | bytes 328
  5.3 9.5 %collective-permute-start.1 = (f32[520,128]{1,0:T(8,128)S(1)}, f32[520,128]{1,0:T(8,128)S(1)}, u32[]{:S(2)}, u32[]{:S(2)}) collective-permute-start(f32[520,128]{1,0:T(8,128)S(1)} %slice.98), channel_id=1, source_target_pairs={{0,4},{4,0},{8,12},{12,8},{1,5},{5,1},{9,13},{13,9},{2,6},{6,2},{1... | collective-permute-start | bytes 798728 | tf_op jit(solution)/shard_map/ppermute | solution.py:116
  15.9 13.1 %collective-permute-start = (f32[520,128]{1,0:T(8,128)S(1)}, f32[520,128]{1,0:T(8,128)S(1)}, u32[]{:S(2)}, u32[]{:S(2)}) collective-permute-start(f32[520,128]{1,0:T(8,128)S(1)} %get-tuple-element.20), channel_id=1, source_target_pairs={{0,4},{4,0},{8,12},{12,8},{1,5},{5,1},{9,13},{13,9},{2,6},{6,2},{1... | collective-permute-start | bytes 798728 | tf_op jit(solution)/shard_map/ppermute | solution.py:117
  17.8 13.7 %collective-permute-start.2 = (f32[520,128]{1,0:T(8,128)S(1)}, f32[520,128]{1,0:T(8,128)S(1)}, u32[]{:S(2)}, u32[]{:S(2)}) collective-permute-start(f32[520,128]{1,0:T(8,128)S(1)} %get-tuple-element.19), channel_id=1, source_target_pairs={{0,8},{4,12},{8,0},{12,4},{1,9},{5,13},{9,1},{13,5},{2,10},{6,14},... | collective-permute-start | bytes 798728 | tf_op jit(solution)/shard_map/ppermute | solution.py:122
  31.6 6.5 %collective-permute-start.3 = (f32[520,128]{1,0:T(8,128)S(1)}, f32[520,128]{1,0:T(8,128)S(1)}, u32[]{:S(2)}, u32[]{:S(2)}) collective-permute-start(f32[520,128]{1,0:T(8,128)S(1)} %join.1.rest_0_), channel_id=1, source_target_pairs={{0,2},{2,0},{1,3},{3,1},{4,6},{6,4},{5,7},{7,5},{8,10},{10,8},{9,1... | collective-permute-start | bytes 798728 | tf_op jit(solution)/shard_map/ppermute | solution.py:312
  38.7 7.6 %collective-permute-start.4 = (f32[12,64,128]{2,1,0:T(8,128)S(1)}, f32[12,64,128]{2,1,0:T(8,128)S(1)}, u32[]{:S(2)}, u32[]{:S(2)}) collective-permute-start(f32[12,64,128]{2,1,0:T(8,128)S(1)} %pad_maximum_fusion.1), channel_id=1, source_target_pairs={{0,4},{4,8},{8,12},{1,5},{5,9},{9,13},{2,6},{6,10},{10,14},{3,7},{... | collective-permute-start | bytes 1179656 | tf_op jit(solution)/shard_map/ppermute | solution.py:293
  41.0 9.7 %collective-permute-start.5 = (f32[12,64,128]{2,1,0:T(8,128)S(1)}, f32[12,64,128]{2,1,0:T(8,128)S(1)}, u32[]{:S(2)}, u32[]{:S(2)}) collective-permute-start(f32[12,64,128]{2,1,0:T(8,128)S(1)} %pad_maximum_fusion.2), channel_id=1, source_target_pairs={{4,0},{8,4},{12,8},{5,1},{9,5},{13,9},{6,2},{10,6},{14,10},{7,3},{... | collective-permute-start | bytes 1179656 | tf_op jit(solution)/shard_map/ppermute | solution.py:293
  50.7 1.5 %collective-permute-start.6 = (f32[40,8,128]{2,1,0:T(8,128)S(1)}, f32[40,8,128]{2,1,0:T(8,128)S(1)}, u32[]{:S(2)}, u32[]{:S(2)}) collective-permute-start(f32[40,8,128]{2,1,0:T(8,128)S(1)} %pad_maximum_fusion.4), channel_id=1, source_target_pairs={{0,1},{1,0},{2,3},{3,2},{4,5},{5,4},{6,7},{7,6},{8,9},{9,8},{10,11... | collective-permute-start | bytes 491528 | tf_op jit(solution)/shard_map/ppermute | solution.py:302
  55.2 10.2 %collective-permute-start.8 = (f32[8,64,128]{2,1,0:T(8,128)S(1)}, f32[8,64,128]{2,1,0:T(8,128)S(1)}, u32[]{:S(2)}, u32[]{:S(2)}) collective-permute-start(f32[8,64,128]{2,1,0:T(8,128)S(1)} %get-tuple-element.4.rest_0_), channel_id=1, source_target_pairs={{4,0},{8,4},{12,8},{5,1},{9,5},{13,9},{6,2},{10,6},{14,10},{7,3},{... | collective-permute-start | bytes 786440 | tf_op jit(solution)/shard_map/ppermute | solution.py:293
  56.5 10.1 %collective-permute-start.7 = (f32[8,64,128]{2,1,0:T(8,128)S(1)}, f32[8,64,128]{2,1,0:T(8,128)S(1)}, u32[]{:S(2)}, u32[]{:S(2)}) collective-permute-start(f32[8,64,128]{2,1,0:T(8,128)S(1)} %get-tuple-element.4.rest_0_), channel_id=1, source_target_pairs={{0,4},{4,8},{8,12},{1,5},{5,9},{9,13},{2,6},{6,10},{10,14},{3,7},{... | collective-permute-start | bytes 786440 | tf_op jit(solution)/shard_map/ppermute | solution.py:293
  66.7 1.4 %collective-permute-start.9 = (f32[24,8,128]{2,1,0:T(8,128)S(1)}, f32[24,8,128]{2,1,0:T(8,128)S(1)}, u32[]{:S(2)}, u32[]{:S(2)}) collective-permute-start(f32[24,8,128]{2,1,0:T(8,128)S(1)} %pad_maximum_fusion.5), channel_id=1, source_target_pairs={{0,1},{1,0},{2,3},{3,2},{4,5},{5,4},{6,7},{7,6},{8,9},{9,8},{10,11... | collective-permute-start | bytes 294920 | tf_op jit(solution)/shard_map/ppermute | solution.py:302

commit v3 on v2

--- a/solution.py
+++ b/solution.py
@@ -19,6 +19,7 @@
 HBM = pl.BlockSpec(memory_space=pltpu.HBM)
 VMEM_BYTES = 48 * 1024 * 1024
 DEPOSIT_VMEM_BYTES = 60 * 1024 * 1024
+LATE_BYTES = 4 * 1024 * 1024
 
 
 def bit_count(count):
@@ -27,17 +28,24 @@
     return bits
 
 
-def reversed_bits(value, bits):
+def step_bits(slabs, odd):
+    order = list(range(bit_count(slabs)))
+    if odd and len(order) > 1:
+        order[:2] = [1, 0]
+    return order
+
+
+def section_of(value, order):
     result = 0
-    for bit in range(bits):
-        result = result | (((value >> bit) & 1) << (bits - 1 - bit))
+    for step, bit in enumerate(order):
+        result = result | (((value >> bit) & 1) << (len(order) - 1 - step))
     return result
 
 
 def deposit_kernel(
-    target_hbm, first_hbm, level_hbm, fraction_hbm, camera_hbm, out_ref, target, first, level, fraction, camera,
-    small_sems, camera_sems, *, bits, section, chunk
+    target_hbm, first_hbm, level_hbm, fraction_hbm, camera_hbm, *rest, slabs, section, chunk
 ):
+    *out_refs, sums_ref, target, first, level, fraction, camera, small_sems, camera_sems = rest
     blocks, planes, rows, cols = camera.shape
     sources = ((target_hbm, target), (first_hbm, first), (level_hbm, level), (fraction_hbm, fraction))
     smalls = [pltpu.make_async_copy(*pair, small_sems.at[i]) for i, pair in enumerate(sources)]
@@ -47,17 +55,19 @@
         parts.append(pltpu.make_async_copy(camera_hbm.at[here], camera.at[here], camera_sems.at[i]))
     for copy in smalls + parts:
         copy.start()
-    out_ref[...] = jnp.zeros(out_ref.shape, F32)
+    sums_ref[...] = jnp.zeros(sums_ref.shape, F32)
     for copy in smalls:
         copy.wait()
     place = lax.axis_index("gz").astype(jnp.int32)
+    odd = lax.axis_index("gy") % 2 == 1
     base_level = level[0].astype(F32)
     upper_share = fraction[0]
     lower_share = 1.0 - upper_share
     plane_at = lax.broadcasted_iota(jnp.int32, (CZ, cols), 0)
 
     def one(block, carry):
-        slab = reversed_bits(target[block] ^ place, bits)
+        away = target[block] ^ place
+        slab = jnp.where(odd, section_of(away, step_bits(slabs, True)), section_of(away, step_bits(slabs, False)))
         at = first[block]
         start = pl.multiple_of(slab * section, SUB)
         base = pl.multiple_of(start + at * rows, SUB)
@@ -65,27 +75,32 @@
         for plane in range(planes - 1):
             upper = camera[block, plane + 1] - base_level
             here = pl.ds(pl.multiple_of(base + plane * rows, SUB), rows)
-            out_ref[here, :] += lower_share * lower + upper_share * upper
+            sums_ref[here, :] += lower_share * lower + upper_share * upper
             lower = upper
         counts = pl.ds(pl.multiple_of(start + CZ * rows, SUB), CZ)
-        out_ref[counts, :] += ((plane_at >= at) & (plane_at < at + planes - 1)).astype(F32)
+        sums_ref[counts, :] += ((plane_at >= at) & (plane_at < at + planes - 1)).astype(F32)
         return carry
 
     for i, copy in enumerate(parts):
         copy.wait()
         lax.fori_loop(i * chunk, (i + 1) * chunk, one, 0, unroll=True)
-
-
-def deposit(camera, target, first, level, fraction, slabs):
+    at = 0
+    for out_ref in out_refs:
+        out_ref[...] = sums_ref[at : at + out_ref.shape[0]]
+        at += out_ref.shape[0]
+
+
+def deposit(camera, target, first, level, fraction, slabs, shares):
     blocks, planes, rows, cols = camera.shape
     section = CZ * rows + CZ
     chunk = SUB if blocks % SUB == 0 else blocks
     return pl.pallas_call(
-        functools.partial(deposit_kernel, bits=bit_count(slabs), section=section, chunk=chunk),
+        functools.partial(deposit_kernel, slabs=slabs, section=section, chunk=chunk),
         in_specs=[HBM] * 5,
-        out_specs=VMEM,
-        out_shape=jax.ShapeDtypeStruct((slabs * section, cols), F32),
+        out_specs=[VMEM] * len(shares),
+        out_shape=[jax.ShapeDtypeStruct((share * section, cols), F32) for share in shares],
         scratch_shapes=[
+            pltpu.VMEM((slabs * section, cols), F32),
             pltpu.SMEM(target.shape, jnp.int32),
             pltpu.SMEM(first.shape, jnp.int32),
             pltpu.SMEM(level.shape, jnp.int32),
@@ -99,30 +114,76 @@
     )(target, first, level, fraction, camera)
 
 
-def butterfly(sums, slabs, section):
-    bits = bit_count(slabs)
-    own = sums
-    count = slabs
-    late = None
-    for bit in range(bits):
-        half = count // 2
-        pairs = [(i, i ^ (1 << bit)) for i in range(slabs)]
-        keep, send = own[: half * section], own[half * section :]
-        if late is not None:
-            send = send + late[1]
-            keep = keep + late[0]
-        if half > 1:
-            cut = half // 2 * section
-            onward = lax.ppermute(send[cut:], "gz", pairs)
-            stays = lax.ppermute(send[:cut], "gz", pairs)
-            late = (stays, onward)
-            next_half = half // 2
-            own = keep
-        else:
-            arrived = lax.ppermute(send, "gz", pairs)
-            return keep, arrived
-        count = half
-    return own, jnp.zeros_like(own)
+def gz_pairs(partner):
+    count, bands = lax.axis_size("gz"), lax.axis_size("gy")
+    pairs = []
+    for place in range(count):
+        for band in range(bands):
+            other = partner(place, band % 2 == 1)
+            if 0 <= other < count:
+                pairs.append((place * bands + band, other * bands + band))
+    return pairs
+
+
+def first_shares(slabs):
+    if slabs <= 2:
+        return [1] * slabs
+    return [slabs // 4] * 4
+
+
+def fetch_kernel(*refs):
+    sources, targets, sems = refs[: len(refs) // 2], refs[len(refs) // 2 : -1], refs[-1]
+    copies = [pltpu.make_async_copy(*pair, sems.at[i]) for i, pair in enumerate(zip(sources, targets))]
+    for copy in copies:
+        copy.start()
+    for copy in copies:
+        copy.wait()
+
+
+def fetch(*arrays):
+    return pl.pallas_call(
+        fetch_kernel,
+        in_specs=[HBM] * len(arrays),
+        out_specs=[VMEM] * len(arrays),
+        out_shape=[jax.ShapeDtypeStruct(array.shape, array.dtype) for array in arrays],
+        scratch_shapes=[pltpu.SemaphoreType.DMA((len(arrays),))],
+        compiler_params=pltpu.CompilerParams(vmem_limit_bytes=VMEM_BYTES),
+        name="fetch",
+    )(*arrays)
+
+
+def add_kernel(left_ref, right_ref, out_ref):
+    out_ref[...] = left_ref[...] + right_ref[...]
+
+
+def add(left, right, cost=None):
+    return pl.pallas_call(
+        add_kernel,
+        in_specs=[VMEM] * 2,
+        out_specs=VMEM,
+        out_shape=jax.ShapeDtypeStruct(left.shape, F32),
+        compiler_params=pltpu.CompilerParams(vmem_limit_bytes=VMEM_BYTES),
+        cost_estimate=cost,
+        name="add",
+    )(left, right)
+
+
+def butterfly(shares, slabs, section):
+    if slabs == 1:
+        return shares[0], jnp.zeros_like(shares[0])
+    for step in range(bit_count(slabs)):
+        pairs = gz_pairs(lambda place, odd: place ^ (1 << step_bits(slabs, odd)[step]))
+        if len(shares) == 2:
+            return shares[0], lax.ppermute(shares[1], ("gz", "gy"), pairs)
+        keep, send, stays, onward = shares
+        if step == 0:
+            keep, send = fetch(keep, send)
+        onward = lax.ppermute(onward, ("gz", "gy"), pairs)
+        stays = lax.ppermute(stays, ("gz", "gy"), pairs)
+        send = add(send, onward)
+        keep = add(keep, stays, pl.CostEstimate(flops=0, bytes_accessed=LATE_BYTES, transcendentals=0))
+        half = keep.shape[0] // 2
+        shares = [keep, send] if keep.shape[0] == section else [keep[:half], keep[half:], send[:half], send[half:]]
 
 
 def join_kernel(small_ref, kept_ref, arrived_ref, message_ref, *, rows):
@@ -293,6 +354,17 @@
     return lax.ppermute(upward, axis, up), lax.ppermute(downward, axis, down)
 
 
+def from_slabs_beside(upward, downward):
+    odd = lax.axis_index("gy") % 2 == 1
+    if upward is downward:
+        sends = (upward, downward)
+    else:
+        sends = (jnp.where(odd, downward, upward), jnp.where(odd, upward, downward))
+    first = lax.ppermute(sends[0], ("gz", "gy"), gz_pairs(lambda place, odd: place - 1 if odd else place + 1))
+    second = lax.ppermute(sends[1], ("gz", "gy"), gz_pairs(lambda place, odd: place + 1 if odd else place - 1))
+    return jnp.where(odd, second, first), jnp.where(odd, first, second)
+
+
 def edge_rows(pieces, width):
     count = lax.axis_size("gy")
     rows = pieces[0].shape[-2]
@@ -321,10 +393,11 @@
     margin = taps // 2
     section = CZ * rows + CZ
     fraction = shift_frac[0]
-    sums = deposit(
-        camera[0], destination.reshape(blocks), offsets.reshape(blocks), background.reshape(1), fraction, slabs
+    shares = deposit(
+        camera[0], destination.reshape(blocks), offsets.reshape(blocks), background.reshape(1), fraction, slabs,
+        first_shares(slabs),
     )
-    kept, arrived = butterfly(sums, slabs, section)
+    kept, arrived = butterfly(shares, slabs, section)
     small = jnp.concatenate(
         [
             jnp.pad(psf_taps[0], ((0, 0), (0, cols - taps))),
@@ -339,7 +412,7 @@
     estimate = jnp.sum(all_joined, axis=0) / views
     upward = jnp.concatenate([all_joined[:, CZ - margin :].reshape(views * margin, rows, cols), estimate[: CZ - margin]])
     downward = jnp.concatenate([all_joined[:, :margin].reshape(views * margin, rows, cols), estimate[margin:]])
-    below, above = from_beside("gz", upward, downward)
+    below, above = from_slabs_beside(upward, downward)
     wide = 2 * margin
     low_rows, high_rows = edge_rows([below, above, all_joined.reshape(views * CZ, rows, cols)], wide)
 
@@ -358,7 +431,7 @@
     later = ()
     for iteration in range(ITERS):
         if iteration:
-            est_below, est_above = from_beside("gz", estimate, estimate)
+            est_below, est_above = from_slabs_beside(estimate, estimate)
             later = (estimate, est_below, est_above) + edge_rows([est_below, estimate, est_above], wide)
         result = update(weights, bands, all_joined, below, above, low_rows, high_rows, message, later, margin)
         estimate = result if later else result[0]

time: 72 us -> 69.2 us (0.961)
  waiting for transfers between devices: 36.6 us -> 30.3 us
  starting transfers between devices: 18.7 us -> 23 us
  other arithmetic: 3.41 us -> 1.43 us
  local copies, waits for them, and re-layouts: 1.71 us -> 2.64 us
    ppermute x7, waiting for transfers between devices: 29.2 us -> 21.4 us  [the longest x2 7.56 us: from_slabs_beside(): lax.ppermute(sends[1], ('gz', 'gy'), gz_pairs(lambda place, odd: place +...]
    ppermute x2, starting transfers between devices: 0.14 us -> 3.07 us  [edge_rows(): arrived = lax.ppermute(jnp.concatenate(parts), 'gy', [(0, 1), (1, 0)])]
    ppermute x1, waiting for transfers between devices: 4.78 us -> 7.09 us  [from_views(): return jnp.stack([message, lax.ppermute(message, 'view', [(0, 1), (1, 0)])])]
    add x2 -> x0, other arithmetic: 2.07 us -> none  [the longest x1 1.09 us: butterfly(): send = send + late[1]]
    unnamed x5 -> x9, local copies, waits for them, and re-layouts: 0.01 us -> 1.91 us
    ppermute x7, starting transfers between devices: 17 us -> 18.4 us  [the longest x2 9.16 us: from_slabs_beside(): lax.ppermute(sends[0], ('gz', 'gy'), gz_pairs(lambda place, odd: place -...]
    slice x3 -> x2, local copies, waits for them, and re-layouts: 1.03 us -> 0.05 us  [the longest x1 0.03 us: on_device(): all_joined[:, CZ - margin:].reshape(views * margin, rows, cols)]
    pallas_call x1 -> x4, Pallas kernels: 3.03 us -> 3.15 us  [the longest x1 3.03 us: deposit(): pl.pallas_call(functools.partial(deposit_kernel, slabs=slabs, section=sec...]
  transfers between devices with their start and end apart: 10 -> 10, of which waited for: 10 -> 9; matrix products, arithmetic and copies ran while one was open for 3% -> 2% of each run, Pallas kernels for 0% -> 0%
where the time goes in v3:
time: 69.2 us; the launch traced here: 68.9 us
  waiting for transfers between devices  30.3 us (44%)
  starting transfers between devices  23 us (33%)
  Pallas kernels  9.88 us (14%)
  local copies, waits for them, and re-layouts  2.64 us (4%)
  between operations  1.61 us (2%)
  other arithmetic  1.43 us (2%)
    ppermute x2, starting transfers between devices, from_slabs_beside(): lax.ppermute(sends[0], ('gz', 'gy'), gz_pairs(lambda place, odd: place -...  9.16 us
    ppermute x2, waiting for transfers between devices, from_slabs_beside(): lax.ppermute(sends[1], ('gz', 'gy'), gz_pairs(lambda place, odd: place +...  7.56 us
    ppermute x1, waiting for transfers between devices, from_views(): return jnp.stack([message, lax.ppermute(message, 'view', [(0, 1), (1, 0)])])  7.09 us
    pallas_call x2, Pallas kernels, update(): pl.pallas_call(functools.partial(update_kernel, views=views, margin=margi...  6.59 us
    ppermute x1, waiting for transfers between devices, butterfly(): stays = lax.ppermute(stays, ('gz', 'gy'), pairs)  6.26 us
    ppermute x1, waiting for transfers between devices, butterfly(): onward = lax.ppermute(onward, ('gz', 'gy'), pairs)  4.73 us
    ppermute x1, starting transfers between devices, butterfly(): return (shares[0], lax.ppermute(shares[1], ('gz', 'gy'), pairs))  3.49 us
    ppermute x1, starting transfers between devices, butterfly(): onward = lax.ppermute(onward, ('gz', 'gy'), pairs)  3.09 us
  transfers between devices with their start and end apart: 10, of which 9 were waited for; matrix products, arithmetic and copies ran while one was open for 2% of the time, Pallas kernels for 0%

profile of v3, /device:TPU:0, one launch (start us, length us, event | category | flops | bytes accessed | tf_op | source)
XLA Modules:
  0.0 68.9 jit_solution(1077477874781019856)
XLA Ops:
  1.3 3.0 %deposit.1 = (f32[520,128]{1,0:T(8,128)}, f32[520,128]{1,0:T(8,128)}, f32[520,128]{1,0:T(8,128)}, f32[520,128]{1,0:T(8,128)}) custom-call(s32[32]{0:T(128)} %bitcast.36, s32[32]{0:T(128)} %bitcast.37, s32[1]{0:T(128)} %bitcast.21.level_hbm, f32[3]{0:T(128)} %bitcast.38, f32[32,3,64,128]{3,2,1,0:T(8,128)} %bitcast.28), custom_call_target="tpu_custom_call" | custom-call | tf_op jit(solution)/shard_map/deposit/pallas_call | solution.py:97
  4.4 3.1 %collective-permute-start.1 = (f32[520,128]{1,0:T(8,128)}, f32[520,128]{1,0:T(8,128)S(1)}, u32[]{:S(2)}, u32[]{:S(2)}) collective-permute-start(f32[520,128]{1,0:T(8,128)} %get-tuple-element.15), channel_id=1, source_target_pairs={{0,4},{1,9},{4,0},{5,13},{8,12},{9,1},{12,8},{13,5},{2,6},{3,11},{... | collective-permute-start | bytes 798728 | tf_op jit(solution)/shard_map/ppermute | solution.py:181
  7.4 0.1 collective-permute-start
  7.8 0.9 %copy-done = f32[520,128]{1,0:T(8,128)S(1)} copy-done((f32[520,128]{1,0:T(8,128)S(1)}, f32[520,128]{1,0:T(8,128)}, u32[]{:S(2)}) %copy-start) | copy-done | bytes 266264
  8.7 0.9 %copy-done.1 = f32[520,128]{1,0:T(8,128)S(1)} copy-done((f32[520,128]{1,0:T(8,128)S(1)}, f32[520,128]{1,0:T(8,128)}, u32[]{:S(2)}) %copy-start.1) | copy-done | bytes 266264
  9.8 4.7 %collective-permute-done.1.right_ref = f32[520,128]{1,0:T(8,128)S(1)} collective-permute-done((f32[520,128]{1,0:T(8,128)}, f32[520,128]{1,0:T(8,128)S(1)}, u32[]{:S(2)}, u32[]{:S(2)}) %collective-permute-start.1) | collective-permute-done | bytes 266272 | tf_op jit(solution)/shard_map/ppermute | solution.py:181
  14.6 3.5 %collective-permute-start.2 = (f32[520,128]{1,0:T(8,128)S(1)}, f32[520,128]{1,0:T(8,128)S(1)}, u32[]{:S(2)}, u32[]{:S(2)}) collective-permute-start(f32[520,128]{1,0:T(8,128)S(1)} %add.315), channel_id=1, source_target_pairs={{0,8},{1,5},{4,12},{5,1},{8,0},{9,13},{12,4},{13,9},{2,10},{3,7},{... | collective-permute-start | bytes 798728 | tf_op jit(solution)/shard_map/ppermute | solution.py:177
  18.3 6.3 %collective-permute-done.right_ref = f32[520,128]{1,0:T(8,128)S(1)} collective-permute-done((f32[520,128]{1,0:T(8,128)}, f32[520,128]{1,0:T(8,128)S(1)}, u32[]{:S(2)}, u32[]{:S(2)}) %collective-permute-start) | collective-permute-done | bytes 266272 | tf_op jit(solution)/shard_map/ppermute | solution.py:182
  24.6 1.1 %collective-permute-done.2.arrived_ref = f32[520,128]{1,0:T(8,128)S(1)} collective-permute-done((f32[520,128]{1,0:T(8,128)S(1)}, f32[520,128]{1,0:T(8,128)S(1)}, u32[]{:S(2)}, u32[]{:S(2)}) %collective-permute-start.2) | collective-permute-done | bytes 266272 | tf_op jit(solution)/shard_map/ppermute | solution.py:177
  25.7 0.1 join.1.rest_0_
  25.9 1.6 %collective-permute-start.3 = (f32[520,128]{1,0:T(8,128)S(1)}, f32[520,128]{1,0:T(8,128)S(1)}, u32[]{:S(2)}, u32[]{:S(2)}) collective-permute-start(f32[520,128]{1,0:T(8,128)S(1)} %join.1.rest_0_), channel_id=1, source_target_pairs={{0,2},{2,0},{1,3},{3,1},{4,6},{6,4},{5,7},{7,5},{8,10},{10,8},{9,1... | collective-permute-start | bytes 798728 | tf_op jit(solution)/shard_map/ppermute | solution.py:384
  27.6 7.1 %collective-permute-done.3 = f32[520,128]{1,0:T(8,128)S(1)} collective-permute-done((f32[520,128]{1,0:T(8,128)S(1)}, f32[520,128]{1,0:T(8,128)S(1)}, u32[]{:S(2)}, u32[]{:S(2)}) %collective-permute-start.3) | collective-permute-done | bytes 266272 | tf_op jit(solution)/shard_map/ppermute | solution.py:384
  34.7 0.1 fusion.22
  34.8 0.1 fusion.23
  35.0 1.3 %collective-permute-start.4 = (f32[12,64,128]{2,1,0:T(8,128)S(1)}, f32[12,64,128]{2,1,0:T(8,128)S(1)}, u32[]{:S(2)}, u32[]{:S(2)}) collective-permute-start(f32[12,64,128]{2,1,0:T(8,128)S(1)} %get-tuple-element.34), channel_id=1, source_target_pairs={{1,5},{4,0},{5,9},{8,4},{9,13},{12,8},{3,7},{6,2},{7,11},{10,6},{1... | collective-permute-start | bytes 1179656 | tf_op jit(solution)/shard_map/ppermute | solution.py:364
  36.3 4.6 %collective-permute-start.5 = (f32[12,64,128]{2,1,0:T(8,128)S(1)}, f32[12,64,128]{2,1,0:T(8,128)S(1)}, u32[]{:S(2)}, u32[]{:S(2)}) collective-permute-start(f32[12,64,128]{2,1,0:T(8,128)S(1)} %get-tuple-element.33), channel_id=1, source_target_pairs={{0,4},{4,8},{5,1},{8,12},{9,5},{13,9},{2,6},{6,10},{7,3},{10,14},{... | collective-permute-start | bytes 1179656 | tf_op jit(solution)/shard_map/ppermute | solution.py:363
  41.0 0.2 slice_reduce_fusion.8
  41.2 0.2 select_add_fusion.1
  41.4 0.1 reshape.179
  41.5 0.2 select_add_fusion
  41.7 5.2 %collective-permute-done.4 = f32[12,64,128]{2,1,0:T(8,128)S(1)} collective-permute-done((f32[12,64,128]{2,1,0:T(8,128)S(1)}, f32[12,64,128]{2,1,0:T(8,128)S(1)}, u32[]{:S(2)}, u32[]{:S(2)}) %collective-permute-start.4) | collective-permute-done | bytes 393248 | tf_op jit(solution)/shard_map/ppermute | solution.py:364
  47.0 1.9 %collective-permute-start.6 = (f32[40,8,128]{2,1,0:T(8,128)S(1)}, f32[40,8,128]{2,1,0:T(8,128)S(1)}, u32[]{:S(2)}, u32[]{:S(2)}) collective-permute-start(f32[40,8,128]{2,1,0:T(8,128)S(1)} %pad_maximum_fusion.4), channel_id=1, source_target_pairs={{0,1},{1,0},{2,3},{3,2},{4,5},{5,4},{6,7},{7,6},{8,9},{9,8},{10,11... | collective-permute-start | bytes 491528 | tf_op jit(solution)/shard_map/ppermute | solution.py:374
  49.0 0.9 %collective-permute-done.6.low_rows_ref.high_rows_ref = f32[40,8,128]{2,1,0:T(8,128)S(1)} collective-permute-done((f32[40,8,128]{2,1,0:T(8,128)S(1)}, f32[40,8,128]{2,1,0:T(8,128)S(1)}, u32[]{:S(2)}, u32[]{:S(2)}) %collective-permute-start.6) | collective-permute-done | bytes 163872 | tf_op jit(solution)/shard_map/ppermute | solution.py:374
  49.9 0.1 broadcast_in_dim.147.weight_ref
  50.1 3.0 %update.2 = (f32[8,64,128]{2,1,0:T(8,128)S(1)}, f32[512,128]{1,0:T(8,128)}) custom-call(f32[56,8,128]{2,1,0:T(8,128)S(1)} %broadcast_in_dim.147.weight_ref, bf16[2,2,128,128]{3,2,1,0:T(8,128)(2,1)S(1)} %get-tuple-element.42.high_band_ref, bf16[2,2,128,128]{3,2,1,0:T(8,128)(2,1)S(1)} %get-tuple-element.41.low_band_ref, f32[2,8,64,128]{3,2,1,0:T(8,128)S(1)} %bitcast.24, ...), custom_call_target="tpu_custom_call" | custom-call | tf_op jit(solution)/shard_map/update/pallas_call | solution.py:339
  53.1 1.3 %collective-permute-start.7 = (f32[8,64,128]{2,1,0:T(8,128)S(1)}, f32[8,64,128]{2,1,0:T(8,128)S(1)}, u32[]{:S(2)}, u32[]{:S(2)}) collective-permute-start(f32[8,64,128]{2,1,0:T(8,128)S(1)} %get-tuple-element.16.rest_0_), channel_id=1, source_target_pairs={{1,5},{4,0},{5,9},{8,4},{9,13},{12,8},{3,7},{6,2},{7,11},{10,6},{1... | collective-permute-start | bytes 786440 | tf_op jit(solution)/shard_map/ppermute | solution.py:364
  54.4 4.6 %collective-permute-start.8 = (f32[8,64,128]{2,1,0:T(8,128)S(1)}, f32[8,64,128]{2,1,0:T(8,128)S(1)}, u32[]{:S(2)}, u32[]{:S(2)}) collective-permute-start(f32[8,64,128]{2,1,0:T(8,128)S(1)} %get-tuple-element.16.rest_0_), channel_id=1, source_target_pairs={{0,4},{4,8},{5,1},{8,12},{9,5},{13,9},{2,6},{6,10},{7,3},{10,14},{... | collective-permute-start | bytes 786440 | tf_op jit(solution)/shard_map/ppermute | solution.py:363
  58.9 2.4 %collective-permute-done.7 = f32[8,64,128]{2,1,0:T(8,128)S(1)} collective-permute-done((f32[8,64,128]{2,1,0:T(8,128)S(1)}, f32[8,64,128]{2,1,0:T(8,128)S(1)}, u32[]{:S(2)}, u32[]{:S(2)}) %collective-permute-start.7) | collective-permute-done | bytes 262176 | tf_op jit(solution)/shard_map/ppermute | solution.py:364
  61.3 1.7 %collective-permute-done.8 = f32[8,64,128]{2,1,0:T(8,128)S(1)} collective-permute-done((f32[8,64,128]{2,1,0:T(8,128)S(1)}, f32[8,64,128]{2,1,0:T(8,128)S(1)}, u32[]{:S(2)}, u32[]{:S(2)}) %collective-permute-start.8) | collective-permute-done | bytes 262176 | tf_op jit(solution)/shard_map/ppermute | solution.py:363
  63.2 1.2 %collective-permute-start.9 = (f32[24,8,128]{2,1,0:T(8,128)S(1)}, f32[24,8,128]{2,1,0:T(8,128)S(1)}, u32[]{:S(2)}, u32[]{:S(2)}) collective-permute-start(f32[24,8,128]{2,1,0:T(8,128)S(1)} %pad_maximum_fusion.5), channel_id=1, source_target_pairs={{0,1},{1,0},{2,3},{3,2},{4,5},{5,4},{6,7},{7,6},{8,9},{9,8},{10,11... | collective-permute-start | bytes 294920 | tf_op jit(solution)/shard_map/ppermute | solution.py:374
  64.4 0.9 %collective-permute-done.9.rest_3_.rest_4_ = f32[24,8,128]{2,1,0:T(8,128)S(1)} collective-permute-done((f32[24,8,128]{2,1,0:T(8,128)S(1)}, f32[24,8,128]{2,1,0:T(8,128)S(1)}, u32[]{:S(2)}, u32[]{:S(2)}) %collective-permute-start.9) | collective-permute-done | bytes 98336 | tf_op jit(solution)/shard_map/ppermute | solution.py:374
  65.3 3.6 %update.3 = f32[8,64,128]{2,1,0:T(8,128)} custom-call(f32[56,8,128]{2,1,0:T(8,128)S(1)} %broadcast_in_dim.147.weight_ref, bf16[2,2,128,128]{3,2,1,0:T(8,128)(2,1)S(1)} %get-tuple-element.42.high_band_ref, bf16[2,2,128,128]{3,2,1,0:T(8,128)(2,1)S(1)} %get-tuple-element.41.low_band_ref, f32[2,8,64,128]{3,2,1,0:T(8,128)S(1)} %bitcast.25, ...), custom_call_target="tpu_custom_call" | custom-call | tf_op jit(solution)/shard_map/update/pallas_call | solution.py:339
  (43 shorter events, 1.3 us)
Async XLA Ops:
  0.6 9.1 %copy-start.3 = (f32[1,3]{1,0:T(1,128)S(1)}, f32[1,3]{1,0:T(1,128)}, u32[]{:S(2)}) copy-start(f32[1,3]{1,0:T(1,128)} %param.10) | copy-start | bytes 40
  0.6 17.5 %copy-start.2 = (f32[1,3,9]{2,0,1:T(1,128)S(1)}, f32[1,3,9]{2,0,1:T(1,128)}, u32[]{:S(2)}) copy-start(f32[1,3,9]{2,0,1:T(1,128)} %param.11) | copy-start | bytes 328
  4.4 10.2 %collective-permute-start.1 = (f32[520,128]{1,0:T(8,128)}, f32[520,128]{1,0:T(8,128)S(1)}, u32[]{:S(2)}, u32[]{:S(2)}) collective-permute-start(f32[520,128]{1,0:T(8,128)} %get-tuple-element.15), channel_id=1, source_target_pairs={{0,4},{1,9},{4,0},{5,13},{8,12},{9,1},{12,8},{13,5},{2,6},{3,11},{... | collective-permute-start | bytes 798728 | tf_op jit(solution)/shard_map/ppermute | solution.py:181
  7.4 17.2 %collective-permute-start = (f32[520,128]{1,0:T(8,128)}, f32[520,128]{1,0:T(8,128)S(1)}, u32[]{:S(2)}, u32[]{:S(2)}) collective-permute-start(f32[520,128]{1,0:T(8,128)} %get-tuple-element.13), channel_id=1, source_target_pairs={{0,4},{1,9},{4,0},{5,13},{8,12},{9,1},{12,8},{13,5},{2,6},{3,11},{... | collective-permute-start | bytes 798728 | tf_op jit(solution)/shard_map/ppermute | solution.py:182
  7.8 1.0 %copy-start = (f32[520,128]{1,0:T(8,128)S(1)}, f32[520,128]{1,0:T(8,128)}, u32[]{:S(2)}) copy-start(f32[520,128]{1,0:T(8,128)} %get-tuple-element.10.refs_0_) | copy-start | bytes 798724
  8.7 1.0 %copy-start.1 = (f32[520,128]{1,0:T(8,128)S(1)}, f32[520,128]{1,0:T(8,128)}, u32[]{:S(2)}) copy-start(f32[520,128]{1,0:T(8,128)} %get-tuple-element.11.refs_1_) | copy-start | bytes 798724
  14.6 11.1 %collective-permute-start.2 = (f32[520,128]{1,0:T(8,128)S(1)}, f32[520,128]{1,0:T(8,128)S(1)}, u32[]{:S(2)}, u32[]{:S(2)}) collective-permute-start(f32[520,128]{1,0:T(8,128)S(1)} %add.315), channel_id=1, source_target_pairs={{0,8},{1,5},{4,12},{5,1},{8,0},{9,13},{12,4},{13,9},{2,10},{3,7},{... | collective-permute-start | bytes 798728 | tf_op jit(solution)/shard_map/ppermute | solution.py:177
  25.9 8.8 %collective-permute-start.3 = (f32[520,128]{1,0:T(8,128)S(1)}, f32[520,128]{1,0:T(8,128)S(1)}, u32[]{:S(2)}, u32[]{:S(2)}) collective-permute-start(f32[520,128]{1,0:T(8,128)S(1)} %join.1.rest_0_), channel_id=1, source_target_pairs={{0,2},{2,0},{1,3},{3,1},{4,6},{6,4},{5,7},{7,5},{8,10},{10,8},{9,1... | collective-permute-start | bytes 798728 | tf_op jit(solution)/shard_map/ppermute | solution.py:384
  35.0 11.9 %collective-permute-start.4 = (f32[12,64,128]{2,1,0:T(8,128)S(1)}, f32[12,64,128]{2,1,0:T(8,128)S(1)}, u32[]{:S(2)}, u32[]{:S(2)}) collective-permute-start(f32[12,64,128]{2,1,0:T(8,128)S(1)} %get-tuple-element.34), channel_id=1, source_target_pairs={{1,5},{4,0},{5,9},{8,4},{9,13},{12,8},{3,7},{6,2},{7,11},{10,6},{1... | collective-permute-start | bytes 1179656 | tf_op jit(solution)/shard_map/ppermute | solution.py:364
  36.3 10.6 %collective-permute-start.5 = (f32[12,64,128]{2,1,0:T(8,128)S(1)}, f32[12,64,128]{2,1,0:T(8,128)S(1)}, u32[]{:S(2)}, u32[]{:S(2)}) collective-permute-start(f32[12,64,128]{2,1,0:T(8,128)S(1)} %get-tuple-element.33), channel_id=1, source_target_pairs={{0,4},{4,8},{5,1},{8,12},{9,5},{13,9},{2,6},{6,10},{7,3},{10,14},{... | collective-permute-start | bytes 1179656 | tf_op jit(solution)/shard_map/ppermute | solution.py:363
  47.0 2.9 %collective-permute-start.6 = (f32[40,8,128]{2,1,0:T(8,128)S(1)}, f32[40,8,128]{2,1,0:T(8,128)S(1)}, u32[]{:S(2)}, u32[]{:S(2)}) collective-permute-start(f32[40,8,128]{2,1,0:T(8,128)S(1)} %pad_maximum_fusion.4), channel_id=1, source_target_pairs={{0,1},{1,0},{2,3},{3,2},{4,5},{5,4},{6,7},{7,6},{8,9},{9,8},{10,11... | collective-permute-start | bytes 491528 | tf_op jit(solution)/shard_map/ppermute | solution.py:374
  53.1 8.3 %collective-permute-start.7 = (f32[8,64,128]{2,1,0:T(8,128)S(1)}, f32[8,64,128]{2,1,0:T(8,128)S(1)}, u32[]{:S(2)}, u32[]{:S(2)}) collective-permute-start(f32[8,64,128]{2,1,0:T(8,128)S(1)} %get-tuple-element.16.rest_0_), channel_id=1, source_target_pairs={{1,5},{4,0},{5,9},{8,4},{9,13},{12,8},{3,7},{6,2},{7,11},{10,6},{1... | collective-permute-start | bytes 786440 | tf_op jit(solution)/shard_map/ppermute | solution.py:364
  54.4 8.7 %collective-permute-start.8 = (f32[8,64,128]{2,1,0:T(8,128)S(1)}, f32[8,64,128]{2,1,0:T(8,128)S(1)}, u32[]{:S(2)}, u32[]{:S(2)}) collective-permute-start(f32[8,64,128]{2,1,0:T(8,128)S(1)} %get-tuple-element.16.rest_0_), channel_id=1, source_target_pairs={{0,4},{4,8},{5,1},{8,12},{9,5},{13,9},{2,6},{6,10},{7,3},{10,14},{... | collective-permute-start | bytes 786440 | tf_op jit(solution)/shard_map/ppermute | solution.py:363
  63.2 2.2 %collective-permute-start.9 = (f32[24,8,128]{2,1,0:T(8,128)S(1)}, f32[24,8,128]{2,1,0:T(8,128)S(1)}, u32[]{:S(2)}, u32[]{:S(2)}) collective-permute-start(f32[24,8,128]{2,1,0:T(8,128)S(1)} %pad_maximum_fusion.5), channel_id=1, source_target_pairs={{0,1},{1,0},{2,3},{3,2},{4,5},{5,4},{6,7},{7,6},{8,9},{9,8},{10,11... | collective-permute-start | bytes 294920 | tf_op jit(solution)/shard_map/ppermute | solution.py:374

commit v4 on v3

--- a/solution.py
+++ b/solution.py
@@ -8,6 +8,7 @@
 from jax.sharding import PartitionSpec as P
 
 CZ = 8
+HALF = CZ // 2
 ITERS = 2
 
 
@@ -19,7 +20,6 @@
 HBM = pl.BlockSpec(memory_space=pltpu.HBM)
 VMEM_BYTES = 48 * 1024 * 1024
 DEPOSIT_VMEM_BYTES = 60 * 1024 * 1024
-LATE_BYTES = 4 * 1024 * 1024
 
 
 def bit_count(count):
@@ -63,22 +63,23 @@
     base_level = level[0].astype(F32)
     upper_share = fraction[0]
     lower_share = 1.0 - upper_share
-    plane_at = lax.broadcasted_iota(jnp.int32, (CZ, cols), 0)
+    count_at = lax.broadcasted_iota(jnp.int32, (SUB, cols), 0)
 
     def one(block, carry):
         away = target[block] ^ place
         slab = jnp.where(odd, section_of(away, step_bits(slabs, True)), section_of(away, step_bits(slabs, False)))
         at = first[block]
-        start = pl.multiple_of(slab * section, SUB)
-        base = pl.multiple_of(start + at * rows, SUB)
         lower = camera[block, 0] - base_level
         for plane in range(planes - 1):
             upper = camera[block, plane + 1] - base_level
-            here = pl.ds(pl.multiple_of(base + plane * rows, SUB), rows)
+            lands = at + plane
+            half = lands // HALF
+            start = (half * slabs + slab) * section
+            here = pl.ds(pl.multiple_of(start + (lands - half * HALF) * rows, SUB), rows)
             sums_ref[here, :] += lower_share * lower + upper_share * upper
+            counts = pl.ds(pl.multiple_of(start + HALF * rows, SUB), SUB)
+            sums_ref[counts, :] += (count_at == lands - half * HALF).astype(F32)
             lower = upper
-        counts = pl.ds(pl.multiple_of(start + CZ * rows, SUB), CZ)
-        sums_ref[counts, :] += ((plane_at >= at) & (plane_at < at + planes - 1)).astype(F32)
         return carry
 
     for i, copy in enumerate(parts):
@@ -92,15 +93,15 @@
 
 def deposit(camera, target, first, level, fraction, slabs, shares):
     blocks, planes, rows, cols = camera.shape
-    section = CZ * rows + CZ
+    section = HALF * rows + SUB
     chunk = SUB if blocks % SUB == 0 else blocks
     return pl.pallas_call(
         functools.partial(deposit_kernel, slabs=slabs, section=section, chunk=chunk),
         in_specs=[HBM] * 5,
-        out_specs=[VMEM] * len(shares),
-        out_shape=[jax.ShapeDtypeStruct((share * section, cols), F32) for share in shares],
+        out_specs=[VMEM] * (2 * len(shares)),
+        out_shape=[jax.ShapeDtypeStruct((share * section, cols), F32) for share in shares * 2],
         scratch_shapes=[
-            pltpu.VMEM((slabs * section, cols), F32),
+            pltpu.VMEM((2 * slabs * section, cols), F32),
             pltpu.SMEM(target.shape, jnp.int32),
             pltpu.SMEM(first.shape, jnp.int32),
             pltpu.SMEM(level.shape, jnp.int32),
@@ -156,45 +157,51 @@
     out_ref[...] = left_ref[...] + right_ref[...]
 
 
-def add(left, right, cost=None):
+def add(left, right):
     return pl.pallas_call(
         add_kernel,
         in_specs=[VMEM] * 2,
         out_specs=VMEM,
         out_shape=jax.ShapeDtypeStruct(left.shape, F32),
         compiler_params=pltpu.CompilerParams(vmem_limit_bytes=VMEM_BYTES),
-        cost_estimate=cost,
         name="add",
     )(left, right)
 
 
-def butterfly(shares, slabs, section):
+def butterfly(halves, slabs, section):
     if slabs == 1:
-        return shares[0], jnp.zeros_like(shares[0])
+        return [(shares[0], jnp.zeros_like(shares[0])) for shares in halves]
     for step in range(bit_count(slabs)):
         pairs = gz_pairs(lambda place, odd: place ^ (1 << step_bits(slabs, odd)[step]))
-        if len(shares) == 2:
-            return shares[0], lax.ppermute(shares[1], ("gz", "gy"), pairs)
-        keep, send, stays, onward = shares
+
+        def exchange(array):
+            return lax.ppermute(array, ("gz", "gy"), pairs)
+
+        if len(halves[0]) == 2:
+            return [(shares[0], exchange(shares[1])) for shares in halves]
         if step == 0:
-            keep, send = fetch(keep, send)
-        onward = lax.ppermute(onward, ("gz", "gy"), pairs)
-        stays = lax.ppermute(stays, ("gz", "gy"), pairs)
-        send = add(send, onward)
-        keep = add(keep, stays, pl.CostEstimate(flops=0, bytes_accessed=LATE_BYTES, transcendentals=0))
-        half = keep.shape[0] // 2
-        shares = [keep, send] if keep.shape[0] == section else [keep[:half], keep[half:], send[:half], send[half:]]
+            fetched = fetch(*(shares[1] for shares in halves))
+            halves = [[shares[0], array, *shares[2:]] for shares, array in zip(halves, fetched)]
+        onward = [exchange(shares[3]) for shares in halves]
+        stays = [exchange(shares[2]) for shares in halves]
+        sends = [add(shares[1], array) for shares, array in zip(halves, onward)]
+        keeps = [add(shares[0], array) for shares, array in zip(halves, stays)]
+        half = keeps[0].shape[0] // 2
+        if keeps[0].shape[0] == section:
+            halves = [list(pair) for pair in zip(keeps, sends)]
+        else:
+            halves = [[keep[:half], keep[half:], send[:half], send[half:]] for keep, send in zip(keeps, sends)]
 
 
 def join_kernel(small_ref, kept_ref, arrived_ref, message_ref, *, rows):
     cols = kept_ref.shape[1]
     total = kept_ref[...] + arrived_ref[...]
-    planes = total[: CZ * rows].reshape(CZ, rows, cols)
-    counts = total[CZ * rows :]
+    planes = total[: HALF * rows].reshape(HALF, rows, cols)
+    counts = total[HALF * rows :]
     fy, fx = small_ref[3:4], small_ref[4:5]
     row_at = lax.broadcasted_iota(jnp.int32, (rows, cols), 0)
     col_at = lax.broadcasted_iota(jnp.int32, (rows, cols), 1)
-    for plane in range(CZ):
+    for plane in range(HALF):
         part = planes[plane]
         follow = jnp.where(row_at == rows - 1, part, pltpu.roll(part, rows - 1, 0))
         part = (1.0 - fy) * part + fy * follow
@@ -202,7 +209,7 @@
         part = (1.0 - fx) * part + fx * follow
         part = jnp.maximum(part / (counts[plane : plane + 1] + 1.0), DATA_FLOOR)
         message_ref[plane * rows : (plane + 1) * rows] = part
-    message_ref[CZ * rows :] = small_ref[...]
+    message_ref[HALF * rows :] = small_ref[...]
 
 
 def join(small, kept, arrived, rows):
@@ -223,41 +230,65 @@
     return result
 
 
-def band_dot(values, high_part, low_part):
+def parts_of(values):
+    top = values.astype(jnp.bfloat16)
+    return top, (values - top.astype(F32)).astype(jnp.bfloat16)
+
+
+def columns_blurred(values, bands):
     cols = values.shape[1]
-    top = values.astype(jnp.bfloat16)
-    rest = (values - top.astype(F32)).astype(jnp.bfloat16)
-    both = jnp.dot(top, jnp.concatenate([high_part, low_part], axis=1), preferred_element_type=F32)
-    return both[:, :cols] + both[:, cols:] + jnp.dot(rest, high_part, preferred_element_type=F32)
+    both = jnp.dot(jnp.concatenate(parts_of(values), axis=1), bands, preferred_element_type=F32)
+    return both[:, :cols] + both[:, cols:]
+
+
+def rows_blurred(planes, bands):
+    results = []
+    for at in range(0, len(planes), 2):
+        stacks = []
+        for plane in planes[at : at + 2]:
+            top, rest = parts_of(plane)
+            stacks.append(jnp.concatenate([top, rest, top], axis=0))
+        both = jnp.dot(bands, jnp.concatenate(stacks, axis=1), preferred_element_type=F32)
+        cols = planes[at].shape[1]
+        results += [both[:, index * cols : (index + 1) * cols] for index in range(len(stacks))]
+    return results
 
 
 def update_kernel(
-    weight_ref, high_band_ref, low_band_ref, own_ref, below_ref, above_ref, low_rows_ref, high_rows_ref, *rest,
+    weight_ref, row_band_ref, col_band_ref, below_ref, above_ref, low_rows_ref, high_rows_ref, *rest,
     views, margin, first
 ):
+    halves, rest = rest[: 2 * views], rest[2 * views :]
     if first:
-        message_ref, out_ref, copied_hbm, *scratch, copied_sem = rest
-        copied = pltpu.make_async_copy(message_ref.at[pl.ds(0, copied_hbm.shape[0])], copied_hbm, copied_sem)
-        copied.start()
+        *own_refs, out_ref, copied_hbm, estimate, joined, first_pass, ratio, back_first, sems = rest
     else:
         est_ref, est_below_ref, est_above_ref, est_low_ref, est_high_ref, out_ref, *scratch = rest
-    estimate, joined, first_pass, ratio, back_first = scratch
-    _, planes, rows, cols = own_ref.shape
+        estimate, joined, first_pass, ratio, back_first = scratch
+    planes, rows, cols = out_ref.shape
+    if first:
+        length = HALF * rows
+        copies = [
+            pltpu.make_async_copy(ref.at[pl.ds(0, length)], copied_hbm.at[pl.ds(i * length, length)], sems.at[i])
+            for i, ref in enumerate(own_refs)
+        ]
+        for copy in copies:
+            copy.start()
     taps = 2 * margin + 1
     wide = 2 * margin
-    flag_low, flag_high = weight_ref[views * 3 * taps], weight_ref[views * 3 * taps + 1]
+    flag_low, flag_high = weight_ref[views * taps], weight_ref[views * taps + 1]
     low, body, high = slice(0, wide), slice(wide, wide + rows), slice(wide + rows, 2 * wide + rows)
 
     above_at = below_ref.shape[0]
     own_at = 2 * above_at
     for view in range(views):
-        pieces = (
-            (0, margin, below_ref, view * margin, view * margin),
-            (margin, planes, own_ref.at[view], 0, own_at + view * planes),
-            (margin + planes, margin, above_ref, view * margin, above_at + view * margin),
-        )
-        for to, length, source, at, edge_at in pieces:
-            joined[view, to : to + length, body] = source[at : at + length]
+        here = slice(view * margin, (view + 1) * margin)
+        pieces = [(0, margin, below_ref[here], view * margin)]
+        for half in range(2):
+            own = halves[2 * view + half][: HALF * rows].reshape(HALF, rows, cols)
+            pieces.append((margin + half * HALF, HALF, own, own_at + (2 * view + half) * HALF))
+        pieces.append((margin + planes, margin, above_ref[here], above_at + view * margin))
+        for to, length, source, edge_at in pieces:
+            joined[view, to : to + length, body] = source
             joined[view, to : to + length, low] = low_rows_ref[edge_at : edge_at + length] * flag_low
             joined[view, to : to + length, high] = high_rows_ref[edge_at : edge_at + length] * flag_high
     if first:
@@ -278,24 +309,22 @@
             estimate[here, high] = est_high_ref[here] * flag_high
 
     mid_planes, mid_rows = planes + 2 * margin, rows + 2 * margin
-    weights = [
-        [[weight_ref[(view * 3 + dim) * taps + tap] for tap in range(taps)] for dim in range(3)] for view in range(views)
-    ]
+    weights = [[weight_ref[view * taps + tap] for tap in range(taps)] for view in range(views)]
 
     def along_z(tile, carry):
         here = pl.ds(pl.multiple_of(tile * SUB, SUB), SUB)
         values = [estimate[plane, here, :] for plane in range(planes + 4 * margin)]
         for view in range(views):
             for plane in range(mid_planes):
-                first_pass[view, plane, here, :] = taps_sum(values[plane : plane + taps], weights[view][0])
+                first_pass[view, plane, here, :] = taps_sum(values[plane : plane + taps], weights[view])
         return carry
 
-    lax.fori_loop(0, (rows + 4 * margin) // SUB, along_z, 0)
+    lax.fori_loop(0, (rows + 4 * margin) // SUB, along_z, 0, unroll=2)
 
     for view in range(views):
-        values = [first_pass[view, :, tap : tap + mid_rows, :].reshape(-1, SUB, cols) for tap in range(taps)]
-        blurred = band_dot(
-            taps_sum(values, weights[view][1]).reshape(-1, cols), high_band_ref[view, 0], low_band_ref[view, 0]
+        blurred = rows_blurred([first_pass[view, plane] for plane in range(mid_planes)], row_band_ref[view, 0])
+        blurred = columns_blurred(
+            jnp.concatenate([plane[:mid_rows] for plane in blurred], axis=0), col_band_ref[view, 0]
         )
         ratio[view] = joined[view, :, margin : margin + mid_rows, :] / blurred.reshape(mid_planes, mid_rows, cols)
 
@@ -304,35 +333,37 @@
         for view in range(views):
             values = [ratio[view, plane, here, :] for plane in range(mid_planes)]
             for plane in range(planes):
-                back_first[view, plane, here, :] = taps_sum(values[plane : plane + taps], weights[view][0][::-1])
+                back_first[view, plane, here, :] = taps_sum(values[plane : plane + taps], weights[view][::-1])
         return carry
 
-    lax.fori_loop(0, mid_rows // SUB, back_z, 0)
+    lax.fori_loop(0, mid_rows // SUB, back_z, 0, unroll=True)
 
     logs = None
     for view in range(views):
-        values = [back_first[view, :, tap : tap + rows, :].reshape(-1, SUB, cols) for tap in range(taps)]
-        correction = band_dot(
-            taps_sum(values, weights[view][1][::-1]).reshape(-1, cols), high_band_ref[view, 1], low_band_ref[view, 1]
-        )
+        back_first[view, :, mid_rows:, :] = jnp.zeros((planes, 2 * margin, cols), F32)
+        blurred = rows_blurred([back_first[view, plane] for plane in range(planes)], row_band_ref[view, 1][:rows])
+        correction = columns_blurred(jnp.concatenate(blurred, axis=0), col_band_ref[view, 1])
         one = jnp.log(correction)
         logs = one if logs is None else logs + one
     out_ref[...] = estimate[wide : wide + planes, body] * jnp.exp(logs / views).reshape(planes, rows, cols)
     if first:
-        copied.wait()
-
-
-def update(weights, bands, own, below, above, low_rows, high_rows, message, later, margin):
-    views, planes, rows, cols = own.shape
+        for copy in copies:
+            copy.wait()
+
+
+def update(weights, bands, halves, below, above, low_rows, high_rows, own, later, margin):
     first = not later
-    arrays = [weights, *bands, own, below, above, low_rows, high_rows] + ([message] if first else list(later))
+    arrays = [weights, *bands, below, above, low_rows, high_rows, *halves] + list(own if first else later)
+    views = len(halves) // 2
+    _, rows, cols = below.shape
+    planes = CZ
     mid_planes, mid_rows = planes + 2 * margin, rows + 2 * margin
     scratch = [
         (planes + 4 * margin, rows + 4 * margin),
         (views, mid_planes, rows + 4 * margin),
         (views, mid_planes, rows + 4 * margin),
         (views, mid_planes, mid_rows),
-        (views, planes, mid_rows),
+        (views, planes, rows + 4 * margin),
     ]
     out_shape = jax.ShapeDtypeStruct((planes, rows, cols), F32)
     copy_shape = jax.ShapeDtypeStruct((planes * rows, cols), F32)
@@ -341,7 +372,7 @@
         in_specs=[VMEM] * len(arrays),
         out_specs=[VMEM, HBM] if first else VMEM,
         out_shape=[out_shape, copy_shape] if first else out_shape,
-        scratch_shapes=[pltpu.VMEM(shape + (cols,), F32) for shape in scratch] + [pltpu.SemaphoreType.DMA] * first,
+        scratch_shapes=[pltpu.VMEM(shape + (cols,), F32) for shape in scratch] + [pltpu.SemaphoreType.DMA((2,))] * first,
         compiler_params=pltpu.CompilerParams(vmem_limit_bytes=VMEM_BYTES),
         name="update",
     )(*arrays)
@@ -378,11 +409,19 @@
     return from_beside("gy", upward, downward)
 
 
+def band_matrix(kernels, length, margin):
+    places = jnp.arange(length, dtype=jnp.int32)
+    shift = places[None, :] - places[:, None] + margin
+    taps = kernels.shape[-1]
+    return sum(jnp.where(shift == tap, kernels[:, tap, None, None], 0.0) for tap in range(taps))
+
+
 def from_views(message):
     count = lax.axis_size("view")
     if count == 2:
-        return jnp.stack([message, lax.ppermute(message, "view", [(0, 1), (1, 0)])])
-    return lax.all_gather(message, "view")
+        return [message, lax.ppermute(message, "view", [(0, 1), (1, 0)])]
+    gathered = lax.all_gather(message, "view")
+    return [gathered[view] for view in range(count)]
 
 
 def on_device(camera, background, destination, offsets, shift_frac, psf_taps):
@@ -391,49 +430,57 @@
     _, blocks, _, rows, cols = camera.shape
     taps = psf_taps.shape[-1]
     margin = taps // 2
-    section = CZ * rows + CZ
+    assert margin == HALF
+    section = HALF * rows + SUB
     fraction = shift_frac[0]
     shares = deposit(
         camera[0], destination.reshape(blocks), offsets.reshape(blocks), background.reshape(1), fraction, slabs,
         first_shares(slabs),
     )
-    kept, arrived = butterfly(shares, slabs, section)
     small = jnp.concatenate(
         [
             jnp.pad(psf_taps[0], ((0, 0), (0, cols - taps))),
             jnp.broadcast_to(fraction[1:, None], (2, cols)),
-            jnp.zeros((CZ - 5, cols), F32),
+            jnp.zeros((SUB - 5, cols), F32),
         ]
     )
-    message = join(small, kept, arrived, rows)
-
-    messages = from_views(message)
-    all_joined = messages[:, : CZ * rows].reshape(views, CZ, rows, cols)
-    estimate = jnp.sum(all_joined, axis=0) / views
-    upward = jnp.concatenate([all_joined[:, CZ - margin :].reshape(views * margin, rows, cols), estimate[: CZ - margin]])
-    downward = jnp.concatenate([all_joined[:, :margin].reshape(views * margin, rows, cols), estimate[margin:]])
+    per = len(shares) // 2
+    own, messages = [], []
+    for kept, arrived in butterfly([shares[:per], shares[per:]], slabs, section):
+        own.append(join(small, kept, arrived, rows))
+        messages.append(from_views(own[-1]))
+    halves = [messages[half][view] for view in range(views) for half in range(2)]
+    low_half, high_half = (
+        [message[: HALF * rows].reshape(HALF, rows, cols) for message in messages[half]] for half in range(2)
+    )
+    upward = jnp.concatenate(high_half + [sum(low_half) / views])
+    downward = jnp.concatenate(low_half + [sum(high_half) / views])
     below, above = from_slabs_beside(upward, downward)
     wide = 2 * margin
-    low_rows, high_rows = edge_rows([below, above, all_joined.reshape(views * CZ, rows, cols)], wide)
-
-    all_taps = messages[:, CZ * rows : CZ * rows + 3, :taps]
+    pieces = [part for view in range(views) for part in (low_half[view], high_half[view])]
+    low_rows, high_rows = edge_rows([below, above] + pieces, wide)
+
+    all_taps = jnp.stack([message[HALF * rows : HALF * rows + 3, :taps] for message in messages[0]])
     kernels = all_taps / jnp.sum(all_taps, axis=-1, keepdims=True)
-    places = jnp.arange(cols, dtype=jnp.int32)
-    shift = places[:, None] - places[None, :] + margin
-    band = sum(jnp.where(shift == tap, kernels[:, 2, tap, None, None], 0.0) for tap in range(taps))
-    band = jnp.stack([band, jnp.swapaxes(band, 1, 2)], axis=1)
-    high_part = lax.reduce_precision(band, 8, 7)
-    bands = (high_part.astype(jnp.bfloat16), (band - high_part).astype(jnp.bfloat16))
+    row_bands = jnp.stack([band_matrix(kernels[:, 1, ::order], rows + 4 * margin, 0) for order in (1, -1)], axis=1)
+    high_part = lax.reduce_precision(row_bands, 8, 7)
+    row_bands = jnp.concatenate([high_part, high_part, row_bands - high_part], axis=-1).astype(jnp.bfloat16)
+    col_bands = jnp.stack([band_matrix(kernels[:, 2, ::order], cols, margin) for order in (1, -1)], axis=1)
+    col_bands = jnp.swapaxes(col_bands, -1, -2)
+    high_part = lax.reduce_precision(col_bands, 8, 7)
+    col_bands = jnp.concatenate([high_part, col_bands - high_part], axis=-1).astype(jnp.bfloat16)
+    bands = (row_bands, jnp.concatenate([col_bands, col_bands], axis=-2))
     row_band = lax.axis_index("gy")
     flags = jnp.stack([row_band > 0, row_band < lax.axis_size("gy") - 1]).astype(F32)
-    weights = jnp.broadcast_to(jnp.concatenate([kernels.reshape(-1), flags])[:, None, None], (views * 3 * taps + 2, SUB, cols))
+    weights = jnp.concatenate([kernels[:, 0].reshape(-1), flags])
+    weights = jnp.broadcast_to(weights[:, None, None], (views * taps + 2, SUB, cols))
 
     later = ()
     for iteration in range(ITERS):
         if iteration:
             est_below, est_above = from_slabs_beside(estimate, estimate)
             later = (estimate, est_below, est_above) + edge_rows([est_below, estimate, est_above], wide)
-        result = update(weights, bands, all_joined, below, above, low_rows, high_rows, message, later, margin)
+        result = update(weights, bands, halves, below, above, low_rows, high_rows, own, later, margin)
         estimate = result if later else result[0]
         joined = joined if later else result[1]
     return (estimate, joined.reshape(1, CZ, rows, cols))

time: 69.2 us -> 66.3 us (0.958)
  waiting for transfers between devices: 30.3 us -> 19.3 us
  starting transfers between devices: 23 us -> 28.6 us
  local copies, waits for them, and re-layouts: 2.64 us -> 5.57 us
  Pallas kernels: 9.88 us -> 9.1 us
    ppermute x4 -> x8, waiting for transfers between devices: 19.2 us -> 9.87 us  [the longest x6 6.82 us: exchange(): return lax.ppermute(array, ('gz', 'gy'), pairs)]
    ppermute x4 -> x8, starting transfers between devices: 8.21 us -> 13.9 us  [the longest x6 10 us: exchange(): return lax.ppermute(array, ('gz', 'gy'), pairs)]
    unnamed x9 -> x18, local copies, waits for them, and re-layouts: 1.91 us -> 3.69 us
    ppermute x2, waiting for transfers between devices: 7.56 us -> 6.08 us  [from_slabs_beside(): lax.ppermute(sends[1], ('gz', 'gy'), gz_pairs(lambda place, odd: place +...]
    pallas_call x2, Pallas kernels: 6.59 us -> 5.39 us  [update(): pl.pallas_call(functools.partial(update_kernel, views=views, margin=margi...]
    slice x3 -> x9, local copies, waits for them, and re-layouts: 0.24 us -> 1.24 us  [the longest x4 1.18 us: band_matrix(): kernels[:, tap, None, None]]
  transfers between devices with their start and end apart: 10 -> 14, of which waited for: 9 -> 10; matrix products, arithmetic and copies ran while one was open for 2% -> 5% of each run, Pallas kernels for 0% -> 1%
where the time goes in v4:
time: 66.3 us; the launch traced here: 66 us
  starting transfers between devices  28.6 us (43%)
  waiting for transfers between devices  19.3 us (29%)
  Pallas kernels  9.1 us (14%)
  local copies, waits for them, and re-layouts  5.57 us (8%)
  other arithmetic  1.75 us (3%)
  between operations  1.74 us (3%)
    ppermute x6, starting transfers between devices, exchange(): return lax.ppermute(array, ('gz', 'gy'), pairs)  10 us
    ppermute x2, starting transfers between devices, from_slabs_beside(): lax.ppermute(sends[0], ('gz', 'gy'), gz_pairs(lambda place, odd: place -...  9.24 us
    ppermute x6, waiting for transfers between devices, exchange(): return lax.ppermute(array, ('gz', 'gy'), pairs)  6.82 us
    ppermute x2, waiting for transfers between devices, from_slabs_beside(): lax.ppermute(sends[1], ('gz', 'gy'), gz_pairs(lambda place, odd: place +...  6.08 us
    pallas_call x2, Pallas kernels, update(): pl.pallas_call(functools.partial(update_kernel, views=views, margin=margi...  5.39 us
    ppermute x2, starting transfers between devices, from_views(): return [message, lax.ppermute(message, 'view', [(0, 1), (1, 0)])]  3.93 us
    unnamed x18, local copies, waits for them, and re-layouts  3.69 us
    pallas_call x1, Pallas kernels, deposit(): pl.pallas_call(functools.partial(deposit_kernel, slabs=slabs, section=sec...  3.08 us
  transfers between devices with their start and end apart: 14, of which 10 were waited for; matrix products, arithmetic and copies ran while one was open for 5% of the time, Pallas kernels for 1%

profile of v4, /device:TPU:0, one launch (start us, length us, event | category | flops | bytes accessed | tf_op | source)
XLA Modules:
  0.0 66.0 jit_solution(199823438004177496)
XLA Ops:
  1.3 3.1 %deposit.1 = (f32[264,128]{1,0:T(8,128)}, f32[264,128]{1,0:T(8,128)}, f32[264,128]{1,0:T(8,128)}, f32[264,128]{1,0:T(8,128)}, f32[264,128]{1,0:T(8,128)}, /*inde...) custom-call(s32[32]{0:T(128)} %bitcast.50, s32[32]{0:T(128)} %bitcast.51, s32[1]{0:T(128)} %bitcast.31.level_hbm, ...), custom_call_target="tpu_custom_call" | custom-call | tf_op jit(solution)/shard_map/deposit/pallas_call | solution.py:98
  4.4 3.1 %collective-permute-start.1 = (f32[264,128]{1,0:T(8,128)}, f32[264,128]{1,0:T(8,128)S(1)}, u32[]{:S(2)}, u32[]{:S(2)}) collective-permute-start(f32[264,128]{1,0:T(8,128)} %get-tuple-element.19), channel_id=1, source_target_pairs={{0,4},{1,9},{4,0},{5,13},{8,12},{9,1},{12,8},{13,5},{2,6},{3,11},{... | collective-permute-start | bytes 405512 | tf_op jit(solution)/shard_map/ppermute | solution.py:178
  7.6 1.9 %collective-permute-start.5 = (f32[264,128]{1,0:T(8,128)}, f32[264,128]{1,0:T(8,128)S(1)}, u32[]{:S(2)}, u32[]{:S(2)}) collective-permute-start(f32[264,128]{1,0:T(8,128)} %get-tuple-element.23), channel_id=1, source_target_pairs={{0,4},{1,9},{4,0},{5,13},{8,12},{9,1},{12,8},{13,5},{2,6},{3,11},{... | collective-permute-start | bytes 405512 | tf_op jit(solution)/shard_map/ppermute | solution.py:178
  10.2 0.9 %copy-done.2 = f32[264,128]{1,0:T(8,128)S(1)} copy-done((f32[264,128]{1,0:T(8,128)S(1)}, f32[264,128]{1,0:T(8,128)}, u32[]{:S(2)}) %copy-start.2) | copy-done | bytes 135192
  11.1 0.9 %copy-done.3 = f32[264,128]{1,0:T(8,128)S(1)} copy-done((f32[264,128]{1,0:T(8,128)S(1)}, f32[264,128]{1,0:T(8,128)}, u32[]{:S(2)}) %copy-start.3) | copy-done | bytes 135192
  12.0 0.3 fetch.1
  12.4 3.0 %collective-permute-start.2 = (f32[264,128]{1,0:T(8,128)S(1)}, f32[264,128]{1,0:T(8,128)S(1)}, u32[]{:S(2)}, u32[]{:S(2)}) collective-permute-start(f32[264,128]{1,0:T(8,128)S(1)} %add.515), channel_id=1, source_target_pairs={{0,8},{1,5},{4,12},{5,1},{8,0},{9,13},{12,4},{13,9},{2,10},{3,7},{... | collective-permute-start | bytes 405512 | tf_op jit(solution)/shard_map/ppermute | solution.py:178
  15.4 4.9 %collective-permute-done.5.right_ref = f32[264,128]{1,0:T(8,128)S(1)} collective-permute-done((f32[264,128]{1,0:T(8,128)}, f32[264,128]{1,0:T(8,128)S(1)}, u32[]{:S(2)}, u32[]{:S(2)}) %collective-permute-start.5) | collective-permute-done | bytes 135200 | tf_op jit(solution)/shard_map/ppermute | solution.py:178
  20.3 1.8 %collective-permute-start.6 = (f32[264,128]{1,0:T(8,128)S(1)}, f32[264,128]{1,0:T(8,128)S(1)}, u32[]{:S(2)}, u32[]{:S(2)}) collective-permute-start(f32[264,128]{1,0:T(8,128)S(1)} %add.517), channel_id=1, source_target_pairs={{0,8},{1,5},{4,12},{5,1},{8,0},{9,13},{12,4},{13,9},{2,10},{3,7},{... | collective-permute-start | bytes 405512 | tf_op jit(solution)/shard_map/ppermute | solution.py:178
  22.2 0.9 %copy-done.1 = f32[264,128]{1,0:T(8,128)S(1)} copy-done((f32[264,128]{1,0:T(8,128)S(1)}, f32[264,128]{1,0:T(8,128)}, u32[]{:S(2)}) %copy-start.1) | copy-done | bytes 135192
  23.1 1.6 %collective-permute-done.4.right_ref = f32[264,128]{1,0:T(8,128)S(1)} collective-permute-done((f32[264,128]{1,0:T(8,128)}, f32[264,128]{1,0:T(8,128)S(1)}, u32[]{:S(2)}, u32[]{:S(2)}) %collective-permute-start.4) | collective-permute-done | bytes 135200 | tf_op jit(solution)/shard_map/ppermute | solution.py:178
  24.8 0.9 %copy-done = f32[264,128]{1,0:T(8,128)S(1)} copy-done((f32[264,128]{1,0:T(8,128)S(1)}, f32[264,128]{1,0:T(8,128)}, u32[]{:S(2)}) %copy-start) | copy-done | bytes 135192
  25.8 2.0 %collective-permute-start.3 = (f32[264,128]{1,0:T(8,128)S(1)}, f32[264,128]{1,0:T(8,128)S(1)}, u32[]{:S(2)}, u32[]{:S(2)}) collective-permute-start(f32[264,128]{1,0:T(8,128)S(1)} %join.2.rest_0_.rest_4_), channel_id=1, source_target_pairs={{0,2},{2,0},{1,3},{3,1},{4,6},{6,4},{5,7},{7,5},{8,10},{10,8},{9,1... | collective-permute-start | bytes 405512 | tf_op jit(solution)/shard_map/ppermute | solution.py:422
  27.8 0.3 collective-permute-done.6.arrived_ref
  28.2 2.0 %collective-permute-start.7 = (f32[264,128]{1,0:T(8,128)S(1)}, f32[264,128]{1,0:T(8,128)S(1)}, u32[]{:S(2)}, u32[]{:S(2)}) collective-permute-start(f32[264,128]{1,0:T(8,128)S(1)} %join.3.rest_1_.rest_5_), channel_id=1, source_target_pairs={{0,2},{2,0},{1,3},{3,1},{4,6},{6,4},{5,7},{7,5},{8,10},{10,8},{9,1... | collective-permute-start | bytes 405512 | tf_op jit(solution)/shard_map/ppermute | solution.py:422
  30.2 1.5 %collective-permute-done.3.rest_2_ = f32[264,128]{1,0:T(8,128)S(1)} collective-permute-done((f32[264,128]{1,0:T(8,128)S(1)}, f32[264,128]{1,0:T(8,128)S(1)}, u32[]{:S(2)}, u32[]{:S(2)}) %collective-permute-start.3) | collective-permute-done | bytes 135200 | tf_op jit(solution)/shard_map/ppermute | solution.py:422
  31.7 1.6 %collective-permute-done.7.rest_3_ = f32[264,128]{1,0:T(8,128)S(1)} collective-permute-done((f32[264,128]{1,0:T(8,128)S(1)}, f32[264,128]{1,0:T(8,128)S(1)}, u32[]{:S(2)}, u32[]{:S(2)}) %collective-permute-start.7) | collective-permute-done | bytes 135200 | tf_op jit(solution)/shard_map/ppermute | solution.py:422
  33.4 1.3 %collective-permute-start.8 = (f32[12,64,128]{2,1,0:T(8,128)S(1)}, f32[12,64,128]{2,1,0:T(8,128)S(1)}, u32[]{:S(2)}, u32[]{:S(2)}) collective-permute-start(f32[12,64,128]{2,1,0:T(8,128)S(1)} %get-tuple-element.65), channel_id=1, source_target_pairs={{1,5},{4,0},{5,9},{8,4},{9,13},{12,8},{3,7},{6,2},{7,11},{10,6},{1... | collective-permute-start | bytes 1179656 | tf_op jit(solution)/shard_map/ppermute | solution.py:395
  34.7 4.6 %collective-permute-start.9 = (f32[12,64,128]{2,1,0:T(8,128)S(1)}, f32[12,64,128]{2,1,0:T(8,128)S(1)}, u32[]{:S(2)}, u32[]{:S(2)}) collective-permute-start(f32[12,64,128]{2,1,0:T(8,128)S(1)} %get-tuple-element.64), channel_id=1, source_target_pairs={{0,4},{4,8},{5,1},{8,12},{9,5},{13,9},{2,6},{6,10},{7,3},{10,14},{... | collective-permute-start | bytes 1179656 | tf_op jit(solution)/shard_map/ppermute | solution.py:394
  39.9 0.3 slice_reduce_fusion.36
  40.2 0.3 slice_reduce_fusion.27
  41.9 3.7 %collective-permute-done.8 = f32[12,64,128]{2,1,0:T(8,128)S(1)} collective-permute-done((f32[12,64,128]{2,1,0:T(8,128)S(1)}, f32[12,64,128]{2,1,0:T(8,128)S(1)}, u32[]{:S(2)}, u32[]{:S(2)}) %collective-permute-start.8) | collective-permute-done | bytes 393248 | tf_op jit(solution)/shard_map/ppermute | solution.py:395
  45.8 1.6 %collective-permute-start.10 = (f32[40,8,128]{2,1,0:T(8,128)S(1)}, f32[40,8,128]{2,1,0:T(8,128)S(1)}, u32[]{:S(2)}, u32[]{:S(2)}) collective-permute-start(f32[40,8,128]{2,1,0:T(8,128)S(1)} %dynamic-slice_dynamic-update-slice_fusion.2), channel_id=1, source_target_pairs={{0,1},{1,0},{2,3},{3,2},{4,5},{5,4},{6,7},{7,6},{8,9},{9,8},{10,11... | collective-permute-start | bytes 491528 | tf_op jit(solution)/shard_map/ppermute | solution.py:405
  47.5 0.9 %collective-permute-done.10.low_rows_ref.high_rows_ref = f32[40,8,128]{2,1,0:T(8,128)S(1)} collective-permute-done((f32[40,8,128]{2,1,0:T(8,128)S(1)}, f32[40,8,128]{2,1,0:T(8,128)S(1)}, u32[]{:S(2)}, u32[]{:S(2)}) %collective-permute-start.10) | collective-permute-done | bytes 163872 | tf_op jit(solution)/shard_map/ppermute | solution.py:405
  48.5 2.4 %update.2 = (f32[8,64,128]{2,1,0:T(8,128)S(1)}, f32[512,128]{1,0:T(8,128)}) custom-call(f32[20,8,128]{2,1,0:T(8,128)S(1)} %broadcast_in_dim.439.weight_ref, bf16[2,2,80,240]{3,2,1,0:T(8,128)(2,1)S(1)} %pad_maximum_fusion.3.row_band_ref, bf16[2,2,256,256]{3,2,1,0:T(8,128)(2,1)S(1)} %maximum_maximum_fusion.col_band_ref, ...), custom_call_target="tpu_custom_call" | custom-call | tf_op jit(solution)/shard_map/update/pallas_call | solution.py:370
  50.9 1.3 %collective-permute-start.11 = (f32[8,64,128]{2,1,0:T(8,128)S(1)}, f32[8,64,128]{2,1,0:T(8,128)S(1)}, u32[]{:S(2)}, u32[]{:S(2)}) collective-permute-start(f32[8,64,128]{2,1,0:T(8,128)S(1)} %get-tuple-element.24.rest_4_), channel_id=1, source_target_pairs={{1,5},{4,0},{5,9},{8,4},{9,13},{12,8},{3,7},{6,2},{7,11},{10,6},{1... | collective-permute-start | bytes 786440 | tf_op jit(solution)/shard_map/ppermute | solution.py:395
  52.2 4.7 %collective-permute-start.12 = (f32[8,64,128]{2,1,0:T(8,128)S(1)}, f32[8,64,128]{2,1,0:T(8,128)S(1)}, u32[]{:S(2)}, u32[]{:S(2)}) collective-permute-start(f32[8,64,128]{2,1,0:T(8,128)S(1)} %get-tuple-element.24.rest_4_), channel_id=1, source_target_pairs={{0,4},{4,8},{5,1},{8,12},{9,5},{13,9},{2,6},{6,10},{7,3},{10,14},{... | collective-permute-start | bytes 786440 | tf_op jit(solution)/shard_map/ppermute | solution.py:394
  56.9 2.4 %collective-permute-done.11 = f32[8,64,128]{2,1,0:T(8,128)S(1)} collective-permute-done((f32[8,64,128]{2,1,0:T(8,128)S(1)}, f32[8,64,128]{2,1,0:T(8,128)S(1)}, u32[]{:S(2)}, u32[]{:S(2)}) %collective-permute-start.11) | collective-permute-done | bytes 262176 | tf_op jit(solution)/shard_map/ppermute | solution.py:395
  59.3 1.5 %collective-permute-done.12 = f32[8,64,128]{2,1,0:T(8,128)S(1)} collective-permute-done((f32[8,64,128]{2,1,0:T(8,128)S(1)}, f32[8,64,128]{2,1,0:T(8,128)S(1)}, u32[]{:S(2)}, u32[]{:S(2)}) %collective-permute-start.12) | collective-permute-done | bytes 262176 | tf_op jit(solution)/shard_map/ppermute | solution.py:394
  60.9 1.2 %collective-permute-start.13 = (f32[24,8,128]{2,1,0:T(8,128)S(1)}, f32[24,8,128]{2,1,0:T(8,128)S(1)}, u32[]{:S(2)}, u32[]{:S(2)}) collective-permute-start(f32[24,8,128]{2,1,0:T(8,128)S(1)} %pad_maximum_fusion.4), channel_id=1, source_target_pairs={{0,1},{1,0},{2,3},{3,2},{4,5},{5,4},{6,7},{7,6},{8,9},{9,8},{10,11... | collective-permute-start | bytes 294920 | tf_op jit(solution)/shard_map/ppermute | solution.py:405
  62.1 0.9 %collective-permute-done.13.rest_7_.rest_8_ = f32[24,8,128]{2,1,0:T(8,128)S(1)} collective-permute-done((f32[24,8,128]{2,1,0:T(8,128)S(1)}, f32[24,8,128]{2,1,0:T(8,128)S(1)}, u32[]{:S(2)}, u32[]{:S(2)}) %collective-permute-start.13) | collective-permute-done | bytes 98336 | tf_op jit(solution)/shard_map/ppermute | solution.py:405
  63.0 3.0 %update.3 = f32[8,64,128]{2,1,0:T(8,128)} custom-call(f32[20,8,128]{2,1,0:T(8,128)S(1)} %broadcast_in_dim.439.weight_ref, bf16[2,2,80,240]{3,2,1,0:T(8,128)(2,1)S(1)} %pad_maximum_fusion.3.row_band_ref, bf16[2,2,256,256]{3,2,1,0:T(8,128)(2,1)S(1)} %maximum_maximum_fusion.col_band_ref, f32[12,64,128]{2,1,0:T(8,128)S(1)} %get-tuple-element.63.below_ref, ...), custom_call_target="tpu_custom_call" | custom-call | tf_op jit(solution)/shard_map/update/pallas_call | solution.py:370
  (75 shorter events, 3.6 us)
Async XLA Ops:
  0.6 9.0 %copy-start.5 = (f32[1,3]{1,0:T(1,128)S(1)}, f32[1,3]{1,0:T(1,128)}, u32[]{:S(2)}) copy-start(f32[1,3]{1,0:T(1,128)} %param.10) | copy-start | bytes 40
  0.6 9.2 %copy-start.4 = (f32[1,3,9]{2,0,1:T(1,128)S(1)}, f32[1,3,9]{2,0,1:T(1,128)}, u32[]{:S(2)}) copy-start(f32[1,3,9]{2,0,1:T(1,128)} %param.11) | copy-start | bytes 328
  4.4 7.9 %collective-permute-start.1 = (f32[264,128]{1,0:T(8,128)}, f32[264,128]{1,0:T(8,128)S(1)}, u32[]{:S(2)}, u32[]{:S(2)}) collective-permute-start(f32[264,128]{1,0:T(8,128)} %get-tuple-element.19), channel_id=1, source_target_pairs={{0,4},{1,9},{4,0},{5,13},{8,12},{9,1},{12,8},{13,5},{2,6},{3,11},{... | collective-permute-start | bytes 405512 | tf_op jit(solution)/shard_map/ppermute | solution.py:178
  7.5 14.7 %collective-permute-start = (f32[264,128]{1,0:T(8,128)}, f32[264,128]{1,0:T(8,128)S(1)}, u32[]{:S(2)}, u32[]{:S(2)}) collective-permute-start(f32[264,128]{1,0:T(8,128)} %get-tuple-element.15), channel_id=1, source_target_pairs={{0,4},{1,9},{4,0},{5,13},{8,12},{9,1},{12,8},{13,5},{2,6},{3,11},{... | collective-permute-start | bytes 405512 | tf_op jit(solution)/shard_map/ppermute | solution.py:178
  7.6 12.7 %collective-permute-start.5 = (f32[264,128]{1,0:T(8,128)}, f32[264,128]{1,0:T(8,128)S(1)}, u32[]{:S(2)}, u32[]{:S(2)}) collective-permute-start(f32[264,128]{1,0:T(8,128)} %get-tuple-element.23), channel_id=1, source_target_pairs={{0,4},{1,9},{4,0},{5,13},{8,12},{9,1},{12,8},{13,5},{2,6},{3,11},{... | collective-permute-start | bytes 405512 | tf_op jit(solution)/shard_map/ppermute | solution.py:178
  9.5 15.3 %collective-permute-start.4 = (f32[264,128]{1,0:T(8,128)}, f32[264,128]{1,0:T(8,128)S(1)}, u32[]{:S(2)}, u32[]{:S(2)}) collective-permute-start(f32[264,128]{1,0:T(8,128)} %get-tuple-element.21), channel_id=1, source_target_pairs={{0,4},{1,9},{4,0},{5,13},{8,12},{9,1},{12,8},{13,5},{2,6},{3,11},{... | collective-permute-start | bytes 405512 | tf_op jit(solution)/shard_map/ppermute | solution.py:178
  10.1 0.9 %copy-start.2 = (f32[264,128]{1,0:T(8,128)S(1)}, f32[264,128]{1,0:T(8,128)}, u32[]{:S(2)}) copy-start(f32[264,128]{1,0:T(8,128)} %get-tuple-element.16.refs_0_) | copy-start | bytes 405508
  11.1 0.9 %copy-start.3 = (f32[264,128]{1,0:T(8,128)S(1)}, f32[264,128]{1,0:T(8,128)}, u32[]{:S(2)}) copy-start(f32[264,128]{1,0:T(8,128)} %get-tuple-element.17.refs_1_) | copy-start | bytes 405508
  12.4 13.3 %collective-permute-start.2 = (f32[264,128]{1,0:T(8,128)S(1)}, f32[264,128]{1,0:T(8,128)S(1)}, u32[]{:S(2)}, u32[]{:S(2)}) collective-permute-start(f32[264,128]{1,0:T(8,128)S(1)} %add.515), channel_id=1, source_target_pairs={{0,8},{1,5},{4,12},{5,1},{8,0},{9,13},{12,4},{13,9},{2,10},{3,7},{... | collective-permute-start | bytes 405512 | tf_op jit(solution)/shard_map/ppermute | solution.py:178
  20.3 7.8 %collective-permute-start.6 = (f32[264,128]{1,0:T(8,128)S(1)}, f32[264,128]{1,0:T(8,128)S(1)}, u32[]{:S(2)}, u32[]{:S(2)}) collective-permute-start(f32[264,128]{1,0:T(8,128)S(1)} %add.517), channel_id=1, source_target_pairs={{0,8},{1,5},{4,12},{5,1},{8,0},{9,13},{12,4},{13,9},{2,10},{3,7},{... | collective-permute-start | bytes 405512 | tf_op jit(solution)/shard_map/ppermute | solution.py:178
  22.2 0.9 %copy-start.1 = (f32[264,128]{1,0:T(8,128)S(1)}, f32[264,128]{1,0:T(8,128)}, u32[]{:S(2)}) copy-start(f32[264,128]{1,0:T(8,128)} %get-tuple-element.14.left_ref) | copy-start | bytes 405508
  24.8 0.9 %copy-start = (f32[264,128]{1,0:T(8,128)S(1)}, f32[264,128]{1,0:T(8,128)}, u32[]{:S(2)}) copy-start(f32[264,128]{1,0:T(8,128)} %get-tuple-element.20.left_ref) | copy-start | bytes 405508
  25.8 5.9 %collective-permute-start.3 = (f32[264,128]{1,0:T(8,128)S(1)}, f32[264,128]{1,0:T(8,128)S(1)}, u32[]{:S(2)}, u32[]{:S(2)}) collective-permute-start(f32[264,128]{1,0:T(8,128)S(1)} %join.2.rest_0_.rest_4_), channel_id=1, source_target_pairs={{0,2},{2,0},{1,3},{3,1},{4,6},{6,4},{5,7},{7,5},{8,10},{10,8},{9,1... | collective-permute-start | bytes 405512 | tf_op jit(solution)/shard_map/ppermute | solution.py:422
  28.2 5.1 %collective-permute-start.7 = (f32[264,128]{1,0:T(8,128)S(1)}, f32[264,128]{1,0:T(8,128)S(1)}, u32[]{:S(2)}, u32[]{:S(2)}) collective-permute-start(f32[264,128]{1,0:T(8,128)S(1)} %join.3.rest_1_.rest_5_), channel_id=1, source_target_pairs={{0,2},{2,0},{1,3},{3,1},{4,6},{6,4},{5,7},{7,5},{8,10},{10,8},{9,1... | collective-permute-start | bytes 405512 | tf_op jit(solution)/shard_map/ppermute | solution.py:422
  33.4 12.2 %collective-permute-start.8 = (f32[12,64,128]{2,1,0:T(8,128)S(1)}, f32[12,64,128]{2,1,0:T(8,128)S(1)}, u32[]{:S(2)}, u32[]{:S(2)}) collective-permute-start(f32[12,64,128]{2,1,0:T(8,128)S(1)} %get-tuple-element.65), channel_id=1, source_target_pairs={{1,5},{4,0},{5,9},{8,4},{9,13},{12,8},{3,7},{6,2},{7,11},{10,6},{1... | collective-permute-start | bytes 1179656 | tf_op jit(solution)/shard_map/ppermute | solution.py:395
  34.7 10.9 %collective-permute-start.9 = (f32[12,64,128]{2,1,0:T(8,128)S(1)}, f32[12,64,128]{2,1,0:T(8,128)S(1)}, u32[]{:S(2)}, u32[]{:S(2)}) collective-permute-start(f32[12,64,128]{2,1,0:T(8,128)S(1)} %get-tuple-element.64), channel_id=1, source_target_pairs={{0,4},{4,8},{5,1},{8,12},{9,5},{13,9},{2,6},{6,10},{7,3},{10,14},{... | collective-permute-start | bytes 1179656 | tf_op jit(solution)/shard_map/ppermute | solution.py:394
  45.8 2.6 %collective-permute-start.10 = (f32[40,8,128]{2,1,0:T(8,128)S(1)}, f32[40,8,128]{2,1,0:T(8,128)S(1)}, u32[]{:S(2)}, u32[]{:S(2)}) collective-permute-start(f32[40,8,128]{2,1,0:T(8,128)S(1)} %dynamic-slice_dynamic-update-slice_fusion.2), channel_id=1, source_target_pairs={{0,1},{1,0},{2,3},{3,2},{4,5},{5,4},{6,7},{7,6},{8,9},{9,8},{10,11... | collective-permute-start | bytes 491528 | tf_op jit(solution)/shard_map/ppermute | solution.py:405
  50.9 8.4 %collective-permute-start.11 = (f32[8,64,128]{2,1,0:T(8,128)S(1)}, f32[8,64,128]{2,1,0:T(8,128)S(1)}, u32[]{:S(2)}, u32[]{:S(2)}) collective-permute-start(f32[8,64,128]{2,1,0:T(8,128)S(1)} %get-tuple-element.24.rest_4_), channel_id=1, source_target_pairs={{1,5},{4,0},{5,9},{8,4},{9,13},{12,8},{3,7},{6,2},{7,11},{10,6},{1... | collective-permute-start | bytes 786440 | tf_op jit(solution)/shard_map/ppermute | solution.py:395
  52.2 8.6 %collective-permute-start.12 = (f32[8,64,128]{2,1,0:T(8,128)S(1)}, f32[8,64,128]{2,1,0:T(8,128)S(1)}, u32[]{:S(2)}, u32[]{:S(2)}) collective-permute-start(f32[8,64,128]{2,1,0:T(8,128)S(1)} %get-tuple-element.24.rest_4_), channel_id=1, source_target_pairs={{0,4},{4,8},{5,1},{8,12},{9,5},{13,9},{2,6},{6,10},{7,3},{10,14},{... | collective-permute-start | bytes 786440 | tf_op jit(solution)/shard_map/ppermute | solution.py:394
  60.9 2.2 %collective-permute-start.13 = (f32[24,8,128]{2,1,0:T(8,128)S(1)}, f32[24,8,128]{2,1,0:T(8,128)S(1)}, u32[]{:S(2)}, u32[]{:S(2)}) collective-permute-start(f32[24,8,128]{2,1,0:T(8,128)S(1)} %pad_maximum_fusion.4), channel_id=1, source_target_pairs={{0,1},{1,0},{2,3},{3,2},{4,5},{5,4},{6,7},{7,6},{8,9},{9,8},{10,11... | collective-permute-start | bytes 294920 | tf_op jit(solution)/shard_map/ppermute | solution.py:405

commit v5 on v4

--- a/solution.py
+++ b/solution.py
@@ -58,6 +58,14 @@
     sums_ref[...] = jnp.zeros(sums_ref.shape, F32)
     for copy in smalls:
         copy.wait()
+    quarter = slabs // 4
+
+    def section_row(half, slab):
+        if not quarter:
+            return (half * slabs + slab) * section
+        ahead = jnp.where(slab < 3 * quarter, half * 3 * quarter, 3 * quarter + half * quarter)
+        return (ahead + slab) * section
+
     place = lax.axis_index("gz").astype(jnp.int32)
     odd = lax.axis_index("gy") % 2 == 1
     base_level = level[0].astype(F32)
@@ -74,7 +82,7 @@
             upper = camera[block, plane + 1] - base_level
             lands = at + plane
             half = lands // HALF
-            start = (half * slabs + slab) * section
+            start = section_row(half, slab)
             here = pl.ds(pl.multiple_of(start + (lands - half * HALF) * rows, SUB), rows)
             sums_ref[here, :] += lower_share * lower + upper_share * upper
             counts = pl.ds(pl.multiple_of(start + HALF * rows, SUB), SUB)
@@ -94,12 +102,12 @@
 def deposit(camera, target, first, level, fraction, slabs, shares):
     blocks, planes, rows, cols = camera.shape
     section = HALF * rows + SUB
-    chunk = SUB if blocks % SUB == 0 else blocks
+    chunk = HALF if blocks % HALF == 0 else blocks
     return pl.pallas_call(
         functools.partial(deposit_kernel, slabs=slabs, section=section, chunk=chunk),
         in_specs=[HBM] * 5,
-        out_specs=[VMEM] * (2 * len(shares)),
-        out_shape=[jax.ShapeDtypeStruct((share * section, cols), F32) for share in shares * 2],
+        out_specs=[VMEM] * len(shares),
+        out_shape=[jax.ShapeDtypeStruct((share * section, cols), F32) for share in shares],
         scratch_shapes=[
             pltpu.VMEM((2 * slabs * section, cols), F32),
             pltpu.SMEM(target.shape, jnp.int32),
@@ -128,8 +136,8 @@
 
 def first_shares(slabs):
     if slabs <= 2:
-        return [1] * slabs
-    return [slabs // 4] * 4
+        return [1] * (2 * slabs)
+    return [slabs // 4] * 6 + [slabs // 2]
 
 
 def fetch_kernel(*refs):
@@ -168,34 +176,43 @@
     )(left, right)
 
 
-def butterfly(halves, slabs, section):
+def butterfly(shares, slabs, section):
     if slabs == 1:
-        return [(shares[0], jnp.zeros_like(shares[0])) for shares in halves]
+        return [(share,) for share in shares]
+    if slabs == 2:
+        halves = [shares[:2], shares[2:]]
+    else:
+        halves, onward = [shares[:3], shares[3:6]], shares[6]
     for step in range(bit_count(slabs)):
         pairs = gz_pairs(lambda place, odd: place ^ (1 << step_bits(slabs, odd)[step]))
 
         def exchange(array):
             return lax.ppermute(array, ("gz", "gy"), pairs)
 
-        if len(halves[0]) == 2:
-            return [(shares[0], exchange(shares[1])) for shares in halves]
+        if step == bit_count(slabs) - 1:
+            return [(*keeps, exchange(send)) for *keeps, send in halves]
         if step == 0:
-            fetched = fetch(*(shares[1] for shares in halves))
-            halves = [[shares[0], array, *shares[2:]] for shares, array in zip(halves, fetched)]
-        onward = [exchange(shares[3]) for shares in halves]
-        stays = [exchange(shares[2]) for shares in halves]
-        sends = [add(shares[1], array) for shares, array in zip(halves, onward)]
-        keeps = [add(shares[0], array) for shares, array in zip(halves, stays)]
-        half = keeps[0].shape[0] // 2
-        if keeps[0].shape[0] == section:
-            halves = [list(pair) for pair in zip(keeps, sends)]
+            fetched = fetch(*(half[1] for half in halves), *(half[0] for half in halves))
+            halves = [[fetched[2 + i], fetched[i], half[2]] for i, half in enumerate(halves)]
+        onward = exchange(onward)
+        stays = [exchange(half[2]) for half in halves]
+        cut = onward.shape[0] // 2
+        sends = [add(half[1], array) for half, array in zip(halves, (onward[:cut], onward[cut:]))]
+        if stays[0].shape[0] == section:
+            halves = [(half[0], array, send) for half, array, send in zip(halves, stays, sends)]
         else:
-            halves = [[keep[:half], keep[half:], send[:half], send[half:]] for keep, send in zip(keeps, sends)]
-
-
-def join_kernel(small_ref, kept_ref, arrived_ref, message_ref, *, rows):
-    cols = kept_ref.shape[1]
-    total = kept_ref[...] + arrived_ref[...]
+            keeps = [add(half[0], array) for half, array in zip(halves, stays)]
+            cut //= 2
+            halves = [(keep[:cut], keep[cut:], send[:cut]) for keep, send in zip(keeps, sends)]
+            onward = jnp.concatenate([send[cut:] for send in sends])
+
+
+def join_kernel(small_ref, *rest, rows):
+    *term_refs, message_ref = rest
+    cols = message_ref.shape[1]
+    total = term_refs[0][...]
+    for term_ref in term_refs[1:]:
+        total = total + term_ref[...]
     planes = total[: HALF * rows].reshape(HALF, rows, cols)
     counts = total[HALF * rows :]
     fy, fx = small_ref[3:4], small_ref[4:5]
@@ -212,15 +229,15 @@
     message_ref[HALF * rows :] = small_ref[...]
 
 
-def join(small, kept, arrived, rows):
+def join(small, terms, rows):
     return pl.pallas_call(
         functools.partial(join_kernel, rows=rows),
-        in_specs=[VMEM] * 3,
+        in_specs=[VMEM] * (1 + len(terms)),
         out_specs=VMEM,
-        out_shape=jax.ShapeDtypeStruct(kept.shape, F32),
+        out_shape=jax.ShapeDtypeStruct(terms[0].shape, F32),
         compiler_params=pltpu.CompilerParams(vmem_limit_bytes=VMEM_BYTES),
         name="join",
-    )(small, kept, arrived)
+    )(small, *terms)
 
 
 def taps_sum(values, weights):
@@ -444,10 +461,9 @@
             jnp.zeros((SUB - 5, cols), F32),
         ]
     )
-    per = len(shares) // 2
     own, messages = [], []
-    for kept, arrived in butterfly([shares[:per], shares[per:]], slabs, section):
-        own.append(join(small, kept, arrived, rows))
+    for terms in butterfly(shares, slabs, section):
+        own.append(join(small, terms, rows))
         messages.append(from_views(own[-1]))
     halves = [messages[half][view] for view in range(views) for half in range(2)]
     low_half, high_half = (

time: 66.3 us -> 65.9 us (level)
  starting transfers between devices: 28.6 us -> 26.8 us
  waiting for transfers between devices: 19.3 us -> 20.4 us
    ppermute x2, waiting for transfers between devices: 3.05 us -> 4.97 us  [from_views(): return [message, lax.ppermute(message, 'view', [(0, 1), (1, 0)])]]
    ppermute x6 -> x5, starting transfers between devices: 10 us -> 8.69 us  [exchange(): return lax.ppermute(array, ('gz', 'gy'), pairs)]
    ppermute x2, starting transfers between devices: 3.93 us -> 3.11 us  [from_views(): return [message, lax.ppermute(message, 'view', [(0, 1), (1, 0)])]]
    ppermute x6 -> x5, waiting for transfers between devices: 6.82 us -> 6.16 us  [exchange(): return lax.ppermute(array, ('gz', 'gy'), pairs)]
  transfers between devices with their start and end apart: 14 -> 13, of which waited for: 10 -> 11; matrix products, arithmetic and copies ran while one was open for 5% -> 5% of each run, Pallas kernels for 1% -> 1%
where the time goes in v5:
time: 65.9 us; the launch traced here: 65.6 us
  starting transfers between devices  26.8 us (41%)
  waiting for transfers between devices  20.4 us (31%)
  Pallas kernels  9.37 us (14%)
  local copies, waits for them, and re-layouts  5.59 us (8%)
  other arithmetic  1.75 us (3%)
  between operations  1.7 us (3%)
    ppermute x2, starting transfers between devices, from_slabs_beside(): lax.ppermute(sends[0], ('gz', 'gy'), gz_pairs(lambda place, odd: place -...  9.26 us
    ppermute x5, starting transfers between devices, exchange(): return lax.ppermute(array, ('gz', 'gy'), pairs)  8.69 us
    ppermute x5, waiting for transfers between devices, exchange(): return lax.ppermute(array, ('gz', 'gy'), pairs)  6.16 us
    ppermute x2, waiting for transfers between devices, from_slabs_beside(): lax.ppermute(sends[1], ('gz', 'gy'), gz_pairs(lambda place, odd: place +...  5.63 us
    pallas_call x2, Pallas kernels, update(): pl.pallas_call(functools.partial(update_kernel, views=views, margin=margi...  5.4 us
    ppermute x2, waiting for transfers between devices, from_views(): return [message, lax.ppermute(message, 'view', [(0, 1), (1, 0)])]  4.97 us
    unnamed x18, local copies, waits for them, and re-layouts  3.7 us
    ppermute x2, starting transfers between devices, edge_rows(): arrived = lax.ppermute(jnp.concatenate(parts), 'gy', [(0, 1), (1, 0)])  3.16 us
  transfers between devices with their start and end apart: 13, of which 11 were waited for; matrix products, arithmetic and copies ran while one was open for 5% of the time, Pallas kernels for 1%

profile of v5, /device:TPU:0, one launch (start us, length us, event | category | flops | bytes accessed | tf_op | source)
XLA Modules:
  0.0 65.6 jit_solution(12025514485085515932)
XLA Ops:
  1.3 3.0 %deposit.1 = (f32[264,128]{1,0:T(8,128)}, f32[264,128]{1,0:T(8,128)}, f32[264,128]{1,0:T(8,128)}, f32[264,128]{1,0:T(8,128)}, f32[264,128]{1,0:T(8,128)}, /*index=5*/f32[264,128]{1,0:T(8,128)}, f32[528,128]{1,0:T(8,128)}) custom-call(s32[32]{0:T(128)} %bitcast.50, s32[32]{0:T(128)} %bitcast.51, s32[1]{0:T(128)} %bitcast.31.level_hbm, f32[3]{0:T(128)} %bitcast.52, ...), custom_call_target="tpu_custom_call" | custom-call | tf_op jit(solution)/shard_map/deposit/pallas_call | solution.py:106
  4.3 3.1 %collective-permute-start.1 = (f32[528,128]{1,0:T(8,128)}, f32[528,128]{1,0:T(8,128)S(1)}, u32[]{:S(2)}, u32[]{:S(2)}) collective-permute-start(f32[528,128]{1,0:T(8,128)} %get-tuple-element.22), channel_id=1, source_target_pairs={{0,4},{1,9},{4,0},{5,13},{8,12},{9,1},{12,8},{13,5},{2,6},{3,11},{... | collective-permute-start | bytes 811016 | tf_op jit(solution)/shard_map/ppermute | solution.py:190
  7.5 1.9 %collective-permute-start.4 = (f32[264,128]{1,0:T(8,128)}, f32[264,128]{1,0:T(8,128)S(1)}, u32[]{:S(2)}, u32[]{:S(2)}) collective-permute-start(f32[264,128]{1,0:T(8,128)} %get-tuple-element.24), channel_id=1, source_target_pairs={{0,4},{1,9},{4,0},{5,13},{8,12},{9,1},{12,8},{13,5},{2,6},{3,11},{... | collective-permute-start | bytes 405512 | tf_op jit(solution)/shard_map/ppermute | solution.py:190
  10.0 0.9 %copy-done = f32[264,128]{1,0:T(8,128)S(1)} copy-done((f32[264,128]{1,0:T(8,128)S(1)}, f32[264,128]{1,0:T(8,128)}, u32[]{:S(2)}) %copy-start) | copy-done | bytes 135192
  10.9 0.9 %copy-done.1 = f32[264,128]{1,0:T(8,128)S(1)} copy-done((f32[264,128]{1,0:T(8,128)S(1)}, f32[264,128]{1,0:T(8,128)}, u32[]{:S(2)}) %copy-start.1) | copy-done | bytes 135192
  11.8 0.9 %copy-done.2 = f32[264,128]{1,0:T(8,128)S(1)} copy-done((f32[264,128]{1,0:T(8,128)S(1)}, f32[264,128]{1,0:T(8,128)}, u32[]{:S(2)}) %copy-start.2) | copy-done | bytes 135192
  12.7 0.9 %copy-done.3 = f32[264,128]{1,0:T(8,128)S(1)} copy-done((f32[264,128]{1,0:T(8,128)S(1)}, f32[264,128]{1,0:T(8,128)}, u32[]{:S(2)}) %copy-start.3) | copy-done | bytes 135192
  13.6 0.7 %fetch.1 = (f32[264,128]{1,0:T(8,128)S(1)}, f32[264,128]{1,0:T(8,128)S(1)}, f32[264,128]{1,0:T(8,128)S(1)}, f32[264,128]{1,0:T(8,128)S(1)}) custom-call(f32[264,128]{1,0:T(8,128)S(1)} %copy-done.1, f32[264,128]{1,0:T(8,128)S(1)} %copy-done.3, f32[264,128]{1,0:T(8,128)S(1)} %copy-done, f32[264,128]{1,0:T(8,128)S(1)} %copy-done.2), custom_call_target="tpu_custom_call" | custom-call | tf_op jit(solution)/shard_map/fetch/pallas_call | solution.py:153
  14.7 3.5 %collective-permute-start.2 = (f32[264,128]{1,0:T(8,128)S(1)}, f32[264,128]{1,0:T(8,128)S(1)}, u32[]{:S(2)}, u32[]{:S(2)}) collective-permute-start(f32[264,128]{1,0:T(8,128)S(1)} %add.512), channel_id=1, source_target_pairs={{0,8},{1,5},{4,12},{5,1},{8,0},{9,13},{12,4},{13,9},{2,10},{3,7},{... | collective-permute-start | bytes 405512 | tf_op jit(solution)/shard_map/ppermute | solution.py:190
  18.4 4.8 %collective-permute-done.2.rest_2_ = f32[264,128]{1,0:T(8,128)S(1)} collective-permute-done((f32[264,128]{1,0:T(8,128)S(1)}, f32[264,128]{1,0:T(8,128)S(1)}, u32[]{:S(2)}, u32[]{:S(2)}) %collective-permute-start.2) | collective-permute-done | bytes 135200 | tf_op jit(solution)/shard_map/ppermute | solution.py:190
  23.3 1.6 %collective-permute-start.3 = (f32[264,128]{1,0:T(8,128)S(1)}, f32[264,128]{1,0:T(8,128)S(1)}, u32[]{:S(2)}, u32[]{:S(2)}) collective-permute-start(f32[264,128]{1,0:T(8,128)S(1)} %join.2.rest_0_.rest_4_), channel_id=1, source_target_pairs={{0,2},{2,0},{1,3},{3,1},{4,6},{6,4},{5,7},{7,5},{8,10},{10,8},{9,1... | collective-permute-start | bytes 405512 | tf_op jit(solution)/shard_map/ppermute | solution.py:439
  24.9 1.1 %collective-permute-done.5.rest_2_ = f32[264,128]{1,0:T(8,128)S(1)} collective-permute-done((f32[264,128]{1,0:T(8,128)S(1)}, f32[264,128]{1,0:T(8,128)S(1)}, u32[]{:S(2)}, u32[]{:S(2)}) %collective-permute-start.5) | collective-permute-done | bytes 135200 | tf_op jit(solution)/shard_map/ppermute | solution.py:190
  26.1 1.6 %collective-permute-start.6 = (f32[264,128]{1,0:T(8,128)S(1)}, f32[264,128]{1,0:T(8,128)S(1)}, u32[]{:S(2)}, u32[]{:S(2)}) collective-permute-start(f32[264,128]{1,0:T(8,128)S(1)} %join.3.rest_1_.rest_5_), channel_id=1, source_target_pairs={{0,2},{2,0},{1,3},{3,1},{4,6},{6,4},{5,7},{7,5},{8,10},{10,8},{9,1... | collective-permute-start | bytes 405512 | tf_op jit(solution)/shard_map/ppermute | solution.py:439
  27.7 1.2 %collective-permute-done.3.rest_2_ = f32[264,128]{1,0:T(8,128)S(1)} collective-permute-done((f32[264,128]{1,0:T(8,128)S(1)}, f32[264,128]{1,0:T(8,128)S(1)}, u32[]{:S(2)}, u32[]{:S(2)}) %collective-permute-start.3) | collective-permute-done | bytes 135200 | tf_op jit(solution)/shard_map/ppermute | solution.py:439
  28.9 3.8 %collective-permute-done.6.rest_3_ = f32[264,128]{1,0:T(8,128)S(1)} collective-permute-done((f32[264,128]{1,0:T(8,128)S(1)}, f32[264,128]{1,0:T(8,128)S(1)}, u32[]{:S(2)}, u32[]{:S(2)}) %collective-permute-start.6) | collective-permute-done | bytes 135200 | tf_op jit(solution)/shard_map/ppermute | solution.py:439
  32.8 1.3 %collective-permute-start.7 = (f32[12,64,128]{2,1,0:T(8,128)S(1)}, f32[12,64,128]{2,1,0:T(8,128)S(1)}, u32[]{:S(2)}, u32[]{:S(2)}) collective-permute-start(f32[12,64,128]{2,1,0:T(8,128)S(1)} %get-tuple-element.67), channel_id=1, source_target_pairs={{1,5},{4,0},{5,9},{8,4},{9,13},{12,8},{3,7},{6,2},{7,11},{10,6},{1... | collective-permute-start | bytes 1179656 | tf_op jit(solution)/shard_map/ppermute | solution.py:412
  34.1 4.7 %collective-permute-start.8 = (f32[12,64,128]{2,1,0:T(8,128)S(1)}, f32[12,64,128]{2,1,0:T(8,128)S(1)}, u32[]{:S(2)}, u32[]{:S(2)}) collective-permute-start(f32[12,64,128]{2,1,0:T(8,128)S(1)} %get-tuple-element.66), channel_id=1, source_target_pairs={{0,4},{4,8},{5,1},{8,12},{9,5},{13,9},{2,6},{6,10},{7,3},{10,14},{... | collective-permute-start | bytes 1179656 | tf_op jit(solution)/shard_map/ppermute | solution.py:411
  39.0 0.3 slice_reduce_fusion.18
  39.4 0.3 slice_reduce_fusion.36
  39.7 0.3 slice_reduce_fusion.27
  40.7 0.3 slice_reduce_fusion.9
  41.4 3.3 %collective-permute-done.7 = f32[12,64,128]{2,1,0:T(8,128)S(1)} collective-permute-done((f32[12,64,128]{2,1,0:T(8,128)S(1)}, f32[12,64,128]{2,1,0:T(8,128)S(1)}, u32[]{:S(2)}, u32[]{:S(2)}) %collective-permute-start.7) | collective-permute-done | bytes 393248 | tf_op jit(solution)/shard_map/ppermute | solution.py:412
  44.9 1.9 %collective-permute-start.9 = (f32[40,8,128]{2,1,0:T(8,128)S(1)}, f32[40,8,128]{2,1,0:T(8,128)S(1)}, u32[]{:S(2)}, u32[]{:S(2)}) collective-permute-start(f32[40,8,128]{2,1,0:T(8,128)S(1)} %dynamic-slice_dynamic-update-slice_fusion.2), channel_id=1, source_target_pairs={{0,1},{1,0},{2,3},{3,2},{4,5},{5,4},{6,7},{7,6},{8,9},{9,8},{10,11... | collective-permute-start | bytes 491528 | tf_op jit(solution)/shard_map/ppermute | solution.py:422
  47.0 0.9 %collective-permute-done.9.low_rows_ref.high_rows_ref = f32[40,8,128]{2,1,0:T(8,128)S(1)} collective-permute-done((f32[40,8,128]{2,1,0:T(8,128)S(1)}, f32[40,8,128]{2,1,0:T(8,128)S(1)}, u32[]{:S(2)}, u32[]{:S(2)}) %collective-permute-start.9) | collective-permute-done | bytes 163872 | tf_op jit(solution)/shard_map/ppermute | solution.py:422
  48.0 2.4 %update.2 = (f32[8,64,128]{2,1,0:T(8,128)S(1)}, f32[512,128]{1,0:T(8,128)}) custom-call(f32[20,8,128]{2,1,0:T(8,128)S(1)} %broadcast_in_dim.439.weight_ref, bf16[2,2,80,240]{3,2,1,0:T(8,128)(2,1)S(1)} %pad_maximum_fusion.3.row_band_ref, bf16[2,2,256,256]{3,2,1,0:T(8,128)(2,1)S(1)} %maximum_maximum_fusion.col_band_ref, ...), custom_call_target="tpu_custom_call" | custom-call | tf_op jit(solution)/shard_map/update/pallas_call | solution.py:387
  50.4 1.3 %collective-permute-start.10 = (f32[8,64,128]{2,1,0:T(8,128)S(1)}, f32[8,64,128]{2,1,0:T(8,128)S(1)}, u32[]{:S(2)}, u32[]{:S(2)}) collective-permute-start(f32[8,64,128]{2,1,0:T(8,128)S(1)} %get-tuple-element.26.rest_4_), channel_id=1, source_target_pairs={{1,5},{4,0},{5,9},{8,4},{9,13},{12,8},{3,7},{6,2},{7,11},{10,6},{1... | collective-permute-start | bytes 786440 | tf_op jit(solution)/shard_map/ppermute | solution.py:412
  51.7 4.6 %collective-permute-start.11 = (f32[8,64,128]{2,1,0:T(8,128)S(1)}, f32[8,64,128]{2,1,0:T(8,128)S(1)}, u32[]{:S(2)}, u32[]{:S(2)}) collective-permute-start(f32[8,64,128]{2,1,0:T(8,128)S(1)} %get-tuple-element.26.rest_4_), channel_id=1, source_target_pairs={{0,4},{4,8},{5,1},{8,12},{9,5},{13,9},{2,6},{6,10},{7,3},{10,14},{... | collective-permute-start | bytes 786440 | tf_op jit(solution)/shard_map/ppermute | solution.py:411
  56.3 2.4 %collective-permute-done.10 = f32[8,64,128]{2,1,0:T(8,128)S(1)} collective-permute-done((f32[8,64,128]{2,1,0:T(8,128)S(1)}, f32[8,64,128]{2,1,0:T(8,128)S(1)}, u32[]{:S(2)}, u32[]{:S(2)}) %collective-permute-start.10) | collective-permute-done | bytes 262176 | tf_op jit(solution)/shard_map/ppermute | solution.py:412
  58.6 1.7 %collective-permute-done.11 = f32[8,64,128]{2,1,0:T(8,128)S(1)} collective-permute-done((f32[8,64,128]{2,1,0:T(8,128)S(1)}, f32[8,64,128]{2,1,0:T(8,128)S(1)}, u32[]{:S(2)}, u32[]{:S(2)}) %collective-permute-start.11) | collective-permute-done | bytes 262176 | tf_op jit(solution)/shard_map/ppermute | solution.py:411
  60.5 1.2 %collective-permute-start.12 = (f32[24,8,128]{2,1,0:T(8,128)S(1)}, f32[24,8,128]{2,1,0:T(8,128)S(1)}, u32[]{:S(2)}, u32[]{:S(2)}) collective-permute-start(f32[24,8,128]{2,1,0:T(8,128)S(1)} %pad_maximum_fusion.4), channel_id=1, source_target_pairs={{0,1},{1,0},{2,3},{3,2},{4,5},{5,4},{6,7},{7,6},{8,9},{9,8},{10,11... | collective-permute-start | bytes 294920 | tf_op jit(solution)/shard_map/ppermute | solution.py:422
  61.7 0.9 %collective-permute-done.12.rest_7_.rest_8_ = f32[24,8,128]{2,1,0:T(8,128)S(1)} collective-permute-done((f32[24,8,128]{2,1,0:T(8,128)S(1)}, f32[24,8,128]{2,1,0:T(8,128)S(1)}, u32[]{:S(2)}, u32[]{:S(2)}) %collective-permute-start.12) | collective-permute-done | bytes 98336 | tf_op jit(solution)/shard_map/ppermute | solution.py:422
  62.6 3.0 %update.3 = f32[8,64,128]{2,1,0:T(8,128)} custom-call(f32[20,8,128]{2,1,0:T(8,128)S(1)} %broadcast_in_dim.439.weight_ref, bf16[2,2,80,240]{3,2,1,0:T(8,128)(2,1)S(1)} %pad_maximum_fusion.3.row_band_ref, bf16[2,2,256,256]{3,2,1,0:T(8,128)(2,1)S(1)} %maximum_maximum_fusion.col_band_ref, f32[12,64,128]{2,1,0:T(8,128)S(1)} %get-tuple-element.65.below_ref, ...), custom_call_target="tpu_custom_call" | custom-call | tf_op jit(solution)/shard_map/update/pallas_call | solution.py:387
  (72 shorter events, 3.3 us)
Async XLA Ops:
  0.6 8.8 %copy-start.5 = (f32[1,3]{1,0:T(1,128)S(1)}, f32[1,3]{1,0:T(1,128)}, u32[]{:S(2)}) copy-start(f32[1,3]{1,0:T(1,128)} %param.10) | copy-start | bytes 40
  0.6 9.1 %copy-start.4 = (f32[1,3,9]{2,0,1:T(1,128)S(1)}, f32[1,3,9]{2,0,1:T(1,128)}, u32[]{:S(2)}) copy-start(f32[1,3,9]{2,0,1:T(1,128)} %param.11) | copy-start | bytes 328
  4.3 10.3 %collective-permute-start.1 = (f32[528,128]{1,0:T(8,128)}, f32[528,128]{1,0:T(8,128)S(1)}, u32[]{:S(2)}, u32[]{:S(2)}) collective-permute-start(f32[528,128]{1,0:T(8,128)} %get-tuple-element.22), channel_id=1, source_target_pairs={{0,4},{1,9},{4,0},{5,13},{8,12},{9,1},{12,8},{13,5},{2,6},{3,11},{... | collective-permute-start | bytes 811016 | tf_op jit(solution)/shard_map/ppermute | solution.py:190
  7.4 10.9 %collective-permute-start = (f32[264,128]{1,0:T(8,128)}, f32[264,128]{1,0:T(8,128)S(1)}, u32[]{:S(2)}, u32[]{:S(2)}) collective-permute-start(f32[264,128]{1,0:T(8,128)} %get-tuple-element.20), channel_id=1, source_target_pairs={{0,4},{1,9},{4,0},{5,13},{8,12},{9,1},{12,8},{13,5},{2,6},{3,11},{... | collective-permute-start | bytes 405512 | tf_op jit(solution)/shard_map/ppermute | solution.py:190
  7.5 17.4 %collective-permute-start.4 = (f32[264,128]{1,0:T(8,128)}, f32[264,128]{1,0:T(8,128)S(1)}, u32[]{:S(2)}, u32[]{:S(2)}) collective-permute-start(f32[264,128]{1,0:T(8,128)} %get-tuple-element.24), channel_id=1, source_target_pairs={{0,4},{1,9},{4,0},{5,13},{8,12},{9,1},{12,8},{13,5},{2,6},{3,11},{... | collective-permute-start | bytes 405512 | tf_op jit(solution)/shard_map/ppermute | solution.py:190
  9.9 0.9 %copy-start = (f32[264,128]{1,0:T(8,128)S(1)}, f32[264,128]{1,0:T(8,128)}, u32[]{:S(2)}) copy-start(f32[264,128]{1,0:T(8,128)} %get-tuple-element.17.refs_2_) | copy-start | bytes 405508
  10.9 0.9 %copy-start.1 = (f32[264,128]{1,0:T(8,128)S(1)}, f32[264,128]{1,0:T(8,128)}, u32[]{:S(2)}) copy-start(f32[264,128]{1,0:T(8,128)} %get-tuple-element.15.refs_0_) | copy-start | bytes 405508
  11.8 0.9 %copy-start.2 = (f32[264,128]{1,0:T(8,128)S(1)}, f32[264,128]{1,0:T(8,128)}, u32[]{:S(2)}) copy-start(f32[264,128]{1,0:T(8,128)} %get-tuple-element.18.refs_3_) | copy-start | bytes 405508
  12.7 0.9 %copy-start.3 = (f32[264,128]{1,0:T(8,128)S(1)}, f32[264,128]{1,0:T(8,128)}, u32[]{:S(2)}) copy-start(f32[264,128]{1,0:T(8,128)} %get-tuple-element.16.refs_1_) | copy-start | bytes 405508
  14.7 8.5 %collective-permute-start.2 = (f32[264,128]{1,0:T(8,128)S(1)}, f32[264,128]{1,0:T(8,128)S(1)}, u32[]{:S(2)}, u32[]{:S(2)}) collective-permute-start(f32[264,128]{1,0:T(8,128)S(1)} %add.512), channel_id=1, source_target_pairs={{0,8},{1,5},{4,12},{5,1},{8,0},{9,13},{12,4},{13,9},{2,10},{3,7},{... | collective-permute-start | bytes 405512 | tf_op jit(solution)/shard_map/ppermute | solution.py:190
  18.2 7.8 %collective-permute-start.5 = (f32[264,128]{1,0:T(8,128)S(1)}, f32[264,128]{1,0:T(8,128)S(1)}, u32[]{:S(2)}, u32[]{:S(2)}) collective-permute-start(f32[264,128]{1,0:T(8,128)S(1)} %add.513), channel_id=1, source_target_pairs={{0,8},{1,5},{4,12},{5,1},{8,0},{9,13},{12,4},{13,9},{2,10},{3,7},{... | collective-permute-start | bytes 405512 | tf_op jit(solution)/shard_map/ppermute | solution.py:190
  23.3 5.6 %collective-permute-start.3 = (f32[264,128]{1,0:T(8,128)S(1)}, f32[264,128]{1,0:T(8,128)S(1)}, u32[]{:S(2)}, u32[]{:S(2)}) collective-permute-start(f32[264,128]{1,0:T(8,128)S(1)} %join.2.rest_0_.rest_4_), channel_id=1, source_target_pairs={{0,2},{2,0},{1,3},{3,1},{4,6},{6,4},{5,7},{7,5},{8,10},{10,8},{9,1... | collective-permute-start | bytes 405512 | tf_op jit(solution)/shard_map/ppermute | solution.py:439
  26.1 6.6 %collective-permute-start.6 = (f32[264,128]{1,0:T(8,128)S(1)}, f32[264,128]{1,0:T(8,128)S(1)}, u32[]{:S(2)}, u32[]{:S(2)}) collective-permute-start(f32[264,128]{1,0:T(8,128)S(1)} %join.3.rest_1_.rest_5_), channel_id=1, source_target_pairs={{0,2},{2,0},{1,3},{3,1},{4,6},{6,4},{5,7},{7,5},{8,10},{10,8},{9,1... | collective-permute-start | bytes 405512 | tf_op jit(solution)/shard_map/ppermute | solution.py:439
  32.8 11.9 %collective-permute-start.7 = (f32[12,64,128]{2,1,0:T(8,128)S(1)}, f32[12,64,128]{2,1,0:T(8,128)S(1)}, u32[]{:S(2)}, u32[]{:S(2)}) collective-permute-start(f32[12,64,128]{2,1,0:T(8,128)S(1)} %get-tuple-element.67), channel_id=1, source_target_pairs={{1,5},{4,0},{5,9},{8,4},{9,13},{12,8},{3,7},{6,2},{7,11},{10,6},{1... | collective-permute-start | bytes 1179656 | tf_op jit(solution)/shard_map/ppermute | solution.py:412
  34.1 10.6 %collective-permute-start.8 = (f32[12,64,128]{2,1,0:T(8,128)S(1)}, f32[12,64,128]{2,1,0:T(8,128)S(1)}, u32[]{:S(2)}, u32[]{:S(2)}) collective-permute-start(f32[12,64,128]{2,1,0:T(8,128)S(1)} %get-tuple-element.66), channel_id=1, source_target_pairs={{0,4},{4,8},{5,1},{8,12},{9,5},{13,9},{2,6},{6,10},{7,3},{10,14},{... | collective-permute-start | bytes 1179656 | tf_op jit(solution)/shard_map/ppermute | solution.py:411
  44.9 3.0 %collective-permute-start.9 = (f32[40,8,128]{2,1,0:T(8,128)S(1)}, f32[40,8,128]{2,1,0:T(8,128)S(1)}, u32[]{:S(2)}, u32[]{:S(2)}) collective-permute-start(f32[40,8,128]{2,1,0:T(8,128)S(1)} %dynamic-slice_dynamic-update-slice_fusion.2), channel_id=1, source_target_pairs={{0,1},{1,0},{2,3},{3,2},{4,5},{5,4},{6,7},{7,6},{8,9},{9,8},{10,11... | collective-permute-start | bytes 491528 | tf_op jit(solution)/shard_map/ppermute | solution.py:422
  50.4 8.3 %collective-permute-start.10 = (f32[8,64,128]{2,1,0:T(8,128)S(1)}, f32[8,64,128]{2,1,0:T(8,128)S(1)}, u32[]{:S(2)}, u32[]{:S(2)}) collective-permute-start(f32[8,64,128]{2,1,0:T(8,128)S(1)} %get-tuple-element.26.rest_4_), channel_id=1, source_target_pairs={{1,5},{4,0},{5,9},{8,4},{9,13},{12,8},{3,7},{6,2},{7,11},{10,6},{1... | collective-permute-start | bytes 786440 | tf_op jit(solution)/shard_map/ppermute | solution.py:412
  51.7 8.7 %collective-permute-start.11 = (f32[8,64,128]{2,1,0:T(8,128)S(1)}, f32[8,64,128]{2,1,0:T(8,128)S(1)}, u32[]{:S(2)}, u32[]{:S(2)}) collective-permute-start(f32[8,64,128]{2,1,0:T(8,128)S(1)} %get-tuple-element.26.rest_4_), channel_id=1, source_target_pairs={{0,4},{4,8},{5,1},{8,12},{9,5},{13,9},{2,6},{6,10},{7,3},{10,14},{... | collective-permute-start | bytes 786440 | tf_op jit(solution)/shard_map/ppermute | solution.py:411
  60.5 2.2 %collective-permute-start.12 = (f32[24,8,128]{2,1,0:T(8,128)S(1)}, f32[24,8,128]{2,1,0:T(8,128)S(1)}, u32[]{:S(2)}, u32[]{:S(2)}) collective-permute-start(f32[24,8,128]{2,1,0:T(8,128)S(1)} %pad_maximum_fusion.4), channel_id=1, source_target_pairs={{0,1},{1,0},{2,3},{3,2},{4,5},{5,4},{6,7},{7,6},{8,9},{9,8},{10,11... | collective-permute-start | bytes 294920 | tf_op jit(solution)/shard_map/ppermute | solution.py:422

commit v6 on v5

--- a/solution.py
+++ b/solution.py
@@ -271,10 +271,56 @@
     return results
 
 
+def prepare_kernel(weight_ref, *rest, views, margin, first):
+    *sources, out_ref = rest
+    _, mid_planes, rows, cols = out_ref.shape
+    planes = mid_planes - 2 * margin
+    taps = 2 * margin + 1
+    weights = [[weight_ref[view * taps + tap] for tap in range(taps)] for view in range(views)]
+
+    def one(tile, carry):
+        here = pl.ds(pl.multiple_of(tile * SUB, SUB), SUB)
+        values = []
+        for plane in range(planes):
+            if first:
+                start = plane % HALF * rows + tile * SUB
+                there = pl.ds(pl.multiple_of(start, SUB), SUB)
+                value = sources[plane // HALF][there, :]
+                for view in range(1, views):
+                    value = value + sources[2 * view + plane // HALF][there, :]
+                values.append(value / views)
+            else:
+                values.append(sources[0][plane, here, :])
+        for view in range(views):
+            for plane in range(mid_planes):
+                pairs = [(tap, plane + tap - 2 * margin) for tap in range(taps) if 0 <= plane + tap - 2 * margin < planes]
+                out_ref[view, plane, here, :] = taps_sum(
+                    [values[at] for _, at in pairs], [weights[view][tap] for tap, _ in pairs]
+                )
+        return carry
+
+    lax.fori_loop(0, rows // SUB, one, 0, unroll=2)
+
+
+def prepare(weights, sources, views, margin, rows):
+    first = len(sources) > 1
+    cols = weights.shape[-1]
+    return pl.pallas_call(
+        functools.partial(prepare_kernel, views=views, margin=margin, first=first),
+        in_specs=[VMEM] * (1 + len(sources)),
+        out_specs=VMEM,
+        out_shape=jax.ShapeDtypeStruct((views, CZ + 2 * margin, rows, cols), F32),
+        compiler_params=pltpu.CompilerParams(vmem_limit_bytes=VMEM_BYTES),
+        name="prepare",
+    )(weights, *sources)
+
+
 def update_kernel(
     weight_ref, row_band_ref, col_band_ref, below_ref, above_ref, low_rows_ref, high_rows_ref, *rest,
-    views, margin, first
+    views, margin, first, prepared
 ):
+    if prepared:
+        partial_ref, *rest = rest
     halves, rest = rest[: 2 * views], rest[2 * views :]
     if first:
         *own_refs, out_ref, copied_hbm, estimate, joined, first_pass, ratio, back_first, sems = rest
@@ -328,15 +374,32 @@
     mid_planes, mid_rows = planes + 2 * margin, rows + 2 * margin
     weights = [[weight_ref[view * taps + tap] for tap in range(taps)] for view in range(views)]
 
+    near = range(2 * margin, 2 * margin + planes) if prepared else ()
+
     def along_z(tile, carry):
-        here = pl.ds(pl.multiple_of(tile * SUB, SUB), SUB)
+        here = pl.ds(pl.multiple_of(wide + tile * SUB, SUB), SUB)
+        there = pl.ds(pl.multiple_of(tile * SUB, SUB), SUB)
+        values = [None if plane in near else estimate[plane, here, :] for plane in range(planes + 4 * margin)]
+        for view in range(views):
+            for plane in range(mid_planes):
+                if prepared:
+                    part = partial_ref[view, plane, there, :]
+                    for tap in range(taps):
+                        if plane + tap not in near:
+                            part = part + weights[view][tap] * values[plane + tap]
+                else:
+                    part = taps_sum(values[plane : plane + taps], weights[view])
+                first_pass[view, plane, here, :] = part
+        return carry
+
+    lax.fori_loop(0, rows // SUB, along_z, 0, unroll=2)
+
+    for start in [*range(0, wide, SUB), *range(wide + rows, 2 * wide + rows, SUB)]:
+        here = slice(start, start + SUB)
         values = [estimate[plane, here, :] for plane in range(planes + 4 * margin)]
         for view in range(views):
             for plane in range(mid_planes):
                 first_pass[view, plane, here, :] = taps_sum(values[plane : plane + taps], weights[view])
-        return carry
-
-    lax.fori_loop(0, (rows + 4 * margin) // SUB, along_z, 0, unroll=2)
 
     for view in range(views):
         blurred = rows_blurred([first_pass[view, plane] for plane in range(mid_planes)], row_band_ref[view, 0])
@@ -368,9 +431,9 @@
             copy.wait()
 
 
-def update(weights, bands, halves, below, above, low_rows, high_rows, own, later, margin):
+def update(weights, bands, partial, halves, below, above, low_rows, high_rows, own, later, margin):
     first = not later
-    arrays = [weights, *bands, below, above, low_rows, high_rows, *halves] + list(own if first else later)
+    arrays = [weights, *bands, below, above, low_rows, high_rows, *partial, *halves] + list(own if first else later)
     views = len(halves) // 2
     _, rows, cols = below.shape
     planes = CZ
@@ -385,7 +448,7 @@
     out_shape = jax.ShapeDtypeStruct((planes, rows, cols), F32)
     copy_shape = jax.ShapeDtypeStruct((planes * rows, cols), F32)
     return pl.pallas_call(
-        functools.partial(update_kernel, views=views, margin=margin, first=first),
+        functools.partial(update_kernel, views=views, margin=margin, first=first, prepared=bool(partial)),
         in_specs=[VMEM] * len(arrays),
         out_specs=[VMEM, HBM] if first else VMEM,
         out_shape=[out_shape, copy_shape] if first else out_shape,
@@ -403,6 +466,19 @@
 
 
 def from_slabs_beside(upward, downward):
+    turned = (lax.axis_index("gz") + lax.axis_index("gy")) % 2 == 1
+    if upward is downward:
+        sends = (upward, downward)
+    else:
+        sends = (jnp.where(turned, downward, upward), jnp.where(turned, upward, downward))
+    ahead = gz_pairs(lambda place, odd: place - 1 if (place + odd) % 2 else place + 1)
+    behind = gz_pairs(lambda place, odd: place + 1 if (place + odd) % 2 else place - 1)
+    first = lax.ppermute(sends[0], ("gz", "gy"), ahead)
+    second = lax.ppermute(sends[1], ("gz", "gy"), behind)
+    return jnp.where(turned, first, second), jnp.where(turned, second, first)
+
+
+def from_slabs_shifted(upward, downward):
     odd = lax.axis_index("gy") % 2 == 1
     if upward is downward:
         sends = (upward, downward)
@@ -471,7 +547,7 @@
     )
     upward = jnp.concatenate(high_half + [sum(low_half) / views])
     downward = jnp.concatenate(low_half + [sum(high_half) / views])
-    below, above = from_slabs_beside(upward, downward)
+    below, above = from_slabs_shifted(upward, downward)
     wide = 2 * margin
     pieces = [part for view in range(views) for part in (low_half[view], high_half[view])]
     low_rows, high_rows = edge_rows([below, above] + pieces, wide)
@@ -496,7 +572,8 @@
         if iteration:
             est_below, est_above = from_slabs_beside(estimate, estimate)
             later = (estimate, est_below, est_above) + edge_rows([est_below, estimate, est_above], wide)
-        result = update(weights, bands, halves, below, above, low_rows, high_rows, own, later, margin)
+        partial = [] if iteration else [prepare(weights, halves, views, margin, rows)]
+        result = update(weights, bands, partial, halves, below, above, low_rows, high_rows, own, later, margin)
         estimate = result if later else result[0]
         joined = joined if later else result[1]
     return (estimate, joined.reshape(1, CZ, rows, cols))

time: 65.9 us -> 65.2 us (0.989)
  starting transfers between devices: 26.8 us -> 26 us
    ppermute x4, starting transfers between devices: 11.8 us -> 10.6 us  [the longest x1 4.7 us: from_slabs_shifted(): lax.ppermute(sends[0], ('gz', 'gy'), gz_pairs(lambda place, odd: place -...]
  transfers between devices with their start and end apart: 13 -> 13, of which waited for: 11 -> 10; matrix products, arithmetic and copies ran while one was open for 5% -> 5% of each run, Pallas kernels for 1% -> 2%
where the time goes in v6:
time: 65.2 us; the launch traced here: 64.9 us
  starting transfers between devices  26 us (40%)
  waiting for transfers between devices  20.5 us (31%)
  Pallas kernels  9.27 us (14%)
  local copies, waits for them, and re-layouts  5.59 us (9%)
  other arithmetic  1.75 us (3%)
  between operations  1.73 us (3%)
    ppermute x5, starting transfers between devices, exchange(): return lax.ppermute(array, ('gz', 'gy'), pairs)  8.69 us
    ppermute x5, waiting for transfers between devices, exchange(): return lax.ppermute(array, ('gz', 'gy'), pairs)  6.16 us
    pallas_call x2, Pallas kernels, update(): pl.pallas_call(functools.partial(update_kernel, views=views, margin=margi...  4.97 us
    ppermute x2, waiting for transfers between devices, from_views(): return [message, lax.ppermute(message, 'view', [(0, 1), (1, 0)])]  4.85 us
    ppermute x1, starting transfers between devices, from_slabs_shifted(): lax.ppermute(sends[0], ('gz', 'gy'), gz_pairs(lambda place, odd: place -...  4.7 us
    ppermute x1, waiting for transfers between devices, from_slabs_beside(): first = lax.ppermute(sends[0], ('gz', 'gy'), ahead)  4.62 us
    ppermute x1, starting transfers between devices, from_slabs_beside(): first = lax.ppermute(sends[0], ('gz', 'gy'), ahead)  3.92 us
    unnamed x18, local copies, waits for them, and re-layouts  3.7 us
  transfers between devices with their start and end apart: 13, of which 10 were waited for; matrix products, arithmetic and copies ran while one was open for 5% of the time, Pallas kernels for 2%

profile of v6, /device:TPU:0, one launch (start us, length us, event | category | flops | bytes accessed | tf_op | source)
XLA Modules:
  0.0 64.9 jit_solution(6688238266293669860)
XLA Ops:
  1.3 3.0 %deposit.1 = (f32[264,128]{1,0:T(8,128)}, f32[264,128]{1,0:T(8,128)}, f32[264,128]{1,0:T(8,128)}, f32[264,128]{1,0:T(8,128)}, f32[264,128]{1,0:T(8,128)}, /*index=5*/f32[264,128]{1,0:T(8,128)}, f32[528,128]{1,0:T(8,128)}) custom-call(s32[32]{0:T(128)} %bitcast.50, s32[32]{0:T(128)} %bitcast.51, s32[1]{0:T(128)} %bitcast.31.level_hbm, f32[3]{0:T(128)} %bitcast.52, ...), custom_call_target="tpu_custom_call" | custom-call | tf_op jit(solution)/shard_map/deposit/pallas_call | solution.py:106
  4.3 3.1 %collective-permute-start.1 = (f32[528,128]{1,0:T(8,128)}, f32[528,128]{1,0:T(8,128)S(1)}, u32[]{:S(2)}, u32[]{:S(2)}) collective-permute-start(f32[528,128]{1,0:T(8,128)} %get-tuple-element.22), channel_id=1, source_target_pairs={{0,4},{1,9},{4,0},{5,13},{8,12},{9,1},{12,8},{13,5},{2,6},{3,11},{... | collective-permute-start | bytes 811016 | tf_op jit(solution)/shard_map/ppermute | solution.py:190
  7.5 1.9 %collective-permute-start.4 = (f32[264,128]{1,0:T(8,128)}, f32[264,128]{1,0:T(8,128)S(1)}, u32[]{:S(2)}, u32[]{:S(2)}) collective-permute-start(f32[264,128]{1,0:T(8,128)} %get-tuple-element.24), channel_id=1, source_target_pairs={{0,4},{1,9},{4,0},{5,13},{8,12},{9,1},{12,8},{13,5},{2,6},{3,11},{... | collective-permute-start | bytes 405512 | tf_op jit(solution)/shard_map/ppermute | solution.py:190
  10.0 0.9 %copy-done = f32[264,128]{1,0:T(8,128)S(1)} copy-done((f32[264,128]{1,0:T(8,128)S(1)}, f32[264,128]{1,0:T(8,128)}, u32[]{:S(2)}) %copy-start) | copy-done | bytes 135192
  10.9 0.9 %copy-done.1 = f32[264,128]{1,0:T(8,128)S(1)} copy-done((f32[264,128]{1,0:T(8,128)S(1)}, f32[264,128]{1,0:T(8,128)}, u32[]{:S(2)}) %copy-start.1) | copy-done | bytes 135192
  11.8 0.9 %copy-done.2 = f32[264,128]{1,0:T(8,128)S(1)} copy-done((f32[264,128]{1,0:T(8,128)S(1)}, f32[264,128]{1,0:T(8,128)}, u32[]{:S(2)}) %copy-start.2) | copy-done | bytes 135192
  12.7 0.9 %copy-done.3 = f32[264,128]{1,0:T(8,128)S(1)} copy-done((f32[264,128]{1,0:T(8,128)S(1)}, f32[264,128]{1,0:T(8,128)}, u32[]{:S(2)}) %copy-start.3) | copy-done | bytes 135192
  13.6 0.7 %fetch.1 = (f32[264,128]{1,0:T(8,128)S(1)}, f32[264,128]{1,0:T(8,128)S(1)}, f32[264,128]{1,0:T(8,128)S(1)}, f32[264,128]{1,0:T(8,128)S(1)}) custom-call(f32[264,128]{1,0:T(8,128)S(1)} %copy-done.1, f32[264,128]{1,0:T(8,128)S(1)} %copy-done.3, f32[264,128]{1,0:T(8,128)S(1)} %copy-done, f32[264,128]{1,0:T(8,128)S(1)} %copy-done.2), custom_call_target="tpu_custom_call" | custom-call | tf_op jit(solution)/shard_map/fetch/pallas_call | solution.py:153
  14.7 3.5 %collective-permute-start.2 = (f32[264,128]{1,0:T(8,128)S(1)}, f32[264,128]{1,0:T(8,128)S(1)}, u32[]{:S(2)}, u32[]{:S(2)}) collective-permute-start(f32[264,128]{1,0:T(8,128)S(1)} %add.519), channel_id=1, source_target_pairs={{0,8},{1,5},{4,12},{5,1},{8,0},{9,13},{12,4},{13,9},{2,10},{3,7},{... | collective-permute-start | bytes 405512 | tf_op jit(solution)/shard_map/ppermute | solution.py:190
  18.4 4.8 %collective-permute-done.2.rest_2_ = f32[264,128]{1,0:T(8,128)S(1)} collective-permute-done((f32[264,128]{1,0:T(8,128)S(1)}, f32[264,128]{1,0:T(8,128)S(1)}, u32[]{:S(2)}, u32[]{:S(2)}) %collective-permute-start.2) | collective-permute-done | bytes 135200 | tf_op jit(solution)/shard_map/ppermute | solution.py:190
  23.3 1.6 %collective-permute-start.3 = (f32[264,128]{1,0:T(8,128)S(1)}, f32[264,128]{1,0:T(8,128)S(1)}, u32[]{:S(2)}, u32[]{:S(2)}) collective-permute-start(f32[264,128]{1,0:T(8,128)S(1)} %join.2.rest_0_.rest_1_.rest_5_), channel_id=1, source_target_pairs={{0,2},{2,0},{1,3},{3,1},{4,6},{6,4},{5,7},{7,5},{8,10},{10,8},{9,1... | collective-permute-start | bytes 405512 | tf_op jit(solution)/shard_map/ppermute | solution.py:515
  24.9 1.1 %collective-permute-done.5.rest_2_ = f32[264,128]{1,0:T(8,128)S(1)} collective-permute-done((f32[264,128]{1,0:T(8,128)S(1)}, f32[264,128]{1,0:T(8,128)S(1)}, u32[]{:S(2)}, u32[]{:S(2)}) %collective-permute-start.5) | collective-permute-done | bytes 135200 | tf_op jit(solution)/shard_map/ppermute | solution.py:190
  26.1 1.6 %collective-permute-start.6 = (f32[264,128]{1,0:T(8,128)S(1)}, f32[264,128]{1,0:T(8,128)S(1)}, u32[]{:S(2)}, u32[]{:S(2)}) collective-permute-start(f32[264,128]{1,0:T(8,128)S(1)} %join.3.rest_1_.rest_2_.rest_6_), channel_id=1, source_target_pairs={{0,2},{2,0},{1,3},{3,1},{4,6},{6,4},{5,7},{7,5},{8,10},{10,8},{9,1... | collective-permute-start | bytes 405512 | tf_op jit(solution)/shard_map/ppermute | solution.py:515
  27.7 1.2 %collective-permute-done.3.rest_2_.rest_3_ = f32[264,128]{1,0:T(8,128)S(1)} collective-permute-done((f32[264,128]{1,0:T(8,128)S(1)}, f32[264,128]{1,0:T(8,128)S(1)}, u32[]{:S(2)}, u32[]{:S(2)}) %collective-permute-start.3) | collective-permute-done | bytes 135200 | tf_op jit(solution)/shard_map/ppermute | solution.py:515
  29.0 3.6 %collective-permute-done.6.rest_3_.rest_4_ = f32[264,128]{1,0:T(8,128)S(1)} collective-permute-done((f32[264,128]{1,0:T(8,128)S(1)}, f32[264,128]{1,0:T(8,128)S(1)}, u32[]{:S(2)}, u32[]{:S(2)}) %collective-permute-start.6) | collective-permute-done | bytes 135200 | tf_op jit(solution)/shard_map/ppermute | solution.py:515
  32.8 1.3 %collective-permute-start.7 = (f32[12,64,128]{2,1,0:T(8,128)S(1)}, f32[12,64,128]{2,1,0:T(8,128)S(1)}, u32[]{:S(2)}, u32[]{:S(2)}) collective-permute-start(f32[12,64,128]{2,1,0:T(8,128)S(1)} %get-tuple-element.67), channel_id=1, source_target_pairs={{1,5},{4,0},{5,9},{8,4},{9,13},{12,8},{3,7},{6,2},{7,11},{10,6},{1... | collective-permute-start | bytes 1179656 | tf_op jit(solution)/shard_map/ppermute | solution.py:488
  34.1 4.7 %collective-permute-start.8 = (f32[12,64,128]{2,1,0:T(8,128)S(1)}, f32[12,64,128]{2,1,0:T(8,128)S(1)}, u32[]{:S(2)}, u32[]{:S(2)}) collective-permute-start(f32[12,64,128]{2,1,0:T(8,128)S(1)} %get-tuple-element.66), channel_id=1, source_target_pairs={{0,4},{4,8},{5,1},{8,12},{9,5},{13,9},{2,6},{6,10},{7,3},{10,14},{... | collective-permute-start | bytes 1179656 | tf_op jit(solution)/shard_map/ppermute | solution.py:487
  38.9 0.3 slice_reduce_fusion.18
  39.3 0.3 slice_reduce_fusion.36
  39.6 0.3 slice_reduce_fusion.27
  40.6 0.3 slice_reduce_fusion.9
  41.3 3.4 %collective-permute-done.7 = f32[12,64,128]{2,1,0:T(8,128)S(1)} collective-permute-done((f32[12,64,128]{2,1,0:T(8,128)S(1)}, f32[12,64,128]{2,1,0:T(8,128)S(1)}, u32[]{:S(2)}, u32[]{:S(2)}) %collective-permute-start.7) | collective-permute-done | bytes 393248 | tf_op jit(solution)/shard_map/ppermute | solution.py:488
  44.9 1.9 %collective-permute-start.9 = (f32[40,8,128]{2,1,0:T(8,128)S(1)}, f32[40,8,128]{2,1,0:T(8,128)S(1)}, u32[]{:S(2)}, u32[]{:S(2)}) collective-permute-start(f32[40,8,128]{2,1,0:T(8,128)S(1)} %dynamic-slice_dynamic-update-slice_fusion.2), channel_id=1, source_target_pairs={{0,1},{1,0},{2,3},{3,2},{4,5},{5,4},{6,7},{7,6},{8,9},{9,8},{10,11... | collective-permute-start | bytes 491528 | tf_op jit(solution)/shard_map/ppermute | solution.py:498
  47.0 0.3 prepare.1.rest_0_
  47.4 0.5 collective-permute-done.9.low_rows_ref.high_rows_ref
  47.9 2.0 %update.2 = (f32[8,64,128]{2,1,0:T(8,128)S(1)}, f32[512,128]{1,0:T(8,128)}) custom-call(f32[20,8,128]{2,1,0:T(8,128)S(1)} %broadcast_in_dim.439.weight_ref, bf16[2,2,80,240]{3,2,1,0:T(8,128)(2,1)S(1)} %pad_maximum_fusion.3.row_band_ref, bf16[2,2,256,256]{3,2,1,0:T(8,128)(2,1)S(1)} %maximum_maximum_fusion.col_band_ref, ...), custom_call_target="tpu_custom_call" | custom-call | tf_op jit(solution)/shard_map/update/pallas_call | solution.py:450
  50.0 3.9 %collective-permute-start.10 = (f32[8,64,128]{2,1,0:T(8,128)S(1)}, f32[8,64,128]{2,1,0:T(8,128)S(1)}, u32[]{:S(2)}, u32[]{:S(2)}) collective-permute-start(f32[8,64,128]{2,1,0:T(8,128)S(1)} %get-tuple-element.26.rest_4_), channel_id=1, source_target_pairs={{0,4},{4,0},{5,9},{8,12},{9,5},{12,8},{2,6},{6,2},{7,11},{10,14},{... | collective-permute-start | bytes 786440 | tf_op jit(solution)/shard_map/ppermute | solution.py:476
  53.9 0.7 %collective-permute-start.11 = (f32[8,64,128]{2,1,0:T(8,128)S(1)}, f32[8,64,128]{2,1,0:T(8,128)S(1)}, u32[]{:S(2)}, u32[]{:S(2)}) collective-permute-start(f32[8,64,128]{2,1,0:T(8,128)S(1)} %get-tuple-element.26.rest_4_), channel_id=1, source_target_pairs={{1,5},{4,8},{5,1},{8,4},{9,13},{13,9},{3,7},{6,10},{7,3},{10,6},{1... | collective-permute-start | bytes 786440 | tf_op jit(solution)/shard_map/ppermute | solution.py:477
  54.6 4.6 %collective-permute-done.10 = f32[8,64,128]{2,1,0:T(8,128)S(1)} collective-permute-done((f32[8,64,128]{2,1,0:T(8,128)S(1)}, f32[8,64,128]{2,1,0:T(8,128)S(1)}, u32[]{:S(2)}, u32[]{:S(2)}) %collective-permute-start.10) | collective-permute-done | bytes 262176 | tf_op jit(solution)/shard_map/ppermute | solution.py:476
  59.3 1.7 %collective-permute-start.12 = (f32[24,8,128]{2,1,0:T(8,128)S(1)}, f32[24,8,128]{2,1,0:T(8,128)S(1)}, u32[]{:S(2)}, u32[]{:S(2)}) collective-permute-start(f32[24,8,128]{2,1,0:T(8,128)S(1)} %pad_maximum_fusion.4), channel_id=1, source_target_pairs={{0,1},{1,0},{2,3},{3,2},{4,5},{5,4},{6,7},{7,6},{8,9},{9,8},{10,11... | collective-permute-start | bytes 294920 | tf_op jit(solution)/shard_map/ppermute | solution.py:498
  61.0 0.9 %collective-permute-done.12.rest_7_.rest_8_ = f32[24,8,128]{2,1,0:T(8,128)S(1)} collective-permute-done((f32[24,8,128]{2,1,0:T(8,128)S(1)}, f32[24,8,128]{2,1,0:T(8,128)S(1)}, u32[]{:S(2)}, u32[]{:S(2)}) %collective-permute-start.12) | collective-permute-done | bytes 98336 | tf_op jit(solution)/shard_map/ppermute | solution.py:498
  62.0 2.9 %update.3 = f32[8,64,128]{2,1,0:T(8,128)} custom-call(f32[20,8,128]{2,1,0:T(8,128)S(1)} %broadcast_in_dim.439.weight_ref, bf16[2,2,80,240]{3,2,1,0:T(8,128)(2,1)S(1)} %pad_maximum_fusion.3.row_band_ref, bf16[2,2,256,256]{3,2,1,0:T(8,128)(2,1)S(1)} %maximum_maximum_fusion.col_band_ref, f32[12,64,128]{2,1,0:T(8,128)S(1)} %get-tuple-element.65.below_ref, ...), custom_call_target="tpu_custom_call" | custom-call | tf_op jit(solution)/shard_map/update/pallas_call | solution.py:450
  (73 shorter events, 3.3 us)
Async XLA Ops:
  0.6 8.8 %copy-start.5 = (f32[1,3]{1,0:T(1,128)S(1)}, f32[1,3]{1,0:T(1,128)}, u32[]{:S(2)}) copy-start(f32[1,3]{1,0:T(1,128)} %param.10) | copy-start | bytes 40
  0.6 9.1 %copy-start.4 = (f32[1,3,9]{2,0,1:T(1,128)S(1)}, f32[1,3,9]{2,0,1:T(1,128)}, u32[]{:S(2)}) copy-start(f32[1,3,9]{2,0,1:T(1,128)} %param.11) | copy-start | bytes 328
  4.3 10.3 %collective-permute-start.1 = (f32[528,128]{1,0:T(8,128)}, f32[528,128]{1,0:T(8,128)S(1)}, u32[]{:S(2)}, u32[]{:S(2)}) collective-permute-start(f32[528,128]{1,0:T(8,128)} %get-tuple-element.22), channel_id=1, source_target_pairs={{0,4},{1,9},{4,0},{5,13},{8,12},{9,1},{12,8},{13,5},{2,6},{3,11},{... | collective-permute-start | bytes 811016 | tf_op jit(solution)/shard_map/ppermute | solution.py:190
  7.4 10.9 %collective-permute-start = (f32[264,128]{1,0:T(8,128)}, f32[264,128]{1,0:T(8,128)S(1)}, u32[]{:S(2)}, u32[]{:S(2)}) collective-permute-start(f32[264,128]{1,0:T(8,128)} %get-tuple-element.20), channel_id=1, source_target_pairs={{0,4},{1,9},{4,0},{5,13},{8,12},{9,1},{12,8},{13,5},{2,6},{3,11},{... | collective-permute-start | bytes 405512 | tf_op jit(solution)/shard_map/ppermute | solution.py:190
  7.5 17.4 %collective-permute-start.4 = (f32[264,128]{1,0:T(8,128)}, f32[264,128]{1,0:T(8,128)S(1)}, u32[]{:S(2)}, u32[]{:S(2)}) collective-permute-start(f32[264,128]{1,0:T(8,128)} %get-tuple-element.24), channel_id=1, source_target_pairs={{0,4},{1,9},{4,0},{5,13},{8,12},{9,1},{12,8},{13,5},{2,6},{3,11},{... | collective-permute-start | bytes 405512 | tf_op jit(solution)/shard_map/ppermute | solution.py:190
  9.9 0.9 %copy-start = (f32[264,128]{1,0:T(8,128)S(1)}, f32[264,128]{1,0:T(8,128)}, u32[]{:S(2)}) copy-start(f32[264,128]{1,0:T(8,128)} %get-tuple-element.17.refs_2_) | copy-start | bytes 405508
  10.9 0.9 %copy-start.1 = (f32[264,128]{1,0:T(8,128)S(1)}, f32[264,128]{1,0:T(8,128)}, u32[]{:S(2)}) copy-start(f32[264,128]{1,0:T(8,128)} %get-tuple-element.15.refs_0_) | copy-start | bytes 405508
  11.8 0.9 %copy-start.2 = (f32[264,128]{1,0:T(8,128)S(1)}, f32[264,128]{1,0:T(8,128)}, u32[]{:S(2)}) copy-start(f32[264,128]{1,0:T(8,128)} %get-tuple-element.18.refs_3_) | copy-start | bytes 405508
  12.7 0.9 %copy-start.3 = (f32[264,128]{1,0:T(8,128)S(1)}, f32[264,128]{1,0:T(8,128)}, u32[]{:S(2)}) copy-start(f32[264,128]{1,0:T(8,128)} %get-tuple-element.16.refs_1_) | copy-start | bytes 405508
  14.7 8.5 %collective-permute-start.2 = (f32[264,128]{1,0:T(8,128)S(1)}, f32[264,128]{1,0:T(8,128)S(1)}, u32[]{:S(2)}, u32[]{:S(2)}) collective-permute-start(f32[264,128]{1,0:T(8,128)S(1)} %add.519), channel_id=1, source_target_pairs={{0,8},{1,5},{4,12},{5,1},{8,0},{9,13},{12,4},{13,9},{2,10},{3,7},{... | collective-permute-start | bytes 405512 | tf_op jit(solution)/shard_map/ppermute | solution.py:190
  18.2 7.8 %collective-permute-start.5 = (f32[264,128]{1,0:T(8,128)S(1)}, f32[264,128]{1,0:T(8,128)S(1)}, u32[]{:S(2)}, u32[]{:S(2)}) collective-permute-start(f32[264,128]{1,0:T(8,128)S(1)} %add.520), channel_id=1, source_target_pairs={{0,8},{1,5},{4,12},{5,1},{8,0},{9,13},{12,4},{13,9},{2,10},{3,7},{... | collective-permute-start | bytes 405512 | tf_op jit(solution)/shard_map/ppermute | solution.py:190
  23.3 5.6 %collective-permute-start.3 = (f32[264,128]{1,0:T(8,128)S(1)}, f32[264,128]{1,0:T(8,128)S(1)}, u32[]{:S(2)}, u32[]{:S(2)}) collective-permute-start(f32[264,128]{1,0:T(8,128)S(1)} %join.2.rest_0_.rest_1_.rest_5_), channel_id=1, source_target_pairs={{0,2},{2,0},{1,3},{3,1},{4,6},{6,4},{5,7},{7,5},{8,10},{10,8},{9,1... | collective-permute-start | bytes 405512 | tf_op jit(solution)/shard_map/ppermute | solution.py:515
  26.1 6.6 %collective-permute-start.6 = (f32[264,128]{1,0:T(8,128)S(1)}, f32[264,128]{1,0:T(8,128)S(1)}, u32[]{:S(2)}, u32[]{:S(2)}) collective-permute-start(f32[264,128]{1,0:T(8,128)S(1)} %join.3.rest_1_.rest_2_.rest_6_), channel_id=1, source_target_pairs={{0,2},{2,0},{1,3},{3,1},{4,6},{6,4},{5,7},{7,5},{8,10},{10,8},{9,1... | collective-permute-start | bytes 405512 | tf_op jit(solution)/shard_map/ppermute | solution.py:515
  32.8 11.9 %collective-permute-start.7 = (f32[12,64,128]{2,1,0:T(8,128)S(1)}, f32[12,64,128]{2,1,0:T(8,128)S(1)}, u32[]{:S(2)}, u32[]{:S(2)}) collective-permute-start(f32[12,64,128]{2,1,0:T(8,128)S(1)} %get-tuple-element.67), channel_id=1, source_target_pairs={{1,5},{4,0},{5,9},{8,4},{9,13},{12,8},{3,7},{6,2},{7,11},{10,6},{1... | collective-permute-start | bytes 1179656 | tf_op jit(solution)/shard_map/ppermute | solution.py:488
  34.1 10.6 %collective-permute-start.8 = (f32[12,64,128]{2,1,0:T(8,128)S(1)}, f32[12,64,128]{2,1,0:T(8,128)S(1)}, u32[]{:S(2)}, u32[]{:S(2)}) collective-permute-start(f32[12,64,128]{2,1,0:T(8,128)S(1)} %get-tuple-element.66), channel_id=1, source_target_pairs={{0,4},{4,8},{5,1},{8,12},{9,5},{13,9},{2,6},{6,10},{7,3},{10,14},{... | collective-permute-start | bytes 1179656 | tf_op jit(solution)/shard_map/ppermute | solution.py:487
  44.9 3.0 %collective-permute-start.9 = (f32[40,8,128]{2,1,0:T(8,128)S(1)}, f32[40,8,128]{2,1,0:T(8,128)S(1)}, u32[]{:S(2)}, u32[]{:S(2)}) collective-permute-start(f32[40,8,128]{2,1,0:T(8,128)S(1)} %dynamic-slice_dynamic-update-slice_fusion.2), channel_id=1, source_target_pairs={{0,1},{1,0},{2,3},{3,2},{4,5},{5,4},{6,7},{7,6},{8,9},{9,8},{10,11... | collective-permute-start | bytes 491528 | tf_op jit(solution)/shard_map/ppermute | solution.py:498
  50.0 9.3 %collective-permute-start.10 = (f32[8,64,128]{2,1,0:T(8,128)S(1)}, f32[8,64,128]{2,1,0:T(8,128)S(1)}, u32[]{:S(2)}, u32[]{:S(2)}) collective-permute-start(f32[8,64,128]{2,1,0:T(8,128)S(1)} %get-tuple-element.26.rest_4_), channel_id=1, source_target_pairs={{0,4},{4,0},{5,9},{8,12},{9,5},{12,8},{2,6},{6,2},{7,11},{10,14},{... | collective-permute-start | bytes 786440 | tf_op jit(solution)/shard_map/ppermute | solution.py:476
  53.9 5.3 %collective-permute-start.11 = (f32[8,64,128]{2,1,0:T(8,128)S(1)}, f32[8,64,128]{2,1,0:T(8,128)S(1)}, u32[]{:S(2)}, u32[]{:S(2)}) collective-permute-start(f32[8,64,128]{2,1,0:T(8,128)S(1)} %get-tuple-element.26.rest_4_), channel_id=1, source_target_pairs={{1,5},{4,8},{5,1},{8,4},{9,13},{13,9},{3,7},{6,10},{7,3},{10,6},{1... | collective-permute-start | bytes 786440 | tf_op jit(solution)/shard_map/ppermute | solution.py:477
  59.3 2.6 %collective-permute-start.12 = (f32[24,8,128]{2,1,0:T(8,128)S(1)}, f32[24,8,128]{2,1,0:T(8,128)S(1)}, u32[]{:S(2)}, u32[]{:S(2)}) collective-permute-start(f32[24,8,128]{2,1,0:T(8,128)S(1)} %pad_maximum_fusion.4), channel_id=1, source_target_pairs={{0,1},{1,0},{2,3},{3,2},{4,5},{5,4},{6,7},{7,6},{8,9},{9,8},{10,11... | collective-permute-start | bytes 294920 | tf_op jit(solution)/shard_map/ppermute | solution.py:498

commit v7 on v6

--- a/solution.py
+++ b/solution.py
@@ -43,7 +43,7 @@
 
 
 def deposit_kernel(
-    target_hbm, first_hbm, level_hbm, fraction_hbm, camera_hbm, *rest, slabs, section, chunk
+    target_hbm, first_hbm, level_hbm, fraction_hbm, camera_hbm, *rest, slabs, sections, chunk
 ):
     *out_refs, sums_ref, target, first, level, fraction, camera, small_sems, camera_sems = rest
     blocks, planes, rows, cols = camera.shape
@@ -61,17 +61,18 @@
     quarter = slabs // 4
 
     def section_row(half, slab):
+        size = jnp.where(half == 0, sections[0], sections[1])
         if not quarter:
-            return (half * slabs + slab) * section
-        ahead = jnp.where(slab < 3 * quarter, half * 3 * quarter, 3 * quarter + half * quarter)
-        return (ahead + slab) * section
+            return half * slabs * sections[0] + slab * size
+        last = 3 * quarter * sum(sections) + half * quarter * sections[0] + (slab - 3 * quarter) * size
+        return jnp.where(slab < 3 * quarter, half * 3 * quarter * sections[0] + slab * size, last)
 
     place = lax.axis_index("gz").astype(jnp.int32)
     odd = lax.axis_index("gy") % 2 == 1
     base_level = level[0].astype(F32)
     upper_share = fraction[0]
     lower_share = 1.0 - upper_share
-    count_at = lax.broadcasted_iota(jnp.int32, (SUB, cols), 0)
+    count_at = lax.broadcasted_iota(jnp.int32, (CZ, cols), 0)
 
     def one(block, carry):
         away = target[block] ^ place
@@ -85,9 +86,9 @@
             start = section_row(half, slab)
             here = pl.ds(pl.multiple_of(start + (lands - half * HALF) * rows, SUB), rows)
             sums_ref[here, :] += lower_share * lower + upper_share * upper
-            counts = pl.ds(pl.multiple_of(start + HALF * rows, SUB), SUB)
-            sums_ref[counts, :] += (count_at == lands - half * HALF).astype(F32)
             lower = upper
+        counts = pl.ds(pl.multiple_of(section_row(0, slab) + HALF * rows, SUB), CZ)
+        sums_ref[counts, :] += ((count_at >= at) & (count_at < at + planes - 1)).astype(F32)
         return carry
 
     for i, copy in enumerate(parts):
@@ -99,17 +100,17 @@
         at += out_ref.shape[0]
 
 
-def deposit(camera, target, first, level, fraction, slabs, shares):
+def deposit(camera, target, first, level, fraction, slabs):
     blocks, planes, rows, cols = camera.shape
-    section = HALF * rows + SUB
+    sections = section_sizes(rows)
     chunk = HALF if blocks % HALF == 0 else blocks
     return pl.pallas_call(
-        functools.partial(deposit_kernel, slabs=slabs, section=section, chunk=chunk),
+        functools.partial(deposit_kernel, slabs=slabs, sections=sections, chunk=chunk),
         in_specs=[HBM] * 5,
-        out_specs=[VMEM] * len(shares),
-        out_shape=[jax.ShapeDtypeStruct((share * section, cols), F32) for share in shares],
+        out_specs=[VMEM] * len(first_shares(slabs, sections)),
+        out_shape=[jax.ShapeDtypeStruct((size, cols), F32) for size in first_shares(slabs, sections)],
         scratch_shapes=[
-            pltpu.VMEM((2 * slabs * section, cols), F32),
+            pltpu.VMEM((slabs * sum(sections), cols), F32),
             pltpu.SMEM(target.shape, jnp.int32),
             pltpu.SMEM(first.shape, jnp.int32),
             pltpu.SMEM(level.shape, jnp.int32),
@@ -134,10 +135,15 @@
     return pairs
 
 
-def first_shares(slabs):
+def section_sizes(rows):
+    return HALF * rows + CZ, HALF * rows
+
+
+def first_shares(slabs, sections):
     if slabs <= 2:
-        return [1] * (2 * slabs)
-    return [slabs // 4] * 6 + [slabs // 2]
+        return [size for size in sections for _ in range(slabs)]
+    quarter = slabs // 4
+    return [quarter * size for size in sections for _ in range(3)] + [quarter * sum(sections)]
 
 
 def fetch_kernel(*refs):
@@ -176,7 +182,7 @@
     )(left, right)
 
 
-def butterfly(shares, slabs, section):
+def butterfly(shares, slabs, sections):
     if slabs == 1:
         return [(share,) for share in shares]
     if slabs == 2:
@@ -196,25 +202,32 @@
             halves = [[fetched[2 + i], fetched[i], half[2]] for i, half in enumerate(halves)]
         onward = exchange(onward)
         stays = [exchange(half[2]) for half in halves]
-        cut = onward.shape[0] // 2
+        cut = stays[0].shape[0]
         sends = [add(half[1], array) for half, array in zip(halves, (onward[:cut], onward[cut:]))]
-        if stays[0].shape[0] == section:
+        if cut == sections[0]:
             halves = [(half[0], array, send) for half, array, send in zip(halves, stays, sends)]
         else:
             keeps = [add(half[0], array) for half, array in zip(halves, stays)]
-            cut //= 2
-            halves = [(keep[:cut], keep[cut:], send[:cut]) for keep, send in zip(keeps, sends)]
-            onward = jnp.concatenate([send[cut:] for send in sends])
-
-
-def join_kernel(small_ref, *rest, rows):
-    *term_refs, message_ref = rest
+            cuts = [keep.shape[0] // 2 for keep in keeps]
+            halves = [(keep[:cut], keep[cut:], send[:cut]) for cut, keep, send in zip(cuts, keeps, sends)]
+            onward = jnp.concatenate([send[cut:] for cut, send in zip(cuts, sends)])
+
+
+def join_kernel(small_ref, *rest, rows, half):
+    if half == 0:
+        *term_refs, message_ref, count_ref = rest
+    else:
+        count_ref, *term_refs, message_ref = rest
     cols = message_ref.shape[1]
     total = term_refs[0][...]
     for term_ref in term_refs[1:]:
         total = total + term_ref[...]
     planes = total[: HALF * rows].reshape(HALF, rows, cols)
-    counts = total[HALF * rows :]
+    if half == 0:
+        counts = total[HALF * rows :]
+        count_ref[...] = counts
+    else:
+        counts = count_ref[HALF:]
     fy, fx = small_ref[3:4], small_ref[4:5]
     row_at = lax.broadcasted_iota(jnp.int32, (rows, cols), 0)
     col_at = lax.broadcasted_iota(jnp.int32, (rows, cols), 1)
@@ -226,18 +239,22 @@
         part = (1.0 - fx) * part + fx * follow
         part = jnp.maximum(part / (counts[plane : plane + 1] + 1.0), DATA_FLOOR)
         message_ref[plane * rows : (plane + 1) * rows] = part
-    message_ref[HALF * rows :] = small_ref[...]
-
-
-def join(small, terms, rows):
+    if half == 0:
+        message_ref[HALF * rows :] = small_ref[...]
+
+
+def join(small, counts, terms, rows):
+    half = 0 if counts is None else 1
+    arrays = [small, *terms] if half == 0 else [small, counts, *terms]
+    message = jax.ShapeDtypeStruct(terms[0].shape, F32)
     return pl.pallas_call(
-        functools.partial(join_kernel, rows=rows),
-        in_specs=[VMEM] * (1 + len(terms)),
-        out_specs=VMEM,
-        out_shape=jax.ShapeDtypeStruct(terms[0].shape, F32),
+        functools.partial(join_kernel, rows=rows, half=half),
+        in_specs=[VMEM] * len(arrays),
+        out_specs=[VMEM] * 2 if half == 0 else VMEM,
+        out_shape=[message, jax.ShapeDtypeStruct(small.shape, F32)] if half == 0 else message,
         compiler_params=pltpu.CompilerParams(vmem_limit_bytes=VMEM_BYTES),
         name="join",
-    )(small, *terms)
+    )(*arrays)
 
 
 def taps_sum(values, weights):
@@ -524,11 +541,9 @@
     taps = psf_taps.shape[-1]
     margin = taps // 2
     assert margin == HALF
-    section = HALF * rows + SUB
     fraction = shift_frac[0]
     shares = deposit(
-        camera[0], destination.reshape(blocks), offsets.reshape(blocks), background.reshape(1), fraction, slabs,
-        first_shares(slabs),
+        camera[0], destination.reshape(blocks), offsets.reshape(blocks), background.reshape(1), fraction, slabs
     )
     small = jnp.concatenate(
         [
@@ -538,9 +553,14 @@
         ]
     )
     own, messages = [], []
-    for terms in butterfly(shares, slabs, section):
-        own.append(join(small, terms, rows))
-        messages.append(from_views(own[-1]))
+    counts = None
+    for terms in butterfly(shares, slabs, section_sizes(rows)):
+        if counts is None:
+            message, counts = join(small, counts, terms, rows)
+        else:
+            message = join(small, counts, terms, rows)
+        own.append(message)
+        messages.append(from_views(message))
     halves = [messages[half][view] for view in range(views) for half in range(2)]
     low_half, high_half = (
         [message[: HALF * rows].reshape(HALF, rows, cols) for message in messages[half]] for half in range(2)

time: 65.2 us -> 65 us (level)
  transfers between devices with their start and end apart: 13 -> 13, of which waited for: 10 -> 8; matrix products, arithmetic and copies ran while one was open for 5% -> 5% of each run, Pallas kernels for 2% -> 2%
where the time goes in v7:
time: 65 us; the launch traced here: 64.7 us
  starting transfers between devices  26.1 us (40%)
  waiting for transfers between devices  20.4 us (31%)
  Pallas kernels  9.2 us (14%)
  local copies, waits for them, and re-layouts  5.57 us (9%)
  other arithmetic  1.75 us (3%)
  between operations  1.74 us (3%)
    ppermute x5, starting transfers between devices, exchange(): return lax.ppermute(array, ('gz', 'gy'), pairs)  8.69 us
    ppermute x5, waiting for transfers between devices, exchange(): return lax.ppermute(array, ('gz', 'gy'), pairs)  5.9 us
    ppermute x2, waiting for transfers between devices, from_views(): return [message, lax.ppermute(message, 'view', [(0, 1), (1, 0)])]  4.95 us
    pallas_call x2, Pallas kernels, update(): pl.pallas_call(functools.partial(update_kernel, views=views, margin=margi...  4.92 us
    ppermute x1, starting transfers between devices, from_slabs_shifted(): lax.ppermute(sends[0], ('gz', 'gy'), gz_pairs(lambda place, odd: place -...  4.78 us
    ppermute x1, waiting for transfers between devices, from_slabs_beside(): first = lax.ppermute(sends[0], ('gz', 'gy'), ahead)  4.62 us
    ppermute x1, starting transfers between devices, from_slabs_beside(): first = lax.ppermute(sends[0], ('gz', 'gy'), ahead)  3.92 us
    unnamed x18, local copies, waits for them, and re-layouts  3.7 us
  transfers between devices with their start and end apart: 13, of which 8 were waited for; matrix products, arithmetic and copies ran while one was open for 5% of the time, Pallas kernels for 2%

profile of v7, /device:TPU:0, one launch (start us, length us, event | category | flops | bytes accessed | tf_op | source)
XLA Modules:
  0.0 64.7 jit_solution(15178664185932987258)
XLA Ops:
  1.3 3.0 %deposit.1 = (f32[264,128]{1,0:T(8,128)}, f32[264,128]{1,0:T(8,128)}, f32[264,128]{1,0:T(8,128)}, f32[256,128]{1,0:T(8,128)}, f32[256,128]{1,0:T(8,128)}, /*index=5*/f32[256,128]{1,0:T(8,128)}, f32[520,128]{1,0:T(8,128)}) custom-call(s32[32]{0:T(128)} %bitcast.50, s32[32]{0:T(128)} %bitcast.51, s32[1]{0:T(128)} %bitcast.31.level_hbm, f32[3]{0:T(128)} %bitcast.52, ...), custom_call_target="tpu_custom_call" | custom-call | tf_op jit(solution)/shard_map/deposit/pallas_call | solution.py:107
  4.3 3.1 %collective-permute-start.1 = (f32[520,128]{1,0:T(8,128)}, f32[520,128]{1,0:T(8,128)S(1)}, u32[]{:S(2)}, u32[]{:S(2)}) collective-permute-start(f32[520,128]{1,0:T(8,128)} %get-tuple-element.24), channel_id=1, source_target_pairs={{0,4},{1,9},{4,0},{5,13},{8,12},{9,1},{12,8},{13,5},{2,6},{3,11},{... | collective-permute-start | bytes 798728 | tf_op jit(solution)/shard_map/ppermute | solution.py:196
  7.5 1.9 %collective-permute-start.4 = (f32[256,128]{1,0:T(8,128)}, f32[256,128]{1,0:T(8,128)S(1)}, u32[]{:S(2)}, u32[]{:S(2)}) collective-permute-start(f32[256,128]{1,0:T(8,128)} %get-tuple-element.28), channel_id=1, source_target_pairs={{0,4},{1,9},{4,0},{5,13},{8,12},{9,1},{12,8},{13,5},{2,6},{3,11},{... | collective-permute-start | bytes 393224 | tf_op jit(solution)/shard_map/ppermute | solution.py:196
  9.9 0.9 %copy-done = f32[264,128]{1,0:T(8,128)S(1)} copy-done((f32[264,128]{1,0:T(8,128)S(1)}, f32[264,128]{1,0:T(8,128)}, u32[]{:S(2)}) %copy-start) | copy-done | bytes 135192
  10.9 0.9 %copy-done.1 = f32[264,128]{1,0:T(8,128)S(1)} copy-done((f32[264,128]{1,0:T(8,128)S(1)}, f32[264,128]{1,0:T(8,128)}, u32[]{:S(2)}) %copy-start.1) | copy-done | bytes 135192
  11.8 0.9 %copy-done.2 = f32[256,128]{1,0:T(8,128)S(1)} copy-done((f32[256,128]{1,0:T(8,128)S(1)}, f32[256,128]{1,0:T(8,128)}, u32[]{:S(2)}) %copy-start.2) | copy-done | bytes 131096
  12.7 0.9 %copy-done.3 = f32[256,128]{1,0:T(8,128)S(1)} copy-done((f32[256,128]{1,0:T(8,128)S(1)}, f32[256,128]{1,0:T(8,128)}, u32[]{:S(2)}) %copy-start.3) | copy-done | bytes 131096
  13.6 0.7 %fetch.1 = (f32[264,128]{1,0:T(8,128)S(1)}, f32[256,128]{1,0:T(8,128)S(1)}, f32[264,128]{1,0:T(8,128)S(1)}, f32[256,128]{1,0:T(8,128)S(1)}) custom-call(f32[264,128]{1,0:T(8,128)S(1)} %copy-done.1, f32[256,128]{1,0:T(8,128)S(1)} %copy-done.3, f32[264,128]{1,0:T(8,128)S(1)} %copy-done, f32[256,128]{1,0:T(8,128)S(1)} %copy-done.2), custom_call_target="tpu_custom_call" | custom-call | tf_op jit(solution)/shard_map/fetch/pallas_call | solution.py:159
  14.6 3.5 %collective-permute-start.2 = (f32[264,128]{1,0:T(8,128)S(1)}, f32[264,128]{1,0:T(8,128)S(1)}, u32[]{:S(2)}, u32[]{:S(2)}) collective-permute-start(f32[264,128]{1,0:T(8,128)S(1)} %add.519), channel_id=1, source_target_pairs={{0,8},{1,5},{4,12},{5,1},{8,0},{9,13},{12,4},{13,9},{2,10},{3,7},{... | collective-permute-start | bytes 405512 | tf_op jit(solution)/shard_map/ppermute | solution.py:196
  18.3 4.7 %collective-permute-done.2.rest_2_ = f32[264,128]{1,0:T(8,128)S(1)} collective-permute-done((f32[264,128]{1,0:T(8,128)S(1)}, f32[264,128]{1,0:T(8,128)S(1)}, u32[]{:S(2)}, u32[]{:S(2)}) %collective-permute-start.2) | collective-permute-done | bytes 135200 | tf_op jit(solution)/shard_map/ppermute | solution.py:196
  23.1 1.6 %collective-permute-start.3 = (f32[264,128]{1,0:T(8,128)S(1)}, f32[264,128]{1,0:T(8,128)S(1)}, u32[]{:S(2)}, u32[]{:S(2)}) collective-permute-start(f32[264,128]{1,0:T(8,128)S(1)} %get-tuple-element.25.rest_0_.rest_1_.rest_5_), channel_id=1, source_target_pairs={{0,2},{2,0},{1,3},{3,1},{4,6},{6,4},{5,7},{7,5},{8,10},{10,8},{9,1... | collective-permute-start | bytes 405512 | tf_op jit(solution)/shard_map/ppermute | solution.py:532
  24.7 1.0 %collective-permute-done.5.rest_3_ = f32[256,128]{1,0:T(8,128)S(1)} collective-permute-done((f32[256,128]{1,0:T(8,128)S(1)}, f32[256,128]{1,0:T(8,128)S(1)}, u32[]{:S(2)}, u32[]{:S(2)}) %collective-permute-start.5) | collective-permute-done | bytes 131104 | tf_op jit(solution)/shard_map/ppermute | solution.py:196
  25.8 1.6 %collective-permute-start.6 = (f32[256,128]{1,0:T(8,128)S(1)}, f32[256,128]{1,0:T(8,128)S(1)}, u32[]{:S(2)}, u32[]{:S(2)}) collective-permute-start(f32[256,128]{1,0:T(8,128)S(1)} %join.3.rest_1_.rest_2_.rest_6_), channel_id=1, source_target_pairs={{0,2},{2,0},{1,3},{3,1},{4,6},{6,4},{5,7},{7,5},{8,10},{10,8},{9,1... | collective-permute-start | bytes 393224 | tf_op jit(solution)/shard_map/ppermute | solution.py:532
  27.4 4.9 %collective-permute-done.6.rest_3_.rest_4_ = f32[256,128]{1,0:T(8,128)S(1)} collective-permute-done((f32[256,128]{1,0:T(8,128)S(1)}, f32[256,128]{1,0:T(8,128)S(1)}, u32[]{:S(2)}, u32[]{:S(2)}) %collective-permute-start.6) | collective-permute-done | bytes 131104 | tf_op jit(solution)/shard_map/ppermute | solution.py:532
  32.6 1.3 %collective-permute-start.7 = (f32[12,64,128]{2,1,0:T(8,128)S(1)}, f32[12,64,128]{2,1,0:T(8,128)S(1)}, u32[]{:S(2)}, u32[]{:S(2)}) collective-permute-start(f32[12,64,128]{2,1,0:T(8,128)S(1)} %get-tuple-element.71), channel_id=1, source_target_pairs={{1,5},{4,0},{5,9},{8,4},{9,13},{12,8},{3,7},{6,2},{7,11},{10,6},{1... | collective-permute-start | bytes 1179656 | tf_op jit(solution)/shard_map/ppermute | solution.py:505
  33.9 4.8 %collective-permute-start.8 = (f32[12,64,128]{2,1,0:T(8,128)S(1)}, f32[12,64,128]{2,1,0:T(8,128)S(1)}, u32[]{:S(2)}, u32[]{:S(2)}) collective-permute-start(f32[12,64,128]{2,1,0:T(8,128)S(1)} %get-tuple-element.70), channel_id=1, source_target_pairs={{0,4},{4,8},{5,1},{8,12},{9,5},{13,9},{2,6},{6,10},{7,3},{10,14},{... | collective-permute-start | bytes 1179656 | tf_op jit(solution)/shard_map/ppermute | solution.py:504
  38.8 0.3 slice_reduce_fusion.18
  39.2 0.3 slice_reduce_fusion.36
  39.5 0.3 slice_reduce_fusion.27
  40.3 0.2 select_add_fusion.1
  40.5 0.3 slice_reduce_fusion.9
  41.2 3.5 %collective-permute-done.7 = f32[12,64,128]{2,1,0:T(8,128)S(1)} collective-permute-done((f32[12,64,128]{2,1,0:T(8,128)S(1)}, f32[12,64,128]{2,1,0:T(8,128)S(1)}, u32[]{:S(2)}, u32[]{:S(2)}) %collective-permute-start.7) | collective-permute-done | bytes 393248 | tf_op jit(solution)/shard_map/ppermute | solution.py:505
  44.8 1.9 %collective-permute-start.9 = (f32[40,8,128]{2,1,0:T(8,128)S(1)}, f32[40,8,128]{2,1,0:T(8,128)S(1)}, u32[]{:S(2)}, u32[]{:S(2)}) collective-permute-start(f32[40,8,128]{2,1,0:T(8,128)S(1)} %dynamic-slice_dynamic-update-slice_fusion.2), channel_id=1, source_target_pairs={{0,1},{1,0},{2,3},{3,2},{4,5},{5,4},{6,7},{7,6},{8,9},{9,8},{10,11... | collective-permute-start | bytes 491528 | tf_op jit(solution)/shard_map/ppermute | solution.py:515
  46.9 0.3 prepare.1.rest_0_
  47.3 0.5 collective-permute-done.9.low_rows_ref.high_rows_ref
  47.8 2.0 %update.2 = (f32[8,64,128]{2,1,0:T(8,128)S(1)}, f32[512,128]{1,0:T(8,128)}) custom-call(f32[20,8,128]{2,1,0:T(8,128)S(1)} %broadcast_in_dim.439.weight_ref, bf16[2,2,80,240]{3,2,1,0:T(8,128)(2,1)S(1)} %pad_maximum_fusion.3.row_band_ref, bf16[2,2,256,256]{3,2,1,0:T(8,128)(2,1)S(1)} %maximum_maximum_fusion.col_band_ref, ...), custom_call_target="tpu_custom_call" | custom-call | tf_op jit(solution)/shard_map/update/pallas_call | solution.py:467
  49.8 3.9 %collective-permute-start.10 = (f32[8,64,128]{2,1,0:T(8,128)S(1)}, f32[8,64,128]{2,1,0:T(8,128)S(1)}, u32[]{:S(2)}, u32[]{:S(2)}) collective-permute-start(f32[8,64,128]{2,1,0:T(8,128)S(1)} %get-tuple-element.30.rest_4_), channel_id=1, source_target_pairs={{0,4},{4,0},{5,9},{8,12},{9,5},{12,8},{2,6},{6,2},{7,11},{10,14},{... | collective-permute-start | bytes 786440 | tf_op jit(solution)/shard_map/ppermute | solution.py:493
  53.8 0.7 %collective-permute-start.11 = (f32[8,64,128]{2,1,0:T(8,128)S(1)}, f32[8,64,128]{2,1,0:T(8,128)S(1)}, u32[]{:S(2)}, u32[]{:S(2)}) collective-permute-start(f32[8,64,128]{2,1,0:T(8,128)S(1)} %get-tuple-element.30.rest_4_), channel_id=1, source_target_pairs={{1,5},{4,8},{5,1},{8,4},{9,13},{13,9},{3,7},{6,10},{7,3},{10,6},{1... | collective-permute-start | bytes 786440 | tf_op jit(solution)/shard_map/ppermute | solution.py:494
  54.5 4.6 %collective-permute-done.10 = f32[8,64,128]{2,1,0:T(8,128)S(1)} collective-permute-done((f32[8,64,128]{2,1,0:T(8,128)S(1)}, f32[8,64,128]{2,1,0:T(8,128)S(1)}, u32[]{:S(2)}, u32[]{:S(2)}) %collective-permute-start.10) | collective-permute-done | bytes 262176 | tf_op jit(solution)/shard_map/ppermute | solution.py:493
  59.2 1.7 %collective-permute-start.12 = (f32[24,8,128]{2,1,0:T(8,128)S(1)}, f32[24,8,128]{2,1,0:T(8,128)S(1)}, u32[]{:S(2)}, u32[]{:S(2)}) collective-permute-start(f32[24,8,128]{2,1,0:T(8,128)S(1)} %pad_maximum_fusion.4), channel_id=1, source_target_pairs={{0,1},{1,0},{2,3},{3,2},{4,5},{5,4},{6,7},{7,6},{8,9},{9,8},{10,11... | collective-permute-start | bytes 294920 | tf_op jit(solution)/shard_map/ppermute | solution.py:515
  60.9 0.9 %collective-permute-done.12.rest_7_.rest_8_ = f32[24,8,128]{2,1,0:T(8,128)S(1)} collective-permute-done((f32[24,8,128]{2,1,0:T(8,128)S(1)}, f32[24,8,128]{2,1,0:T(8,128)S(1)}, u32[]{:S(2)}, u32[]{:S(2)}) %collective-permute-start.12) | collective-permute-done | bytes 98336 | tf_op jit(solution)/shard_map/ppermute | solution.py:515
  61.8 2.9 %update.3 = f32[8,64,128]{2,1,0:T(8,128)} custom-call(f32[20,8,128]{2,1,0:T(8,128)S(1)} %broadcast_in_dim.439.weight_ref, bf16[2,2,80,240]{3,2,1,0:T(8,128)(2,1)S(1)} %pad_maximum_fusion.3.row_band_ref, bf16[2,2,256,256]{3,2,1,0:T(8,128)(2,1)S(1)} %maximum_maximum_fusion.col_band_ref, f32[12,64,128]{2,1,0:T(8,128)S(1)} %get-tuple-element.69.below_ref, ...), custom_call_target="tpu_custom_call" | custom-call | tf_op jit(solution)/shard_map/update/pallas_call | solution.py:467
  (72 shorter events, 2.9 us)
Async XLA Ops:
  0.6 8.8 %copy-start.5 = (f32[1,3]{1,0:T(1,128)S(1)}, f32[1,3]{1,0:T(1,128)}, u32[]{:S(2)}) copy-start(f32[1,3]{1,0:T(1,128)} %param.10) | copy-start | bytes 40
  0.6 9.1 %copy-start.4 = (f32[1,3,9]{2,0,1:T(1,128)S(1)}, f32[1,3,9]{2,0,1:T(1,128)}, u32[]{:S(2)}) copy-start(f32[1,3,9]{2,0,1:T(1,128)} %param.11) | copy-start | bytes 328
  4.3 10.2 %collective-permute-start.1 = (f32[520,128]{1,0:T(8,128)}, f32[520,128]{1,0:T(8,128)S(1)}, u32[]{:S(2)}, u32[]{:S(2)}) collective-permute-start(f32[520,128]{1,0:T(8,128)} %get-tuple-element.24), channel_id=1, source_target_pairs={{0,4},{1,9},{4,0},{5,13},{8,12},{9,1},{12,8},{13,5},{2,6},{3,11},{... | collective-permute-start | bytes 798728 | tf_op jit(solution)/shard_map/ppermute | solution.py:196
  7.4 10.9 %collective-permute-start = (f32[264,128]{1,0:T(8,128)}, f32[264,128]{1,0:T(8,128)S(1)}, u32[]{:S(2)}, u32[]{:S(2)}) collective-permute-start(f32[264,128]{1,0:T(8,128)} %get-tuple-element.22), channel_id=1, source_target_pairs={{0,4},{1,9},{4,0},{5,13},{8,12},{9,1},{12,8},{13,5},{2,6},{3,11},{... | collective-permute-start | bytes 405512 | tf_op jit(solution)/shard_map/ppermute | solution.py:196
  7.5 17.2 %collective-permute-start.4 = (f32[256,128]{1,0:T(8,128)}, f32[256,128]{1,0:T(8,128)S(1)}, u32[]{:S(2)}, u32[]{:S(2)}) collective-permute-start(f32[256,128]{1,0:T(8,128)} %get-tuple-element.28), channel_id=1, source_target_pairs={{0,4},{1,9},{4,0},{5,13},{8,12},{9,1},{12,8},{13,5},{2,6},{3,11},{... | collective-permute-start | bytes 393224 | tf_op jit(solution)/shard_map/ppermute | solution.py:196
  9.9 0.9 %copy-start = (f32[264,128]{1,0:T(8,128)S(1)}, f32[264,128]{1,0:T(8,128)}, u32[]{:S(2)}) copy-start(f32[264,128]{1,0:T(8,128)} %get-tuple-element.19.refs_2_) | copy-start | bytes 405508
  10.9 0.9 %copy-start.1 = (f32[264,128]{1,0:T(8,128)S(1)}, f32[264,128]{1,0:T(8,128)}, u32[]{:S(2)}) copy-start(f32[264,128]{1,0:T(8,128)} %get-tuple-element.17.refs_0_) | copy-start | bytes 405508
  11.8 0.9 %copy-start.2 = (f32[256,128]{1,0:T(8,128)S(1)}, f32[256,128]{1,0:T(8,128)}, u32[]{:S(2)}) copy-start(f32[256,128]{1,0:T(8,128)} %get-tuple-element.20.refs_3_) | copy-start | bytes 393220
  12.7 0.9 %copy-start.3 = (f32[256,128]{1,0:T(8,128)S(1)}, f32[256,128]{1,0:T(8,128)}, u32[]{:S(2)}) copy-start(f32[256,128]{1,0:T(8,128)} %get-tuple-element.18.refs_1_) | copy-start | bytes 393220
  14.6 8.5 %collective-permute-start.2 = (f32[264,128]{1,0:T(8,128)S(1)}, f32[264,128]{1,0:T(8,128)S(1)}, u32[]{:S(2)}, u32[]{:S(2)}) collective-permute-start(f32[264,128]{1,0:T(8,128)S(1)} %add.519), channel_id=1, source_target_pairs={{0,8},{1,5},{4,12},{5,1},{8,0},{9,13},{12,4},{13,9},{2,10},{3,7},{... | collective-permute-start | bytes 405512 | tf_op jit(solution)/shard_map/ppermute | solution.py:196
  18.1 7.6 %collective-permute-start.5 = (f32[256,128]{1,0:T(8,128)S(1)}, f32[256,128]{1,0:T(8,128)S(1)}, u32[]{:S(2)}, u32[]{:S(2)}) collective-permute-start(f32[256,128]{1,0:T(8,128)S(1)} %add.520), channel_id=1, source_target_pairs={{0,8},{1,5},{4,12},{5,1},{8,0},{9,13},{12,4},{13,9},{2,10},{3,7},{... | collective-permute-start | bytes 393224 | tf_op jit(solution)/shard_map/ppermute | solution.py:196
  23.1 9.2 %collective-permute-start.3 = (f32[264,128]{1,0:T(8,128)S(1)}, f32[264,128]{1,0:T(8,128)S(1)}, u32[]{:S(2)}, u32[]{:S(2)}) collective-permute-start(f32[264,128]{1,0:T(8,128)S(1)} %get-tuple-element.25.rest_0_.rest_1_.rest_5_), channel_id=1, source_target_pairs={{0,2},{2,0},{1,3},{3,1},{4,6},{6,4},{5,7},{7,5},{8,10},{10,8},{9,1... | collective-permute-start | bytes 405512 | tf_op jit(solution)/shard_map/ppermute | solution.py:532
  25.8 6.5 %collective-permute-start.6 = (f32[256,128]{1,0:T(8,128)S(1)}, f32[256,128]{1,0:T(8,128)S(1)}, u32[]{:S(2)}, u32[]{:S(2)}) collective-permute-start(f32[256,128]{1,0:T(8,128)S(1)} %join.3.rest_1_.rest_2_.rest_6_), channel_id=1, source_target_pairs={{0,2},{2,0},{1,3},{3,1},{4,6},{6,4},{5,7},{7,5},{8,10},{10,8},{9,1... | collective-permute-start | bytes 393224 | tf_op jit(solution)/shard_map/ppermute | solution.py:532
  32.6 12.1 %collective-permute-start.7 = (f32[12,64,128]{2,1,0:T(8,128)S(1)}, f32[12,64,128]{2,1,0:T(8,128)S(1)}, u32[]{:S(2)}, u32[]{:S(2)}) collective-permute-start(f32[12,64,128]{2,1,0:T(8,128)S(1)} %get-tuple-element.71), channel_id=1, source_target_pairs={{1,5},{4,0},{5,9},{8,4},{9,13},{12,8},{3,7},{6,2},{7,11},{10,6},{1... | collective-permute-start | bytes 1179656 | tf_op jit(solution)/shard_map/ppermute | solution.py:505
  33.9 10.8 %collective-permute-start.8 = (f32[12,64,128]{2,1,0:T(8,128)S(1)}, f32[12,64,128]{2,1,0:T(8,128)S(1)}, u32[]{:S(2)}, u32[]{:S(2)}) collective-permute-start(f32[12,64,128]{2,1,0:T(8,128)S(1)} %get-tuple-element.70), channel_id=1, source_target_pairs={{0,4},{4,8},{5,1},{8,12},{9,5},{13,9},{2,6},{6,10},{7,3},{10,14},{... | collective-permute-start | bytes 1179656 | tf_op jit(solution)/shard_map/ppermute | solution.py:504
  44.8 3.0 %collective-permute-start.9 = (f32[40,8,128]{2,1,0:T(8,128)S(1)}, f32[40,8,128]{2,1,0:T(8,128)S(1)}, u32[]{:S(2)}, u32[]{:S(2)}) collective-permute-start(f32[40,8,128]{2,1,0:T(8,128)S(1)} %dynamic-slice_dynamic-update-slice_fusion.2), channel_id=1, source_target_pairs={{0,1},{1,0},{2,3},{3,2},{4,5},{5,4},{6,7},{7,6},{8,9},{9,8},{10,11... | collective-permute-start | bytes 491528 | tf_op jit(solution)/shard_map/ppermute | solution.py:515
  49.8 9.3 %collective-permute-start.10 = (f32[8,64,128]{2,1,0:T(8,128)S(1)}, f32[8,64,128]{2,1,0:T(8,128)S(1)}, u32[]{:S(2)}, u32[]{:S(2)}) collective-permute-start(f32[8,64,128]{2,1,0:T(8,128)S(1)} %get-tuple-element.30.rest_4_), channel_id=1, source_target_pairs={{0,4},{4,0},{5,9},{8,12},{9,5},{12,8},{2,6},{6,2},{7,11},{10,14},{... | collective-permute-start | bytes 786440 | tf_op jit(solution)/shard_map/ppermute | solution.py:493
  53.8 5.3 %collective-permute-start.11 = (f32[8,64,128]{2,1,0:T(8,128)S(1)}, f32[8,64,128]{2,1,0:T(8,128)S(1)}, u32[]{:S(2)}, u32[]{:S(2)}) collective-permute-start(f32[8,64,128]{2,1,0:T(8,128)S(1)} %get-tuple-element.30.rest_4_), channel_id=1, source_target_pairs={{1,5},{4,8},{5,1},{8,4},{9,13},{13,9},{3,7},{6,10},{7,3},{10,6},{1... | collective-permute-start | bytes 786440 | tf_op jit(solution)/shard_map/ppermute | solution.py:494
  59.2 2.6 %collective-permute-start.12 = (f32[24,8,128]{2,1,0:T(8,128)S(1)}, f32[24,8,128]{2,1,0:T(8,128)S(1)}, u32[]{:S(2)}, u32[]{:S(2)}) collective-permute-start(f32[24,8,128]{2,1,0:T(8,128)S(1)} %pad_maximum_fusion.4), channel_id=1, source_target_pairs={{0,1},{1,0},{2,3},{3,2},{4,5},{5,4},{6,7},{7,6},{8,9},{9,8},{10,11... | collective-permute-start | bytes 294920 | tf_op jit(solution)/shard_map/ppermute | solution.py:515

commit v8 on v7

--- a/solution.py
+++ b/solution.py
@@ -79,16 +79,20 @@
         slab = jnp.where(odd, section_of(away, step_bits(slabs, True)), section_of(away, step_bits(slabs, False)))
         at = first[block]
         lower = camera[block, 0] - base_level
+        landings = []
         for plane in range(planes - 1):
             upper = camera[block, plane + 1] - base_level
             lands = at + plane
             half = lands // HALF
             start = section_row(half, slab)
             here = pl.ds(pl.multiple_of(start + (lands - half * HALF) * rows, SUB), rows)
-            sums_ref[here, :] += lower_share * lower + upper_share * upper
+            landings.append((here, lower_share * lower + upper_share * upper))
             lower = upper
         counts = pl.ds(pl.multiple_of(section_row(0, slab) + HALF * rows, SUB), CZ)
-        sums_ref[counts, :] += ((count_at >= at) & (count_at < at + planes - 1)).astype(F32)
+        landings.append((counts, ((count_at >= at) & (count_at < at + planes - 1)).astype(F32)))
+        sums = [sums_ref[here, :] + value for here, value in landings]
+        for (here, _), value in zip(landings, sums):
+            sums_ref[here, :] = value
         return carry
 
     for i, copy in enumerate(parts):

time: 65 us -> 65 us (level)
  no operation moved by 1% of the time
where the time goes in v8:
time: 65 us; the launch traced here: 64.7 us
  starting transfers between devices  26.1 us (40%)
  waiting for transfers between devices  20.4 us (31%)
  Pallas kernels  9.21 us (14%)
  local copies, waits for them, and re-layouts  5.57 us (9%)
  other arithmetic  1.75 us (3%)
  between operations  1.74 us (3%)
    ppermute x5, starting transfers between devices, exchange(): return lax.ppermute(array, ('gz', 'gy'), pairs)  8.69 us
    ppermute x5, waiting for transfers between devices, exchange(): return lax.ppermute(array, ('gz', 'gy'), pairs)  5.89 us
    ppermute x2, waiting for transfers between devices, from_views(): return [message, lax.ppermute(message, 'view', [(0, 1), (1, 0)])]  4.95 us
    pallas_call x2, Pallas kernels, update(): pl.pallas_call(functools.partial(update_kernel, views=views, margin=margi...  4.92 us
    ppermute x1, starting transfers between devices, from_slabs_shifted(): lax.ppermute(sends[0], ('gz', 'gy'), gz_pairs(lambda place, odd: place -...  4.79 us
    ppermute x1, waiting for transfers between devices, from_slabs_beside(): first = lax.ppermute(sends[0], ('gz', 'gy'), ahead)  4.62 us
    ppermute x1, starting transfers between devices, from_slabs_beside(): first = lax.ppermute(sends[0], ('gz', 'gy'), ahead)  3.92 us
    unnamed x18, local copies, waits for them, and re-layouts  3.7 us
  transfers between devices with their start and end apart: 13, of which 8 were waited for; matrix products, arithmetic and copies ran while one was open for 5% of the time, Pallas kernels for 2%

profile of v8, /device:TPU:0, one launch (start us, length us, event | category | flops | bytes accessed | tf_op | source)
XLA Modules:
  0.0 64.7 jit_solution(2696096564781331717)
XLA Ops:
  1.3 3.0 %deposit.1 = (f32[264,128]{1,0:T(8,128)}, f32[264,128]{1,0:T(8,128)}, f32[264,128]{1,0:T(8,128)}, f32[256,128]{1,0:T(8,128)}, f32[256,128]{1,0:T(8,128)}, /*index=5*/f32[256,128]{1,0:T(8,128)}, f32[520,128]{1,0:T(8,128)}) custom-call(s32[32]{0:T(128)} %bitcast.50, s32[32]{0:T(128)} %bitcast.51, s32[1]{0:T(128)} %bitcast.31.level_hbm, f32[3]{0:T(128)} %bitcast.52, ...), custom_call_target="tpu_custom_call" | custom-call | tf_op jit(solution)/shard_map/deposit/pallas_call | solution.py:111
  4.3 3.1 %collective-permute-start.1 = (f32[520,128]{1,0:T(8,128)}, f32[520,128]{1,0:T(8,128)S(1)}, u32[]{:S(2)}, u32[]{:S(2)}) collective-permute-start(f32[520,128]{1,0:T(8,128)} %get-tuple-element.24), channel_id=1, source_target_pairs={{0,4},{1,9},{4,0},{5,13},{8,12},{9,1},{12,8},{13,5},{2,6},{3,11},{... | collective-permute-start | bytes 798728 | tf_op jit(solution)/shard_map/ppermute | solution.py:200
  7.5 1.9 %collective-permute-start.4 = (f32[256,128]{1,0:T(8,128)}, f32[256,128]{1,0:T(8,128)S(1)}, u32[]{:S(2)}, u32[]{:S(2)}) collective-permute-start(f32[256,128]{1,0:T(8,128)} %get-tuple-element.28), channel_id=1, source_target_pairs={{0,4},{1,9},{4,0},{5,13},{8,12},{9,1},{12,8},{13,5},{2,6},{3,11},{... | collective-permute-start | bytes 393224 | tf_op jit(solution)/shard_map/ppermute | solution.py:200
  10.0 0.9 %copy-done = f32[264,128]{1,0:T(8,128)S(1)} copy-done((f32[264,128]{1,0:T(8,128)S(1)}, f32[264,128]{1,0:T(8,128)}, u32[]{:S(2)}) %copy-start) | copy-done | bytes 135192
  10.9 0.9 %copy-done.1 = f32[264,128]{1,0:T(8,128)S(1)} copy-done((f32[264,128]{1,0:T(8,128)S(1)}, f32[264,128]{1,0:T(8,128)}, u32[]{:S(2)}) %copy-start.1) | copy-done | bytes 135192
  11.8 0.9 %copy-done.2 = f32[256,128]{1,0:T(8,128)S(1)} copy-done((f32[256,128]{1,0:T(8,128)S(1)}, f32[256,128]{1,0:T(8,128)}, u32[]{:S(2)}) %copy-start.2) | copy-done | bytes 131096
  12.7 0.9 %copy-done.3 = f32[256,128]{1,0:T(8,128)S(1)} copy-done((f32[256,128]{1,0:T(8,128)S(1)}, f32[256,128]{1,0:T(8,128)}, u32[]{:S(2)}) %copy-start.3) | copy-done | bytes 131096
  13.6 0.7 %fetch.1 = (f32[264,128]{1,0:T(8,128)S(1)}, f32[256,128]{1,0:T(8,128)S(1)}, f32[264,128]{1,0:T(8,128)S(1)}, f32[256,128]{1,0:T(8,128)S(1)}) custom-call(f32[264,128]{1,0:T(8,128)S(1)} %copy-done.1, f32[256,128]{1,0:T(8,128)S(1)} %copy-done.3, f32[264,128]{1,0:T(8,128)S(1)} %copy-done, f32[256,128]{1,0:T(8,128)S(1)} %copy-done.2), custom_call_target="tpu_custom_call" | custom-call | tf_op jit(solution)/shard_map/fetch/pallas_call | solution.py:163
  14.6 3.5 %collective-permute-start.2 = (f32[264,128]{1,0:T(8,128)S(1)}, f32[264,128]{1,0:T(8,128)S(1)}, u32[]{:S(2)}, u32[]{:S(2)}) collective-permute-start(f32[264,128]{1,0:T(8,128)S(1)} %add.519), channel_id=1, source_target_pairs={{0,8},{1,5},{4,12},{5,1},{8,0},{9,13},{12,4},{13,9},{2,10},{3,7},{... | collective-permute-start | bytes 405512 | tf_op jit(solution)/shard_map/ppermute | solution.py:200
  18.3 4.7 %collective-permute-done.2.rest_2_ = f32[264,128]{1,0:T(8,128)S(1)} collective-permute-done((f32[264,128]{1,0:T(8,128)S(1)}, f32[264,128]{1,0:T(8,128)S(1)}, u32[]{:S(2)}, u32[]{:S(2)}) %collective-permute-start.2) | collective-permute-done | bytes 135200 | tf_op jit(solution)/shard_map/ppermute | solution.py:200
  23.1 1.6 %collective-permute-start.3 = (f32[264,128]{1,0:T(8,128)S(1)}, f32[264,128]{1,0:T(8,128)S(1)}, u32[]{:S(2)}, u32[]{:S(2)}) collective-permute-start(f32[264,128]{1,0:T(8,128)S(1)} %get-tuple-element.25.rest_0_.rest_1_.rest_5_), channel_id=1, source_target_pairs={{0,2},{2,0},{1,3},{3,1},{4,6},{6,4},{5,7},{7,5},{8,10},{10,8},{9,1... | collective-permute-start | bytes 405512 | tf_op jit(solution)/shard_map/ppermute | solution.py:536
  24.7 1.0 %collective-permute-done.5.rest_3_ = f32[256,128]{1,0:T(8,128)S(1)} collective-permute-done((f32[256,128]{1,0:T(8,128)S(1)}, f32[256,128]{1,0:T(8,128)S(1)}, u32[]{:S(2)}, u32[]{:S(2)}) %collective-permute-start.5) | collective-permute-done | bytes 131104 | tf_op jit(solution)/shard_map/ppermute | solution.py:200
  25.8 1.6 %collective-permute-start.6 = (f32[256,128]{1,0:T(8,128)S(1)}, f32[256,128]{1,0:T(8,128)S(1)}, u32[]{:S(2)}, u32[]{:S(2)}) collective-permute-start(f32[256,128]{1,0:T(8,128)S(1)} %join.3.rest_1_.rest_2_.rest_6_), channel_id=1, source_target_pairs={{0,2},{2,0},{1,3},{3,1},{4,6},{6,4},{5,7},{7,5},{8,10},{10,8},{9,1... | collective-permute-start | bytes 393224 | tf_op jit(solution)/shard_map/ppermute | solution.py:536
  27.4 4.9 %collective-permute-done.6.rest_3_.rest_4_ = f32[256,128]{1,0:T(8,128)S(1)} collective-permute-done((f32[256,128]{1,0:T(8,128)S(1)}, f32[256,128]{1,0:T(8,128)S(1)}, u32[]{:S(2)}, u32[]{:S(2)}) %collective-permute-start.6) | collective-permute-done | bytes 131104 | tf_op jit(solution)/shard_map/ppermute | solution.py:536
  32.6 1.3 %collective-permute-start.7 = (f32[12,64,128]{2,1,0:T(8,128)S(1)}, f32[12,64,128]{2,1,0:T(8,128)S(1)}, u32[]{:S(2)}, u32[]{:S(2)}) collective-permute-start(f32[12,64,128]{2,1,0:T(8,128)S(1)} %get-tuple-element.71), channel_id=1, source_target_pairs={{1,5},{4,0},{5,9},{8,4},{9,13},{12,8},{3,7},{6,2},{7,11},{10,6},{1... | collective-permute-start | bytes 1179656 | tf_op jit(solution)/shard_map/ppermute | solution.py:509
  33.9 4.8 %collective-permute-start.8 = (f32[12,64,128]{2,1,0:T(8,128)S(1)}, f32[12,64,128]{2,1,0:T(8,128)S(1)}, u32[]{:S(2)}, u32[]{:S(2)}) collective-permute-start(f32[12,64,128]{2,1,0:T(8,128)S(1)} %get-tuple-element.70), channel_id=1, source_target_pairs={{0,4},{4,8},{5,1},{8,12},{9,5},{13,9},{2,6},{6,10},{7,3},{10,14},{... | collective-permute-start | bytes 1179656 | tf_op jit(solution)/shard_map/ppermute | solution.py:508
  38.8 0.3 slice_reduce_fusion.18
  39.2 0.3 slice_reduce_fusion.36
  39.5 0.3 slice_reduce_fusion.27
  40.3 0.2 select_add_fusion.1
  40.5 0.3 slice_reduce_fusion.9
  41.2 3.5 %collective-permute-done.7 = f32[12,64,128]{2,1,0:T(8,128)S(1)} collective-permute-done((f32[12,64,128]{2,1,0:T(8,128)S(1)}, f32[12,64,128]{2,1,0:T(8,128)S(1)}, u32[]{:S(2)}, u32[]{:S(2)}) %collective-permute-start.7) | collective-permute-done | bytes 393248 | tf_op jit(solution)/shard_map/ppermute | solution.py:509
  44.8 1.9 %collective-permute-start.9 = (f32[40,8,128]{2,1,0:T(8,128)S(1)}, f32[40,8,128]{2,1,0:T(8,128)S(1)}, u32[]{:S(2)}, u32[]{:S(2)}) collective-permute-start(f32[40,8,128]{2,1,0:T(8,128)S(1)} %dynamic-slice_dynamic-update-slice_fusion.2), channel_id=1, source_target_pairs={{0,1},{1,0},{2,3},{3,2},{4,5},{5,4},{6,7},{7,6},{8,9},{9,8},{10,11... | collective-permute-start | bytes 491528 | tf_op jit(solution)/shard_map/ppermute | solution.py:519
  46.9 0.3 prepare.1.rest_0_
  47.3 0.5 collective-permute-done.9.low_rows_ref.high_rows_ref
  47.8 2.0 %update.2 = (f32[8,64,128]{2,1,0:T(8,128)S(1)}, f32[512,128]{1,0:T(8,128)}) custom-call(f32[20,8,128]{2,1,0:T(8,128)S(1)} %broadcast_in_dim.439.weight_ref, bf16[2,2,80,240]{3,2,1,0:T(8,128)(2,1)S(1)} %pad_maximum_fusion.3.row_band_ref, bf16[2,2,256,256]{3,2,1,0:T(8,128)(2,1)S(1)} %maximum_maximum_fusion.col_band_ref, ...), custom_call_target="tpu_custom_call" | custom-call | tf_op jit(solution)/shard_map/update/pallas_call | solution.py:471
  49.8 3.9 %collective-permute-start.10 = (f32[8,64,128]{2,1,0:T(8,128)S(1)}, f32[8,64,128]{2,1,0:T(8,128)S(1)}, u32[]{:S(2)}, u32[]{:S(2)}) collective-permute-start(f32[8,64,128]{2,1,0:T(8,128)S(1)} %get-tuple-element.30.rest_4_), channel_id=1, source_target_pairs={{0,4},{4,0},{5,9},{8,12},{9,5},{12,8},{2,6},{6,2},{7,11},{10,14},{... | collective-permute-start | bytes 786440 | tf_op jit(solution)/shard_map/ppermute | solution.py:497
  53.8 0.7 %collective-permute-start.11 = (f32[8,64,128]{2,1,0:T(8,128)S(1)}, f32[8,64,128]{2,1,0:T(8,128)S(1)}, u32[]{:S(2)}, u32[]{:S(2)}) collective-permute-start(f32[8,64,128]{2,1,0:T(8,128)S(1)} %get-tuple-element.30.rest_4_), channel_id=1, source_target_pairs={{1,5},{4,8},{5,1},{8,4},{9,13},{13,9},{3,7},{6,10},{7,3},{10,6},{1... | collective-permute-start | bytes 786440 | tf_op jit(solution)/shard_map/ppermute | solution.py:498
  54.5 4.6 %collective-permute-done.10 = f32[8,64,128]{2,1,0:T(8,128)S(1)} collective-permute-done((f32[8,64,128]{2,1,0:T(8,128)S(1)}, f32[8,64,128]{2,1,0:T(8,128)S(1)}, u32[]{:S(2)}, u32[]{:S(2)}) %collective-permute-start.10) | collective-permute-done | bytes 262176 | tf_op jit(solution)/shard_map/ppermute | solution.py:497
  59.2 1.7 %collective-permute-start.12 = (f32[24,8,128]{2,1,0:T(8,128)S(1)}, f32[24,8,128]{2,1,0:T(8,128)S(1)}, u32[]{:S(2)}, u32[]{:S(2)}) collective-permute-start(f32[24,8,128]{2,1,0:T(8,128)S(1)} %pad_maximum_fusion.4), channel_id=1, source_target_pairs={{0,1},{1,0},{2,3},{3,2},{4,5},{5,4},{6,7},{7,6},{8,9},{9,8},{10,11... | collective-permute-start | bytes 294920 | tf_op jit(solution)/shard_map/ppermute | solution.py:519
  60.9 0.9 %collective-permute-done.12.rest_7_.rest_8_ = f32[24,8,128]{2,1,0:T(8,128)S(1)} collective-permute-done((f32[24,8,128]{2,1,0:T(8,128)S(1)}, f32[24,8,128]{2,1,0:T(8,128)S(1)}, u32[]{:S(2)}, u32[]{:S(2)}) %collective-permute-start.12) | collective-permute-done | bytes 98336 | tf_op jit(solution)/shard_map/ppermute | solution.py:519
  61.8 2.9 %update.3 = f32[8,64,128]{2,1,0:T(8,128)} custom-call(f32[20,8,128]{2,1,0:T(8,128)S(1)} %broadcast_in_dim.439.weight_ref, bf16[2,2,80,240]{3,2,1,0:T(8,128)(2,1)S(1)} %pad_maximum_fusion.3.row_band_ref, bf16[2,2,256,256]{3,2,1,0:T(8,128)(2,1)S(1)} %maximum_maximum_fusion.col_band_ref, f32[12,64,128]{2,1,0:T(8,128)S(1)} %get-tuple-element.69.below_ref, ...), custom_call_target="tpu_custom_call" | custom-call | tf_op jit(solution)/shard_map/update/pallas_call | solution.py:471
  (72 shorter events, 2.9 us)
Async XLA Ops:
  0.6 8.8 %copy-start.5 = (f32[1,3]{1,0:T(1,128)S(1)}, f32[1,3]{1,0:T(1,128)}, u32[]{:S(2)}) copy-start(f32[1,3]{1,0:T(1,128)} %param.10) | copy-start | bytes 40
  0.6 9.1 %copy-start.4 = (f32[1,3,9]{2,0,1:T(1,128)S(1)}, f32[1,3,9]{2,0,1:T(1,128)}, u32[]{:S(2)}) copy-start(f32[1,3,9]{2,0,1:T(1,128)} %param.11) | copy-start | bytes 328
  4.3 10.2 %collective-permute-start.1 = (f32[520,128]{1,0:T(8,128)}, f32[520,128]{1,0:T(8,128)S(1)}, u32[]{:S(2)}, u32[]{:S(2)}) collective-permute-start(f32[520,128]{1,0:T(8,128)} %get-tuple-element.24), channel_id=1, source_target_pairs={{0,4},{1,9},{4,0},{5,13},{8,12},{9,1},{12,8},{13,5},{2,6},{3,11},{... | collective-permute-start | bytes 798728 | tf_op jit(solution)/shard_map/ppermute | solution.py:200
  7.4 10.9 %collective-permute-start = (f32[264,128]{1,0:T(8,128)}, f32[264,128]{1,0:T(8,128)S(1)}, u32[]{:S(2)}, u32[]{:S(2)}) collective-permute-start(f32[264,128]{1,0:T(8,128)} %get-tuple-element.22), channel_id=1, source_target_pairs={{0,4},{1,9},{4,0},{5,13},{8,12},{9,1},{12,8},{13,5},{2,6},{3,11},{... | collective-permute-start | bytes 405512 | tf_op jit(solution)/shard_map/ppermute | solution.py:200
  7.5 17.2 %collective-permute-start.4 = (f32[256,128]{1,0:T(8,128)}, f32[256,128]{1,0:T(8,128)S(1)}, u32[]{:S(2)}, u32[]{:S(2)}) collective-permute-start(f32[256,128]{1,0:T(8,128)} %get-tuple-element.28), channel_id=1, source_target_pairs={{0,4},{1,9},{4,0},{5,13},{8,12},{9,1},{12,8},{13,5},{2,6},{3,11},{... | collective-permute-start | bytes 393224 | tf_op jit(solution)/shard_map/ppermute | solution.py:200
  10.0 0.9 %copy-start = (f32[264,128]{1,0:T(8,128)S(1)}, f32[264,128]{1,0:T(8,128)}, u32[]{:S(2)}) copy-start(f32[264,128]{1,0:T(8,128)} %get-tuple-element.19.refs_2_) | copy-start | bytes 405508
  10.9 0.9 %copy-start.1 = (f32[264,128]{1,0:T(8,128)S(1)}, f32[264,128]{1,0:T(8,128)}, u32[]{:S(2)}) copy-start(f32[264,128]{1,0:T(8,128)} %get-tuple-element.17.refs_0_) | copy-start | bytes 405508
  11.8 0.9 %copy-start.2 = (f32[256,128]{1,0:T(8,128)S(1)}, f32[256,128]{1,0:T(8,128)}, u32[]{:S(2)}) copy-start(f32[256,128]{1,0:T(8,128)} %get-tuple-element.20.refs_3_) | copy-start | bytes 393220
  12.7 0.9 %copy-start.3 = (f32[256,128]{1,0:T(8,128)S(1)}, f32[256,128]{1,0:T(8,128)}, u32[]{:S(2)}) copy-start(f32[256,128]{1,0:T(8,128)} %get-tuple-element.18.refs_1_) | copy-start | bytes 393220
  14.6 8.5 %collective-permute-start.2 = (f32[264,128]{1,0:T(8,128)S(1)}, f32[264,128]{1,0:T(8,128)S(1)}, u32[]{:S(2)}, u32[]{:S(2)}) collective-permute-start(f32[264,128]{1,0:T(8,128)S(1)} %add.519), channel_id=1, source_target_pairs={{0,8},{1,5},{4,12},{5,1},{8,0},{9,13},{12,4},{13,9},{2,10},{3,7},{... | collective-permute-start | bytes 405512 | tf_op jit(solution)/shard_map/ppermute | solution.py:200
  18.1 7.6 %collective-permute-start.5 = (f32[256,128]{1,0:T(8,128)S(1)}, f32[256,128]{1,0:T(8,128)S(1)}, u32[]{:S(2)}, u32[]{:S(2)}) collective-permute-start(f32[256,128]{1,0:T(8,128)S(1)} %add.520), channel_id=1, source_target_pairs={{0,8},{1,5},{4,12},{5,1},{8,0},{9,13},{12,4},{13,9},{2,10},{3,7},{... | collective-permute-start | bytes 393224 | tf_op jit(solution)/shard_map/ppermute | solution.py:200
  23.1 9.2 %collective-permute-start.3 = (f32[264,128]{1,0:T(8,128)S(1)}, f32[264,128]{1,0:T(8,128)S(1)}, u32[]{:S(2)}, u32[]{:S(2)}) collective-permute-start(f32[264,128]{1,0:T(8,128)S(1)} %get-tuple-element.25.rest_0_.rest_1_.rest_5_), channel_id=1, source_target_pairs={{0,2},{2,0},{1,3},{3,1},{4,6},{6,4},{5,7},{7,5},{8,10},{10,8},{9,1... | collective-permute-start | bytes 405512 | tf_op jit(solution)/shard_map/ppermute | solution.py:536
  25.8 6.5 %collective-permute-start.6 = (f32[256,128]{1,0:T(8,128)S(1)}, f32[256,128]{1,0:T(8,128)S(1)}, u32[]{:S(2)}, u32[]{:S(2)}) collective-permute-start(f32[256,128]{1,0:T(8,128)S(1)} %join.3.rest_1_.rest_2_.rest_6_), channel_id=1, source_target_pairs={{0,2},{2,0},{1,3},{3,1},{4,6},{6,4},{5,7},{7,5},{8,10},{10,8},{9,1... | collective-permute-start | bytes 393224 | tf_op jit(solution)/shard_map/ppermute | solution.py:536
  32.6 12.1 %collective-permute-start.7 = (f32[12,64,128]{2,1,0:T(8,128)S(1)}, f32[12,64,128]{2,1,0:T(8,128)S(1)}, u32[]{:S(2)}, u32[]{:S(2)}) collective-permute-start(f32[12,64,128]{2,1,0:T(8,128)S(1)} %get-tuple-element.71), channel_id=1, source_target_pairs={{1,5},{4,0},{5,9},{8,4},{9,13},{12,8},{3,7},{6,2},{7,11},{10,6},{1... | collective-permute-start | bytes 1179656 | tf_op jit(solution)/shard_map/ppermute | solution.py:509
  33.9 10.8 %collective-permute-start.8 = (f32[12,64,128]{2,1,0:T(8,128)S(1)}, f32[12,64,128]{2,1,0:T(8,128)S(1)}, u32[]{:S(2)}, u32[]{:S(2)}) collective-permute-start(f32[12,64,128]{2,1,0:T(8,128)S(1)} %get-tuple-element.70), channel_id=1, source_target_pairs={{0,4},{4,8},{5,1},{8,12},{9,5},{13,9},{2,6},{6,10},{7,3},{10,14},{... | collective-permute-start | bytes 1179656 | tf_op jit(solution)/shard_map/ppermute | solution.py:508
  44.8 3.0 %collective-permute-start.9 = (f32[40,8,128]{2,1,0:T(8,128)S(1)}, f32[40,8,128]{2,1,0:T(8,128)S(1)}, u32[]{:S(2)}, u32[]{:S(2)}) collective-permute-start(f32[40,8,128]{2,1,0:T(8,128)S(1)} %dynamic-slice_dynamic-update-slice_fusion.2), channel_id=1, source_target_pairs={{0,1},{1,0},{2,3},{3,2},{4,5},{5,4},{6,7},{7,6},{8,9},{9,8},{10,11... | collective-permute-start | bytes 491528 | tf_op jit(solution)/shard_map/ppermute | solution.py:519
  49.8 9.3 %collective-permute-start.10 = (f32[8,64,128]{2,1,0:T(8,128)S(1)}, f32[8,64,128]{2,1,0:T(8,128)S(1)}, u32[]{:S(2)}, u32[]{:S(2)}) collective-permute-start(f32[8,64,128]{2,1,0:T(8,128)S(1)} %get-tuple-element.30.rest_4_), channel_id=1, source_target_pairs={{0,4},{4,0},{5,9},{8,12},{9,5},{12,8},{2,6},{6,2},{7,11},{10,14},{... | collective-permute-start | bytes 786440 | tf_op jit(solution)/shard_map/ppermute | solution.py:497
  53.8 5.3 %collective-permute-start.11 = (f32[8,64,128]{2,1,0:T(8,128)S(1)}, f32[8,64,128]{2,1,0:T(8,128)S(1)}, u32[]{:S(2)}, u32[]{:S(2)}) collective-permute-start(f32[8,64,128]{2,1,0:T(8,128)S(1)} %get-tuple-element.30.rest_4_), channel_id=1, source_target_pairs={{1,5},{4,8},{5,1},{8,4},{9,13},{13,9},{3,7},{6,10},{7,3},{10,6},{1... | collective-permute-start | bytes 786440 | tf_op jit(solution)/shard_map/ppermute | solution.py:498
  59.2 2.6 %collective-permute-start.12 = (f32[24,8,128]{2,1,0:T(8,128)S(1)}, f32[24,8,128]{2,1,0:T(8,128)S(1)}, u32[]{:S(2)}, u32[]{:S(2)}) collective-permute-start(f32[24,8,128]{2,1,0:T(8,128)S(1)} %pad_maximum_fusion.4), channel_id=1, source_target_pairs={{0,1},{1,0},{2,3},{3,2},{4,5},{5,4},{6,7},{7,6},{8,9},{9,8},{10,11... | collective-permute-start | bytes 294920 | tf_op jit(solution)/shard_map/ppermute | solution.py:519

commit v9 on v8

--- a/solution.py
+++ b/solution.py
@@ -241,7 +241,7 @@
         part = (1.0 - fy) * part + fy * follow
         follow = jnp.where(col_at == cols - 1, part, pltpu.roll(part, cols - 1, 1))
         part = (1.0 - fx) * part + fx * follow
-        part = jnp.maximum(part / (counts[plane : plane + 1] + 1.0), DATA_FLOOR)
+        part = jnp.maximum(part * (1.0 / (counts[plane : plane + 1] + 1.0)), DATA_FLOOR)
         message_ref[plane * rows : (plane + 1) * rows] = part
     if half == 0:
         message_ref[HALF * rows :] = small_ref[...]

time: 65 us -> 65 us (level)
  no operation moved by 1% of the time
where the time goes in v9:
time: 65 us; the launch traced here: 64.7 us
  starting transfers between devices  26.1 us (40%)
  waiting for transfers between devices  20.4 us (31%)
  Pallas kernels  9.21 us (14%)
  local copies, waits for them, and re-layouts  5.57 us (9%)
  other arithmetic  1.75 us (3%)
  between operations  1.74 us (3%)
    ppermute x5, starting transfers between devices, exchange(): return lax.ppermute(array, ('gz', 'gy'), pairs)  8.68 us
    ppermute x5, waiting for transfers between devices, exchange(): return lax.ppermute(array, ('gz', 'gy'), pairs)  5.9 us
    ppermute x2, waiting for transfers between devices, from_views(): return [message, lax.ppermute(message, 'view', [(0, 1), (1, 0)])]  4.95 us
    pallas_call x2, Pallas kernels, update(): pl.pallas_call(functools.partial(update_kernel, views=views, margin=margi...  4.92 us
    ppermute x1, starting transfers between devices, from_slabs_shifted(): lax.ppermute(sends[0], ('gz', 'gy'), gz_pairs(lambda place, odd: place -...  4.78 us
    ppermute x1, waiting for transfers between devices, from_slabs_beside(): first = lax.ppermute(sends[0], ('gz', 'gy'), ahead)  4.62 us
    ppermute x1, starting transfers between devices, from_slabs_beside(): first = lax.ppermute(sends[0], ('gz', 'gy'), ahead)  3.92 us
    unnamed x18, local copies, waits for them, and re-layouts  3.7 us
  transfers between devices with their start and end apart: 13, of which 8 were waited for; matrix products, arithmetic and copies ran while one was open for 5% of the time, Pallas kernels for 2%

profile of v9, /device:TPU:0, one launch (start us, length us, event | category | flops | bytes accessed | tf_op | source)
XLA Modules:
  0.0 64.7 jit_solution(17721513207756876813)
XLA Ops:
  1.3 3.0 %deposit.1 = (f32[264,128]{1,0:T(8,128)}, f32[264,128]{1,0:T(8,128)}, f32[264,128]{1,0:T(8,128)}, f32[256,128]{1,0:T(8,128)}, f32[256,128]{1,0:T(8,128)}, /*index=5*/f32[256,128]{1,0:T(8,128)}, f32[520,128]{1,0:T(8,128)}) custom-call(s32[32]{0:T(128)} %bitcast.50, s32[32]{0:T(128)} %bitcast.51, s32[1]{0:T(128)} %bitcast.31.level_hbm, f32[3]{0:T(128)} %bitcast.52, ...), custom_call_target="tpu_custom_call" | custom-call | tf_op jit(solution)/shard_map/deposit/pallas_call | solution.py:111
  4.3 3.1 %collective-permute-start.1 = (f32[520,128]{1,0:T(8,128)}, f32[520,128]{1,0:T(8,128)S(1)}, u32[]{:S(2)}, u32[]{:S(2)}) collective-permute-start(f32[520,128]{1,0:T(8,128)} %get-tuple-element.24), channel_id=1, source_target_pairs={{0,4},{1,9},{4,0},{5,13},{8,12},{9,1},{12,8},{13,5},{2,6},{3,11},{... | collective-permute-start | bytes 798728 | tf_op jit(solution)/shard_map/ppermute | solution.py:200
  7.5 1.9 %collective-permute-start.4 = (f32[256,128]{1,0:T(8,128)}, f32[256,128]{1,0:T(8,128)S(1)}, u32[]{:S(2)}, u32[]{:S(2)}) collective-permute-start(f32[256,128]{1,0:T(8,128)} %get-tuple-element.28), channel_id=1, source_target_pairs={{0,4},{1,9},{4,0},{5,13},{8,12},{9,1},{12,8},{13,5},{2,6},{3,11},{... | collective-permute-start | bytes 393224 | tf_op jit(solution)/shard_map/ppermute | solution.py:200
  10.0 0.9 %copy-done = f32[264,128]{1,0:T(8,128)S(1)} copy-done((f32[264,128]{1,0:T(8,128)S(1)}, f32[264,128]{1,0:T(8,128)}, u32[]{:S(2)}) %copy-start) | copy-done | bytes 135192
  10.9 0.9 %copy-done.1 = f32[264,128]{1,0:T(8,128)S(1)} copy-done((f32[264,128]{1,0:T(8,128)S(1)}, f32[264,128]{1,0:T(8,128)}, u32[]{:S(2)}) %copy-start.1) | copy-done | bytes 135192
  11.8 0.9 %copy-done.2 = f32[256,128]{1,0:T(8,128)S(1)} copy-done((f32[256,128]{1,0:T(8,128)S(1)}, f32[256,128]{1,0:T(8,128)}, u32[]{:S(2)}) %copy-start.2) | copy-done | bytes 131096
  12.7 0.9 %copy-done.3 = f32[256,128]{1,0:T(8,128)S(1)} copy-done((f32[256,128]{1,0:T(8,128)S(1)}, f32[256,128]{1,0:T(8,128)}, u32[]{:S(2)}) %copy-start.3) | copy-done | bytes 131096
  13.6 0.7 %fetch.1 = (f32[264,128]{1,0:T(8,128)S(1)}, f32[256,128]{1,0:T(8,128)S(1)}, f32[264,128]{1,0:T(8,128)S(1)}, f32[256,128]{1,0:T(8,128)S(1)}) custom-call(f32[264,128]{1,0:T(8,128)S(1)} %copy-done.1, f32[256,128]{1,0:T(8,128)S(1)} %copy-done.3, f32[264,128]{1,0:T(8,128)S(1)} %copy-done, f32[256,128]{1,0:T(8,128)S(1)} %copy-done.2), custom_call_target="tpu_custom_call" | custom-call | tf_op jit(solution)/shard_map/fetch/pallas_call | solution.py:163
  14.6 3.5 %collective-permute-start.2 = (f32[264,128]{1,0:T(8,128)S(1)}, f32[264,128]{1,0:T(8,128)S(1)}, u32[]{:S(2)}, u32[]{:S(2)}) collective-permute-start(f32[264,128]{1,0:T(8,128)S(1)} %add.519), channel_id=1, source_target_pairs={{0,8},{1,5},{4,12},{5,1},{8,0},{9,13},{12,4},{13,9},{2,10},{3,7},{... | collective-permute-start | bytes 405512 | tf_op jit(solution)/shard_map/ppermute | solution.py:200
  18.3 4.7 %collective-permute-done.2.rest_2_ = f32[264,128]{1,0:T(8,128)S(1)} collective-permute-done((f32[264,128]{1,0:T(8,128)S(1)}, f32[264,128]{1,0:T(8,128)S(1)}, u32[]{:S(2)}, u32[]{:S(2)}) %collective-permute-start.2) | collective-permute-done | bytes 135200 | tf_op jit(solution)/shard_map/ppermute | solution.py:200
  23.1 1.6 %collective-permute-start.3 = (f32[264,128]{1,0:T(8,128)S(1)}, f32[264,128]{1,0:T(8,128)S(1)}, u32[]{:S(2)}, u32[]{:S(2)}) collective-permute-start(f32[264,128]{1,0:T(8,128)S(1)} %get-tuple-element.25.rest_0_.rest_1_.rest_5_), channel_id=1, source_target_pairs={{0,2},{2,0},{1,3},{3,1},{4,6},{6,4},{5,7},{7,5},{8,10},{10,8},{9,1... | collective-permute-start | bytes 405512 | tf_op jit(solution)/shard_map/ppermute | solution.py:536
  24.7 1.0 %collective-permute-done.5.rest_3_ = f32[256,128]{1,0:T(8,128)S(1)} collective-permute-done((f32[256,128]{1,0:T(8,128)S(1)}, f32[256,128]{1,0:T(8,128)S(1)}, u32[]{:S(2)}, u32[]{:S(2)}) %collective-permute-start.5) | collective-permute-done | bytes 131104 | tf_op jit(solution)/shard_map/ppermute | solution.py:200
  25.8 1.6 %collective-permute-start.6 = (f32[256,128]{1,0:T(8,128)S(1)}, f32[256,128]{1,0:T(8,128)S(1)}, u32[]{:S(2)}, u32[]{:S(2)}) collective-permute-start(f32[256,128]{1,0:T(8,128)S(1)} %join.3.rest_1_.rest_2_.rest_6_), channel_id=1, source_target_pairs={{0,2},{2,0},{1,3},{3,1},{4,6},{6,4},{5,7},{7,5},{8,10},{10,8},{9,1... | collective-permute-start | bytes 393224 | tf_op jit(solution)/shard_map/ppermute | solution.py:536
  27.4 4.9 %collective-permute-done.6.rest_3_.rest_4_ = f32[256,128]{1,0:T(8,128)S(1)} collective-permute-done((f32[256,128]{1,0:T(8,128)S(1)}, f32[256,128]{1,0:T(8,128)S(1)}, u32[]{:S(2)}, u32[]{:S(2)}) %collective-permute-start.6) | collective-permute-done | bytes 131104 | tf_op jit(solution)/shard_map/ppermute | solution.py:536
  32.6 1.3 %collective-permute-start.7 = (f32[12,64,128]{2,1,0:T(8,128)S(1)}, f32[12,64,128]{2,1,0:T(8,128)S(1)}, u32[]{:S(2)}, u32[]{:S(2)}) collective-permute-start(f32[12,64,128]{2,1,0:T(8,128)S(1)} %get-tuple-element.71), channel_id=1, source_target_pairs={{1,5},{4,0},{5,9},{8,4},{9,13},{12,8},{3,7},{6,2},{7,11},{10,6},{1... | collective-permute-start | bytes 1179656 | tf_op jit(solution)/shard_map/ppermute | solution.py:509
  33.9 4.8 %collective-permute-start.8 = (f32[12,64,128]{2,1,0:T(8,128)S(1)}, f32[12,64,128]{2,1,0:T(8,128)S(1)}, u32[]{:S(2)}, u32[]{:S(2)}) collective-permute-start(f32[12,64,128]{2,1,0:T(8,128)S(1)} %get-tuple-element.70), channel_id=1, source_target_pairs={{0,4},{4,8},{5,1},{8,12},{9,5},{13,9},{2,6},{6,10},{7,3},{10,14},{... | collective-permute-start | bytes 1179656 | tf_op jit(solution)/shard_map/ppermute | solution.py:508
  38.8 0.3 slice_reduce_fusion.18
  39.2 0.3 slice_reduce_fusion.36
  39.5 0.3 slice_reduce_fusion.27
  40.3 0.2 select_add_fusion.1
  40.5 0.3 slice_reduce_fusion.9
  41.2 3.5 %collective-permute-done.7 = f32[12,64,128]{2,1,0:T(8,128)S(1)} collective-permute-done((f32[12,64,128]{2,1,0:T(8,128)S(1)}, f32[12,64,128]{2,1,0:T(8,128)S(1)}, u32[]{:S(2)}, u32[]{:S(2)}) %collective-permute-start.7) | collective-permute-done | bytes 393248 | tf_op jit(solution)/shard_map/ppermute | solution.py:509
  44.8 1.9 %collective-permute-start.9 = (f32[40,8,128]{2,1,0:T(8,128)S(1)}, f32[40,8,128]{2,1,0:T(8,128)S(1)}, u32[]{:S(2)}, u32[]{:S(2)}) collective-permute-start(f32[40,8,128]{2,1,0:T(8,128)S(1)} %dynamic-slice_dynamic-update-slice_fusion.2), channel_id=1, source_target_pairs={{0,1},{1,0},{2,3},{3,2},{4,5},{5,4},{6,7},{7,6},{8,9},{9,8},{10,11... | collective-permute-start | bytes 491528 | tf_op jit(solution)/shard_map/ppermute | solution.py:519
  46.9 0.3 prepare.1.rest_0_
  47.3 0.5 collective-permute-done.9.low_rows_ref.high_rows_ref
  47.8 2.0 %update.2 = (f32[8,64,128]{2,1,0:T(8,128)S(1)}, f32[512,128]{1,0:T(8,128)}) custom-call(f32[20,8,128]{2,1,0:T(8,128)S(1)} %broadcast_in_dim.439.weight_ref, bf16[2,2,80,240]{3,2,1,0:T(8,128)(2,1)S(1)} %pad_maximum_fusion.3.row_band_ref, bf16[2,2,256,256]{3,2,1,0:T(8,128)(2,1)S(1)} %maximum_maximum_fusion.col_band_ref, ...), custom_call_target="tpu_custom_call" | custom-call | tf_op jit(solution)/shard_map/update/pallas_call | solution.py:471
  49.8 3.9 %collective-permute-start.10 = (f32[8,64,128]{2,1,0:T(8,128)S(1)}, f32[8,64,128]{2,1,0:T(8,128)S(1)}, u32[]{:S(2)}, u32[]{:S(2)}) collective-permute-start(f32[8,64,128]{2,1,0:T(8,128)S(1)} %get-tuple-element.30.rest_4_), channel_id=1, source_target_pairs={{0,4},{4,0},{5,9},{8,12},{9,5},{12,8},{2,6},{6,2},{7,11},{10,14},{... | collective-permute-start | bytes 786440 | tf_op jit(solution)/shard_map/ppermute | solution.py:497
  53.8 0.7 %collective-permute-start.11 = (f32[8,64,128]{2,1,0:T(8,128)S(1)}, f32[8,64,128]{2,1,0:T(8,128)S(1)}, u32[]{:S(2)}, u32[]{:S(2)}) collective-permute-start(f32[8,64,128]{2,1,0:T(8,128)S(1)} %get-tuple-element.30.rest_4_), channel_id=1, source_target_pairs={{1,5},{4,8},{5,1},{8,4},{9,13},{13,9},{3,7},{6,10},{7,3},{10,6},{1... | collective-permute-start | bytes 786440 | tf_op jit(solution)/shard_map/ppermute | solution.py:498
  54.5 4.6 %collective-permute-done.10 = f32[8,64,128]{2,1,0:T(8,128)S(1)} collective-permute-done((f32[8,64,128]{2,1,0:T(8,128)S(1)}, f32[8,64,128]{2,1,0:T(8,128)S(1)}, u32[]{:S(2)}, u32[]{:S(2)}) %collective-permute-start.10) | collective-permute-done | bytes 262176 | tf_op jit(solution)/shard_map/ppermute | solution.py:497
  59.2 1.7 %collective-permute-start.12 = (f32[24,8,128]{2,1,0:T(8,128)S(1)}, f32[24,8,128]{2,1,0:T(8,128)S(1)}, u32[]{:S(2)}, u32[]{:S(2)}) collective-permute-start(f32[24,8,128]{2,1,0:T(8,128)S(1)} %pad_maximum_fusion.4), channel_id=1, source_target_pairs={{0,1},{1,0},{2,3},{3,2},{4,5},{5,4},{6,7},{7,6},{8,9},{9,8},{10,11... | collective-permute-start | bytes 294920 | tf_op jit(solution)/shard_map/ppermute | solution.py:519
  60.9 0.9 %collective-permute-done.12.rest_7_.rest_8_ = f32[24,8,128]{2,1,0:T(8,128)S(1)} collective-permute-done((f32[24,8,128]{2,1,0:T(8,128)S(1)}, f32[24,8,128]{2,1,0:T(8,128)S(1)}, u32[]{:S(2)}, u32[]{:S(2)}) %collective-permute-start.12) | collective-permute-done | bytes 98336 | tf_op jit(solution)/shard_map/ppermute | solution.py:519
  61.8 2.9 %update.3 = f32[8,64,128]{2,1,0:T(8,128)} custom-call(f32[20,8,128]{2,1,0:T(8,128)S(1)} %broadcast_in_dim.439.weight_ref, bf16[2,2,80,240]{3,2,1,0:T(8,128)(2,1)S(1)} %pad_maximum_fusion.3.row_band_ref, bf16[2,2,256,256]{3,2,1,0:T(8,128)(2,1)S(1)} %maximum_maximum_fusion.col_band_ref, f32[12,64,128]{2,1,0:T(8,128)S(1)} %get-tuple-element.69.below_ref, ...), custom_call_target="tpu_custom_call" | custom-call | tf_op jit(solution)/shard_map/update/pallas_call | solution.py:471
  (72 shorter events, 2.9 us)
Async XLA Ops:
  0.6 8.8 %copy-start.5 = (f32[1,3]{1,0:T(1,128)S(1)}, f32[1,3]{1,0:T(1,128)}, u32[]{:S(2)}) copy-start(f32[1,3]{1,0:T(1,128)} %param.10) | copy-start | bytes 40
  0.6 9.1 %copy-start.4 = (f32[1,3,9]{2,0,1:T(1,128)S(1)}, f32[1,3,9]{2,0,1:T(1,128)}, u32[]{:S(2)}) copy-start(f32[1,3,9]{2,0,1:T(1,128)} %param.11) | copy-start | bytes 328
  4.3 10.2 %collective-permute-start.1 = (f32[520,128]{1,0:T(8,128)}, f32[520,128]{1,0:T(8,128)S(1)}, u32[]{:S(2)}, u32[]{:S(2)}) collective-permute-start(f32[520,128]{1,0:T(8,128)} %get-tuple-element.24), channel_id=1, source_target_pairs={{0,4},{1,9},{4,0},{5,13},{8,12},{9,1},{12,8},{13,5},{2,6},{3,11},{... | collective-permute-start | bytes 798728 | tf_op jit(solution)/shard_map/ppermute | solution.py:200
  7.4 10.9 %collective-permute-start = (f32[264,128]{1,0:T(8,128)}, f32[264,128]{1,0:T(8,128)S(1)}, u32[]{:S(2)}, u32[]{:S(2)}) collective-permute-start(f32[264,128]{1,0:T(8,128)} %get-tuple-element.22), channel_id=1, source_target_pairs={{0,4},{1,9},{4,0},{5,13},{8,12},{9,1},{12,8},{13,5},{2,6},{3,11},{... | collective-permute-start | bytes 405512 | tf_op jit(solution)/shard_map/ppermute | solution.py:200
  7.5 17.2 %collective-permute-start.4 = (f32[256,128]{1,0:T(8,128)}, f32[256,128]{1,0:T(8,128)S(1)}, u32[]{:S(2)}, u32[]{:S(2)}) collective-permute-start(f32[256,128]{1,0:T(8,128)} %get-tuple-element.28), channel_id=1, source_target_pairs={{0,4},{1,9},{4,0},{5,13},{8,12},{9,1},{12,8},{13,5},{2,6},{3,11},{... | collective-permute-start | bytes 393224 | tf_op jit(solution)/shard_map/ppermute | solution.py:200
  10.0 0.9 %copy-start = (f32[264,128]{1,0:T(8,128)S(1)}, f32[264,128]{1,0:T(8,128)}, u32[]{:S(2)}) copy-start(f32[264,128]{1,0:T(8,128)} %get-tuple-element.19.refs_2_) | copy-start | bytes 405508
  10.9 0.9 %copy-start.1 = (f32[264,128]{1,0:T(8,128)S(1)}, f32[264,128]{1,0:T(8,128)}, u32[]{:S(2)}) copy-start(f32[264,128]{1,0:T(8,128)} %get-tuple-element.17.refs_0_) | copy-start | bytes 405508
  11.8 0.9 %copy-start.2 = (f32[256,128]{1,0:T(8,128)S(1)}, f32[256,128]{1,0:T(8,128)}, u32[]{:S(2)}) copy-start(f32[256,128]{1,0:T(8,128)} %get-tuple-element.20.refs_3_) | copy-start | bytes 393220
  12.7 0.9 %copy-start.3 = (f32[256,128]{1,0:T(8,128)S(1)}, f32[256,128]{1,0:T(8,128)}, u32[]{:S(2)}) copy-start(f32[256,128]{1,0:T(8,128)} %get-tuple-element.18.refs_1_) | copy-start | bytes 393220
  14.6 8.5 %collective-permute-start.2 = (f32[264,128]{1,0:T(8,128)S(1)}, f32[264,128]{1,0:T(8,128)S(1)}, u32[]{:S(2)}, u32[]{:S(2)}) collective-permute-start(f32[264,128]{1,0:T(8,128)S(1)} %add.519), channel_id=1, source_target_pairs={{0,8},{1,5},{4,12},{5,1},{8,0},{9,13},{12,4},{13,9},{2,10},{3,7},{... | collective-permute-start | bytes 405512 | tf_op jit(solution)/shard_map/ppermute | solution.py:200
  18.1 7.6 %collective-permute-start.5 = (f32[256,128]{1,0:T(8,128)S(1)}, f32[256,128]{1,0:T(8,128)S(1)}, u32[]{:S(2)}, u32[]{:S(2)}) collective-permute-start(f32[256,128]{1,0:T(8,128)S(1)} %add.520), channel_id=1, source_target_pairs={{0,8},{1,5},{4,12},{5,1},{8,0},{9,13},{12,4},{13,9},{2,10},{3,7},{... | collective-permute-start | bytes 393224 | tf_op jit(solution)/shard_map/ppermute | solution.py:200
  23.1 9.2 %collective-permute-start.3 = (f32[264,128]{1,0:T(8,128)S(1)}, f32[264,128]{1,0:T(8,128)S(1)}, u32[]{:S(2)}, u32[]{:S(2)}) collective-permute-start(f32[264,128]{1,0:T(8,128)S(1)} %get-tuple-element.25.rest_0_.rest_1_.rest_5_), channel_id=1, source_target_pairs={{0,2},{2,0},{1,3},{3,1},{4,6},{6,4},{5,7},{7,5},{8,10},{10,8},{9,1... | collective-permute-start | bytes 405512 | tf_op jit(solution)/shard_map/ppermute | solution.py:536
  25.8 6.5 %collective-permute-start.6 = (f32[256,128]{1,0:T(8,128)S(1)}, f32[256,128]{1,0:T(8,128)S(1)}, u32[]{:S(2)}, u32[]{:S(2)}) collective-permute-start(f32[256,128]{1,0:T(8,128)S(1)} %join.3.rest_1_.rest_2_.rest_6_), channel_id=1, source_target_pairs={{0,2},{2,0},{1,3},{3,1},{4,6},{6,4},{5,7},{7,5},{8,10},{10,8},{9,1... | collective-permute-start | bytes 393224 | tf_op jit(solution)/shard_map/ppermute | solution.py:536
  32.6 12.0 %collective-permute-start.7 = (f32[12,64,128]{2,1,0:T(8,128)S(1)}, f32[12,64,128]{2,1,0:T(8,128)S(1)}, u32[]{:S(2)}, u32[]{:S(2)}) collective-permute-start(f32[12,64,128]{2,1,0:T(8,128)S(1)} %get-tuple-element.71), channel_id=1, source_target_pairs={{1,5},{4,0},{5,9},{8,4},{9,13},{12,8},{3,7},{6,2},{7,11},{10,6},{1... | collective-permute-start | bytes 1179656 | tf_op jit(solution)/shard_map/ppermute | solution.py:509
  33.9 10.8 %collective-permute-start.8 = (f32[12,64,128]{2,1,0:T(8,128)S(1)}, f32[12,64,128]{2,1,0:T(8,128)S(1)}, u32[]{:S(2)}, u32[]{:S(2)}) collective-permute-start(f32[12,64,128]{2,1,0:T(8,128)S(1)} %get-tuple-element.70), channel_id=1, source_target_pairs={{0,4},{4,8},{5,1},{8,12},{9,5},{13,9},{2,6},{6,10},{7,3},{10,14},{... | collective-permute-start | bytes 1179656 | tf_op jit(solution)/shard_map/ppermute | solution.py:508
  44.8 3.0 %collective-permute-start.9 = (f32[40,8,128]{2,1,0:T(8,128)S(1)}, f32[40,8,128]{2,1,0:T(8,128)S(1)}, u32[]{:S(2)}, u32[]{:S(2)}) collective-permute-start(f32[40,8,128]{2,1,0:T(8,128)S(1)} %dynamic-slice_dynamic-update-slice_fusion.2), channel_id=1, source_target_pairs={{0,1},{1,0},{2,3},{3,2},{4,5},{5,4},{6,7},{7,6},{8,9},{9,8},{10,11... | collective-permute-start | bytes 491528 | tf_op jit(solution)/shard_map/ppermute | solution.py:519
  49.8 9.3 %collective-permute-start.10 = (f32[8,64,128]{2,1,0:T(8,128)S(1)}, f32[8,64,128]{2,1,0:T(8,128)S(1)}, u32[]{:S(2)}, u32[]{:S(2)}) collective-permute-start(f32[8,64,128]{2,1,0:T(8,128)S(1)} %get-tuple-element.30.rest_4_), channel_id=1, source_target_pairs={{0,4},{4,0},{5,9},{8,12},{9,5},{12,8},{2,6},{6,2},{7,11},{10,14},{... | collective-permute-start | bytes 786440 | tf_op jit(solution)/shard_map/ppermute | solution.py:497
  53.8 5.3 %collective-permute-start.11 = (f32[8,64,128]{2,1,0:T(8,128)S(1)}, f32[8,64,128]{2,1,0:T(8,128)S(1)}, u32[]{:S(2)}, u32[]{:S(2)}) collective-permute-start(f32[8,64,128]{2,1,0:T(8,128)S(1)} %get-tuple-element.30.rest_4_), channel_id=1, source_target_pairs={{1,5},{4,8},{5,1},{8,4},{9,13},{13,9},{3,7},{6,10},{7,3},{10,6},{1... | collective-permute-start | bytes 786440 | tf_op jit(solution)/shard_map/ppermute | solution.py:498
  59.2 2.6 %collective-permute-start.12 = (f32[24,8,128]{2,1,0:T(8,128)S(1)}, f32[24,8,128]{2,1,0:T(8,128)S(1)}, u32[]{:S(2)}, u32[]{:S(2)}) collective-permute-start(f32[24,8,128]{2,1,0:T(8,128)S(1)} %pad_maximum_fusion.4), channel_id=1, source_target_pairs={{0,1},{1,0},{2,3},{3,2},{4,5},{5,4},{6,7},{7,6},{8,9},{9,8},{10,11... | collective-permute-start | bytes 294920 | tf_op jit(solution)/shard_map/ppermute | solution.py:519
